TPU v7x, 32 devices: a whole 2x2x4 slice. The times are simulated.
32 devices in a mesh: seq: 8 (over y, x, core), dp: 4 (over z).
Axes of the slice: x: 2, y: 2, z: 4, core: 2. Of those that a mesh axis runs over, the one named last changes fastest.
Arguments:
- inputs: bfloat16 [8, 2048, 768], P('dp', 'seq'), may hold values from -6 to 6
- w_query: bfloat16 [768, 768], P(('seq', 'dp')), may hold values from -0.21875 to 0.21875
- w_keyval: bfloat16 [768, 128], P(('seq', 'dp')), may hold values from -0.21875 to 0.21875
- w_out: bfloat16 [768, 768], P(('seq', 'dp')), may hold values from -2.5 to 2.5
- w_up: bfloat16 [768, 3072], P(('seq', 'dp')), may hold values from -0.21875 to 0.21875
- w_down: bfloat16 [3072, 768], P(('seq', 'dp')), may hold values from -0.109375 to 0.109375
- norm_gain: bfloat16 [768, 2], P(('seq', 'dp')), may hold values from 0.099609375 to 1.8984375
- norm_bias: bfloat16 [768, 2], P(('seq', 'dp')), may hold values from -1.5 to 1.5
- out_cotangent: bfloat16 [8, 2048, 768], P('dp', 'seq'), may hold values from -6 to 6
- kv_cotangent: bfloat16 [8, 2048, 128], P('dp', 'seq'), may hold values from -6 to 6
Outputs:
- output: bfloat16 [8, 2048, 768], P('dp', 'seq')
- keyval: bfloat16 [8, 2048, 128], P('dp', 'seq')
- grad_inputs: float32 [8, 2048, 768], P('dp', 'seq')
- grad_query: float32 [768, 768], P(('seq', 'dp'))
- grad_keyval: float32 [768, 128], P(('seq', 'dp'))
- grad_out: float32 [768, 768], P(('seq', 'dp'))
- grad_up: float32 [768, 3072], P(('seq', 'dp'))
- grad_down: float32 [3072, 768], P(('seq', 'dp'))
- grad_gain: float32 [768, 2], P(('seq', 'dp'))
- grad_bias: float32 [768, 2], P(('seq', 'dp'))
All inputs are finite; a program needn't handle non-finite values.
Results may differ from a plain program's by a relative error of at most 0.011.
Values may be sent and summed in bfloat16 or wider, within the bound.
No kernel may reach another device: no remote copies, remote signals or barrier semaphores. Data moves between devices by JAX's collectives and lax.ppermute only.
A program may use at most 128 MiB of HBM per device.

v0:
```python
import functools
import math

import jax
import jax.numpy as jnp
import numpy as np
from jax import lax
from jax.experimental import pallas as pl
from jax.experimental.pallas import tpu as pltpu
from jax.sharding import PartitionSpec as P

HEADS = 12
HEAD = 64
ROT = 16
TEAM = 4
MINE = HEADS // TEAM
WIDE = 2 * HEAD
EPSILON = 1e-05
BF = jnp.bfloat16
F32 = jnp.float32
SCALE = 1.0 / math.sqrt(HEAD)
MB = 1 << 20


def dot(left, right):
    return lax.dot_general(left, right, (((1,), (0,)), ((), ())), preferred_element_type=F32)


def dot_rt(left, right):
    return lax.dot_general(left, right, (((1,), (1,)), ((), ())), preferred_element_type=F32)


def dot_lt(left, right):
    return lax.dot_general(left, right, (((0,), (0,)), ((), ())), preferred_element_type=F32)


def lanes(shape):
    return lax.broadcasted_iota(jnp.int32, shape, len(shape) - 1)


def angle_tables(rows, count):
    lane = np.arange(WIDE) % HEAD
    frequency = np.exp(-math.log(10000.0) * (lane % (ROT // 2)) * (2.0 / ROT)) * (lane < ROT)
    sign = np.where(lane < ROT // 2, -1.0, 1.0)
    out = []
    for positions in (np.arange(rows), np.arange(count) * rows):
        angles = 0.25 * positions[:, None] * frequency
        out.append(np.stack([np.cos(angles), sign * np.sin(angles)]).astype(np.float32))
    return out


def table_of(place_ref, start_ref, rank):
    cos_row, sin_row = place_ref[0], place_ref[1]
    cos_start, sin_start = start_ref[0, pl.ds(rank, 1)], start_ref[1, pl.ds(rank, 1)]
    return cos_row * cos_start - sin_row * sin_start, sin_row * cos_start + cos_row * sin_start


def keys_only(tables):
    keys_side = lanes(tables[0].shape) < HEAD
    return jnp.where(keys_side, tables[0], 1.0), jnp.where(keys_side, tables[1], 0.0)


def turn(values, tables, sign):
    near = (lanes(values.shape) % HEAD) < ROT // 2
    swapped = jnp.where(
        near, pltpu.roll(values, WIDE - ROT // 2, 1), pltpu.roll(values, ROT // 2, 1)
    )
    return values * tables[0] + (sign * swapped) * tables[1]


def standardize(tokens):
    center = tokens - jnp.mean(tokens, axis=-1, keepdims=True)
    spread = jnp.mean(center * center, axis=-1, keepdims=True)
    scale = lax.rsqrt(spread + EPSILON)
    return center * scale, scale


def norm_back(hat, scale, pulled):
    return scale * (
        pulled
        - jnp.mean(pulled, axis=-1, keepdims=True)
        - hat * jnp.mean(pulled * hat, axis=-1, keepdims=True)
    )


def three_parts(column):
    high = column.astype(BF)
    rest = column - high.astype(F32)
    mid = rest.astype(BF)
    low = (rest - mid.astype(F32)).astype(BF)
    return high, mid, low


def marked(lane, base, parts):
    out = jnp.zeros(lane.shape, BF)
    for index, part in enumerate(parts):
        out = jnp.where(lane == base + index, part, out)
    return out


def fetch(refs, held, arrived):
    step = pl.program_id(0)

    def start(r):
        for index, ref in enumerate(refs):

            @pl.when(r == index)
            def _(ref=ref):
                pltpu.make_async_copy(ref, held.at[r % 2], arrived.at[r % 2]).start()

    @pl.when(step == 0)
    def _():
        start(step)

    @pl.when(step + 1 < len(refs))
    def _():
        start(step + 1)

    pltpu.make_async_copy(refs[0], held.at[step % 2], arrived.at[step % 2]).wait()
    return held[step % 2]


def normalize(hat, norm_ref, which):
    return (hat * norm_ref[which : which + 1, :] + norm_ref[which + 2 : which + 3, :]).astype(BF)


def put(r, near_ref, far_ref, value):
    @pl.when(r < 2)
    def _():
        near_ref[0] = value

    @pl.when(r >= 2)
    def _():
        far_ref[0] = value


def assemble(own_x, refs, groups, held):
    wide = sum(ref.shape[0] for ref in refs)
    relative = 0
    for ref in refs:
        block = ref.shape[2]
        for index in range(ref.shape[0]):
            x = own_x ^ relative
            for group in range(groups):
                place = (group // 2 * wide + x) * 2 + group % 2 if groups > 1 else x
                start = pl.multiple_of(place * block, block)
                held[pl.ds(start, block), :] = ref[index, group]
            relative += 1


def prepare_kernel(parts, first, last, top, wide, own_ref, *refs):
    x_refs, refs = refs[: TEAM * last], refs[TEAM * last :]
    front_refs, refs = refs[:parts], refs[parts:]
    place_ref, start_ref, query_ref, keyval_ref, *refs = refs
    *refs, held, arrived = refs
    own = own_ref[0]
    copies = [pltpu.make_async_copy(ref, held.at[i], arrived.at[i]) for i, ref in enumerate(x_refs)]
    for copy in copies:
        copy.start()
    if first:
        front_ref, norm_ref = refs
        assemble((own // 2) % wide, front_refs, TEAM, front_ref)
        norm_ref[...] = jnp.transpose(front_ref[:, 2 * WIDE :].astype(F32))[HEAD : HEAD + 8]
    else:
        front_ref, norm_ref = front_refs
        (mlp_ref,) = refs

    for copy in copies:
        copy.wait()

    @pl.loop(0, TEAM)
    def _(r):
        hat, _ = standardize(held[r, 0].astype(F32))
        made = dot(normalize(hat, norm_ref, 0), front_ref[...])
        tables = table_of(place_ref, start_ref, rank_of(own, r, top))
        keyval_ref[r] = turn(made[:, :WIDE], keys_only(tables), 1.0).astype(BF)
        for part in range(2):
            piece = made[:, WIDE * (part + 1) : WIDE * (part + 2)]
            query_ref[r, :, WIDE * part : WIDE * (part + 1)] = (turn(piece, tables, 1.0) * SCALE).astype(BF)
        if not first:
            mlp_ref[r, last - 1] = normalize(hat, norm_ref, 1)
            for index in range(1, last):
                hat, _ = standardize(held[index * TEAM + r, 0].astype(F32))
                mlp_ref[r, index - 1] = normalize(hat, norm_ref, 1)


def rank_of(own, block, top):
    return own ^ ((block % 2) * top) ^ (block // 2)


def slot_of(away, top, wide):
    return ((away // 2) % wide) * TEAM + (away // top) % 2 + 2 * (away % 2)


def load_keyval(own, top, wide, refs, keys_ref, values_ref, base):
    slots = {}
    start = 0
    for ref in refs:
        for index in range(ref.shape[0]):
            slots[start + index] = ref, index
        start += ref.shape[0]
    for away in range(start):
        ref, index = slots[(away // 2) % wide * TEAM + (away // top) % 2 + 2 * (away % 2)]
        block = ref[index]
        rows = block.shape[0]
        at = pl.ds(pl.multiple_of((own ^ away) * rows, rows), rows)
        lane = lanes((rows, WIDE))
        keys_ref[at] = jnp.where(lane < HEAD, block, base[1])
        values_ref[at] = jnp.where(lane < HEAD, base[0], block)


def forward_kernel(top, wide, own_ref, query_ref, *refs):
    kv_refs, (context_ref, marked_ref, low_ref, score_ref, peak_ref, keys_ref, values_ref) = refs[:-7], refs[-7:]
    rows = query_ref.shape[2]
    groups = 2 * MINE
    own = own_ref[0]
    step = pl.program_id(0)
    mine = own ^ (step * top)
    base = mine // 2 * 2
    lane = lanes((rows, WIDE))

    @pl.when(step == 0)
    def _():
        one = jnp.ones((rows, WIDE), BF)
        load_keyval(own, top, wide, kv_refs, keys_ref, values_ref, (one, jnp.zeros_like(one)))

    for c in range(2):
        first = query_ref[c, 0, :, :WIDE]
        at = c * MINE * rows
        low_ref[at : at + rows] = first
        low_ref[at + rows : at + 2 * rows] = pltpu.roll(first.astype(F32), HEAD, 1).astype(BF)
        low_ref[at + 2 * rows : at + 3 * rows] = query_ref[c, 0, :, WIDE:]

    count = base // 2
    key = lax.broadcasted_iota(jnp.int32, (rows, 2 * rows), 1)
    query = lax.broadcasted_iota(jnp.int32, (rows, 2 * rows), 0)
    peak_ref[...] = jnp.full(peak_ref.shape, -1e30, F32)

    @pl.loop(0, count + 1)
    def _(index):
        at = pl.ds(pl.multiple_of(index * 2 * rows, 2 * rows), 2 * rows)
        scores = dot_rt(low_ref[...], keys_ref[at])
        keeps = [key <= query + ((mine ^ c) - 2 * index) * rows for c in range(2)]
        for group in range(groups):
            at = slice(group * rows, (group + 1) * rows)
            part = jnp.where(keeps[group // MINE], scores[at], -1e30)
            score_ref[index, at] = part
            best = functools.reduce(
                jnp.maximum, [part[:, column : column + WIDE] for column in range(0, 2 * rows, WIDE)]
            )
            peak_ref[at] = jnp.maximum(peak_ref[at], best)

    peak_ref[...] = jnp.broadcast_to(jnp.max(peak_ref[...], axis=-1, keepdims=True), peak_ref.shape)

    def weigh(index, sums):
        at = pl.ds(pl.multiple_of(index * 2 * rows, 2 * rows), 2 * rows)
        peak = peak_ref[...]
        weights = jnp.exp(score_ref[index] - jnp.concatenate([peak] * (2 * rows // WIDE), axis=1))
        return sums + dot(weights.astype(BF), values_ref[at])

    sums = lax.fori_loop(0, count + 1, weigh, jnp.zeros((groups * rows, WIDE), F32))
    for c in range(2):
        made = []
        for head in range(MINE):
            at = slice((c * MINE + head) * rows, (c * MINE + head + 1) * rows)
            part = sums[at]
            swapped = pltpu.roll(part, HEAD, 1)
            total = jnp.where(lane < HEAD, part, swapped)
            made.append(jnp.where(lane < HEAD, swapped, part) / total)
            logsum = peak_ref[at] + jnp.log(total)
            marked_ref[c, 0, head] = jnp.where(
                lane < HEAD, low_ref[at], marked(lane, HEAD, three_parts(-logsum))
            )
        context_ref[c, 0, :, :WIDE] = jnp.where(lane < HEAD, made[0], made[1]).astype(BF)
        context_ref[c, 0, :, WIDE:] = jnp.where(lane < HEAD, made[2], 0.0).astype(BF)


def backward_kernel(top, wide, own_ref, query_ref, grad_ref, place_ref, start_ref, *refs):
    kv_refs, (dquery_ref, keep_ref, send_ref, sum_ref, keys_ref, values_ref, dkeyval_ref) = refs[:-7], refs[-7:]
    rows = query_ref.shape[3]
    own = own_ref[0]
    step = pl.program_id(0)
    mine = own ^ (step * top)
    base = mine // 2 * 2
    lane = lanes((rows, WIDE))
    wide_lane = lanes((2 * rows, WIDE))

    @pl.when(step == 0)
    def _():
        dkeyval_ref[...] = jnp.zeros_like(dkeyval_ref)
        ones_low = jnp.where(lane < 3, 1.0, 0.0).astype(BF)
        ones_high = jnp.where((lane >= HEAD) & (lane < HEAD + 3), 1.0, 0.0).astype(BF)
        load_keyval(own, top, wide, kv_refs, keys_ref, values_ref, (ones_low, ones_high))

    key = lax.broadcasted_iota(jnp.int32, (2 * rows, rows), 0)
    row = lax.broadcasted_iota(jnp.int32, (2 * rows, rows), 1)
    sum_ref[...] = jnp.zeros_like(sum_ref)

    @pl.loop(0, base // 2 + 1)
    def _(index):
        at = pl.ds(pl.multiple_of(index * 2 * rows, 2 * rows), 2 * rows)
        keys = keys_ref[at]
        values = values_ref[at]
        d_keys = jnp.zeros((2 * rows, WIDE), F32)
        d_values = jnp.zeros((2 * rows, WIDE), F32)
        for c in range(2):
            keep = key <= row + ((mine ^ c) - 2 * index) * rows
            for head in range(MINE):
                query = query_ref[c, 0, head]
                grad = grad_ref[c, 0, head]
                probs = jnp.where(keep, jnp.exp(dot_rt(keys, query)), 0.0)
                d_scores = (probs * dot_rt(values, grad)).astype(BF)
                d_values += dot(probs.astype(BF), grad)
                d_keys += dot(d_scores, query)
                sum_ref[c, head] += dot_lt(keys, d_scores)
        dkeyval_ref[at] += jnp.where(wide_lane < HEAD, d_keys, d_values)

    for c in range(2):
        turned = [jnp.transpose(sum_ref[c, head]) * SCALE for head in range(MINE)]
        both = jnp.where(lane < HEAD, turned[0], pltpu.roll(turned[1], HEAD, 1))
        last = jnp.where(lane < HEAD, turned[2], 0.0)
        tables = table_of(place_ref, start_ref, mine ^ c)
        dquery_ref[c, 0, :, :WIDE] = turn(both, tables, -1.0).astype(BF)
        dquery_ref[c, 0, :, WIDE:] = turn(last, tables, -1.0).astype(BF)

    @pl.when(step == pl.num_programs(0) - 1)
    def _():
        half = send_ref.shape[0]
        for rank in range(2 * half):
            slot = slot_of(rank ^ own, top, wide)
            block = dkeyval_ref[rank * rows : (rank + 1) * rows]

            @pl.when(slot < half)
            def _():
                keep_ref[jnp.minimum(slot, half - 1)] = block

            @pl.when(slot >= half)
            def _():
                send_ref[jnp.maximum(slot - half, 0)] = block.astype(BF)


def split_rows(own_x, groups, total, keep_ref, send_ref):
    wide = 2 * keep_ref.shape[0]
    block = keep_ref.shape[2]
    for side, ref in enumerate((keep_ref, send_ref)):
        half = own_x // (wide // 2) ^ side
        for index in range(wide // 2):
            x = half * (wide // 2) + index
            for group in range(groups):
                place = (group // 2 * wide + x) * 2 + group % 2 if groups > 1 else x
                start = pl.multiple_of(place * block, block)
                ref[index, group] = total[pl.ds(start, block), :].astype(ref.dtype)


def split_z(own_z, total, keep_ref, send_ref):
    wide, half, block = keep_ref.shape[:3]
    for side, ref in enumerate((keep_ref, send_ref)):
        for x in range(wide):
            for index in range(half):
                place = (x * half + index) * 2 + (own_z % 2 ^ side)
                start = pl.multiple_of(place * block, block)
                ref[x, index] = total[pl.ds(start, block), :].astype(ref.dtype)


def hidden_kernel(count, parts, down_parts, own_ref, *refs):
    grad_refs, refs = refs[:4], refs[4:]
    normed_ref, *refs = refs
    context_refs, refs = refs[:count], refs[count:]
    more_refs, refs = refs[:parts], refs[parts:]
    down_refs, refs = refs[:down_parts], refs[down_parts:]
    (made_ref, made_far_ref, dnormed_ref, marked_ref, more_keep, more_send, down_keep, down_send, *refs) = refs
    (up_sum, low_sum, held, arrived, up_ref, low_ref) = refs
    step = pl.program_id(0)
    own_x = own_ref[0]
    rows = context_refs[0].shape[1]
    units = up_ref.shape[1]

    @pl.when(step == 0)
    def _():
        low_ref[units:] = jnp.zeros_like(low_ref[units:])
        assemble(own_x, more_refs, TEAM, up_ref)
        assemble(own_x, [ref.at[:, TEAM:] for ref in more_refs], 1, low_ref.at[units:])
        assemble(own_x, down_refs, 1, low_ref)

    normed = normed_ref[0].reshape(count * rows, normed_ref.shape[-1])
    context = jnp.concatenate([ref[0] for ref in context_refs], axis=0)
    grad = fetch(grad_refs, held, arrived).reshape(normed.shape)
    raw = dot(normed, up_ref[...])
    bell = 0.5 + 0.5 * lax.erf(raw * math.sqrt(0.5))
    slope = bell + raw * (jnp.exp(raw * raw * -0.5) * (1.0 / math.sqrt(2.0 * math.pi)))
    low = jnp.concatenate([(raw * bell).astype(BF), context], axis=1)
    pulled = dot_rt(grad, low_ref[...])
    d_raw = (pulled[:, :units] * slope).astype(BF)
    made = dot(low, low_ref[...]).astype(BF)
    put(step, made_ref, made_far_ref, made.reshape(made_ref.shape[1:]))
    dnormed_ref[0] = dot_rt(d_raw, up_ref[...]).astype(BF).reshape(dnormed_ref.shape[1:])
    glow = dot_lt(low, grad)
    gup = dot_lt(normed, d_raw)

    pulled = pulled[:, units:].astype(BF)
    product = pulled.astype(F32) * context.astype(F32)
    lane = lanes((grad.shape[0], WIDE))
    for head in range(MINE):
        column = WIDE * (head // 2)
        side = (lane < HEAD) if head % 2 == 0 else (lane >= HEAD)
        delta = jnp.sum(
            jnp.where(side, product[:, column : column + WIDE], 0.0), axis=-1, keepdims=True
        )
        piece = pulled[:, column : column + WIDE]
        if head % 2 == 0:
            piece = pltpu.roll(piece.astype(F32), HEAD, 1).astype(BF)
        piece = jnp.where(
            lane >= HEAD, piece, marked(lane, 0, three_parts(jnp.broadcast_to(-delta, lane.shape)))
        )
        marked_ref[0, :, head] = piece.reshape(count, rows, WIDE)

    @pl.when(step == 0)
    def _():
        low_sum[...] = glow
        up_sum[...] = gup

    @pl.when(step > 0)
    def _():
        low_sum[...] += glow
        up_sum[...] += gup

    @pl.when(step == pl.num_programs(0) - 1)
    def _():
        split_rows(own_x, TEAM, up_sum, more_keep, more_send)
        split_rows(own_x, 1, low_sum.at[units:], more_keep.at[:, TEAM:], more_send.at[:, TEAM:])
        split_z(own_ref[1], low_sum, down_keep, down_send)


def tokens_kernel(last, top, wide, own_ref, x0_ref, x1_ref, x2_ref, x3_ref, dnormed_ref, dquery_ref, dkeyval_ref, cotangent_ref, weight_ref, norm_ref, place_ref, start_ref, *refs):
    if last:
        before_ref, nbefore_ref, dx_ref, dx_far_ref, keep_ref, send_ref, gfront_ref, gnorm_ref, held, arrived = refs
    else:
        dx_ref, dx_far_ref, gfront_ref, gnorm_ref, held, arrived = refs
    step = pl.program_id(0)
    tokens = fetch((x0_ref, x1_ref, x2_ref, x3_ref), held, arrived)
    hat, scale = standardize(tokens[0].astype(F32))
    tables = table_of(place_ref, start_ref, rank_of(own_ref[0], step, top))
    d_keyval = dkeyval_ref[0] + jnp.where(step == 0, cotangent_ref[0].astype(F32), 0.0)
    d_keyval = turn(d_keyval, keys_only(tables), -1.0).astype(BF)
    d_front = jnp.concatenate([d_keyval, dquery_ref[0]], axis=1)
    d_attn = dot_rt(d_front, weight_ref[...])
    d_mlp = dnormed_ref[0, 0].astype(F32)
    d_tokens = norm_back(hat, scale, d_attn * norm_ref[0:1, :] + d_mlp * norm_ref[1:2, :])
    put(step, dx_ref, dx_far_ref, d_tokens.astype(BF))
    sums = [
        jnp.sum(piece, axis=0, keepdims=True) for piece in (d_attn * hat, d_mlp * hat, d_attn, d_mlp)
    ]
    sums = jnp.concatenate(sums + [jnp.zeros_like(sums[0])] * 4, axis=0)
    gfront = dot_lt(normalize(hat, norm_ref, 0), d_front)

    @pl.when(step == 0)
    def _():
        gfront_ref[...] = before_ref[...] + gfront if last else gfront
        gnorm_ref[...] = nbefore_ref[...] + sums if last else sums

    @pl.when(step > 0)
    def _():
        gfront_ref[...] += gfront
        gnorm_ref[...] += sums

    if last:

        @pl.when(step == pl.num_programs(0) - 1)
        def _():
            width = gnorm_ref.shape[1]
            sums = jnp.concatenate(
                [jnp.zeros((HEAD, width), F32), gnorm_ref[...], jnp.zeros((HEAD - 8, width), F32)], axis=0
            )
            gfront_ref[:, 2 * WIDE :] += jnp.transpose(sums)
            split_rows((own_ref[0] // 2) % wide, TEAM, gfront_ref, keep_ref, send_ref)


def finish_kernel(own_ref, mine_ref, c_ref, y_ref, both_ref, query_ref, keyval_ref, gain_ref, bias_ref, turned_ref):
    parts = [mine_ref[...]] + [ref[...].astype(F32) for ref in (c_ref, y_ref, both_ref)]
    total = parts[0] + parts[1] + parts[2] + parts[3]
    keyval_ref[...] = total[:, :WIDE]
    turned_ref[...] = jnp.zeros_like(turned_ref)
    turned_ref[: total.shape[0]] = total[:, 2 * WIDE :]
    ends = jnp.transpose(turned_ref[...])[HEAD : HEAD + 4, : total.shape[0]]
    gain_ref[...] = ends[:2]
    bias_ref[...] = ends[2:]
    for index in range(2):
        bit = own_ref[index] == 0
        parts = [jnp.where(bit, parts[place], parts[place ^ (1 << index)]) for place in range(TEAM)]
    query_ref[...] = jnp.concatenate([part[:, WIDE : WIDE + MINE * HEAD] for part in parts], axis=1)


def params(limit):
    return pltpu.CompilerParams(vmem_limit_bytes=limit * MB)


def cost(micros):
    return pl.CostEstimate(flops=int(micros * 1.1e9), bytes_accessed=0, transcendentals=0)


def struct(shape, kind):
    return jax.ShapeDtypeStruct(shape, kind)


def whole(*shape):
    return pl.BlockSpec(shape, lambda *_: (0,) * len(shape))


def on_device(nseq, ndp, inputs, w_query, w_keyval, w_out, w_up, w_down, norm_gain, norm_bias, out_cotangent, kv_cotangent):
    count, rows, width = inputs.shape
    top = nseq // 2
    wide = nseq // TEAM
    own = lax.axis_index("seq")
    own_y, own_x, own_c = own // top, (own // 2) % wide, own % 2
    own_z = lax.axis_index("dp")
    share = w_query.shape[0]
    down_share = w_down.shape[0]
    hidden = w_up.shape[1] // TEAM
    heads_wide = MINE * HEAD
    front_wide = 3 * WIDE
    slots = TEAM * wide

    def flip(value, mask, what):
        with jax.named_scope("swap_" + what):
            return lax.ppermute(value, "seq", [(i, i ^ mask) for i in range(nseq)])

    def flip_z(value, mask, what):
        with jax.named_scope("swap_" + what):
            return lax.ppermute(value, "dp", [(i, i ^ mask) for i in range(ndp)])

    def hold(*values):
        return lax.optimization_barrier(values)

    def after(value, *others):
        return hold(value, *others)[0]

    def in_order(bit, mine, other, axis):
        return jnp.where(
            bit == 0, jnp.stack([mine, other], axis), jnp.stack([other, mine], axis)
        )

    def merge(value, axis):
        return value.reshape(value.shape[:axis] + (-1,) + value.shape[axis + 2 :])

    def pick(value, index, axis):
        return lax.dynamic_index_in_dim(value, index, axis, keepdims=False)

    def swap_z(value, mask, axis, what):
        other = flip_z(value, mask, f"{what}_z{mask}")

        def join(other):
            return merge(in_order((own_z // mask) % 2, value, other, axis + 1), axis)

        return other, join

    def gather_z(value, axis, what, step=None):
        masks = [ndp >> (index + 1) for index in range(ndp.bit_length() - 1)]
        for mask in masks if step is None else masks[step]:
            other, join = swap_z(value, mask, axis, what)
            value = join(other)
        return value

    def by_place(relative, bits):
        for index, bit in enumerate(bits):
            relative = [
                jnp.where(bit == 0, relative[place], relative[place ^ (1 << index)])
                for place in range(len(relative))
            ]
        return relative

    z_bits = [(own_z >> index) % 2 for index in range(ndp.bit_length() - 1)]

    def gather_x(value, what):
        parts = [value[None]]
        mask = 1
        while mask < wide:
            sent = jnp.concatenate(parts) if mask > 1 else parts[0]
            parts.append(flip(sent, 2 * mask, f"{what}_x{mask}"))
            mask *= 2
        return parts

    def flip_x(send, what):
        return flip(send, wide, f"{what}_x{wide // 2}")

    def scatter_x(keep, got, what):
        mask = wide // 2
        while True:
            value = keep.astype(F32) + got.astype(F32)
            mask //= 2
            if mask == 0:
                return value[0]
            bit = (own_x // mask) % 2
            value = value.reshape((2, -1) + value.shape[1:])
            keep = pick(value, bit, 0)
            got = flip(pick(value, 1 - bit, 0).astype(BF), 2 * mask, f"{what}_x{mask}")

    def halve_z(value, axis, what, mask):
        bit = (own_z // mask) % 2
        value = value.reshape(value.shape[:axis] + (-1, 2) + value.shape[axis + 1 :])
        got = flip_z(pick(value, 1 - bit, axis + 1).astype(BF), mask, f"{what}_z{mask}")
        return pick(value, bit, axis + 1), got

    def add_z(pair):
        return pair[0].astype(F32) + pair[1].astype(F32)

    def finish_z(value, axis, what):
        mask = 2
        while mask < ndp:
            value = add_z(halve_z(value, axis, what, mask))
            mask *= 2
        return jnp.squeeze(value, axis)

    def moved(onward):
        pairs = []
        for rank in range(nseq):
            for z in range(ndp):
                member = 2 * (rank // top) + rank % 2
                place = ((rank // 2) % wide) * ndp + z
                pairs.append((member * (nseq * ndp // TEAM) + place, rank * ndp + z))
        return [pair if onward else pair[::-1] for pair in pairs]

    def team(value, what, first, second):
        across = flip(after(value, first), top, what + "_y")
        return [value, across, flip(value, 1, what + "_c"), flip(after(across, second), 1, what + "_yc")]

    norms = jnp.concatenate([norm_gain, norm_bias], axis=1)
    queries_of = w_query.reshape(share, 2, 2, heads_wide).transpose(1, 2, 0, 3)
    same = jnp.concatenate([w_keyval, norms], axis=1)
    ups = w_up.reshape(share, 2, wide, 2, hidden // wide).transpose(1, 3, 0, 2, 4)
    ups = ups.reshape(2, 2, share, hidden)
    pad = jnp.zeros((2, 2, share, 2 * WIDE - heads_wide - norms.shape[1]), BF)
    spread = (2, 2, share)
    pack = jnp.concatenate(
        [
            jnp.broadcast_to(same[:, :WIDE], spread + (WIDE,)),
            queries_of,
            jnp.broadcast_to(same[:, WIDE:], spread + (norms.shape[1],)),
            pad,
            ups,
        ],
        axis=3,
    )
    masks = [ndp >> (index + 1) for index in range(ndp.bit_length() - 1)]
    near_masks, far_masks = masks[-1:], masks[:-1]

    def spread_z(value, axis, what, some):
        for mask in some:
            other, join = swap_z(value, mask, axis, what)
            value = join(other)
        return value

    def begin_z(value, axis, what, some):
        if not some:
            return value, lambda value: value
        return swap_z(spread_z(value, axis, what, some[:-1]), some[-1], axis, what)

    sequences = [inputs[b : b + 1] for b in range(count)]
    got = [
        flip(pick(pick(pack, own_y ^ (d // 2), 0), own_c ^ (d % 2), 0), top * (d // 2) + d % 2, f"pack_{d}")
        for d in range(1, TEAM)
    ]
    pack, got, sequences, w_out = hold(pack, got, sequences, w_out)
    across = [flip(sequences[0], top, "tokens0_y")]
    mine = pick(pick(pack, own_y, 0), own_c, 0)
    pack = jnp.stack(by_place([mine] + got, [own_c, own_y])).reshape(2, 2, share, -1)
    with jax.named_scope("swap_out_moved"):
        out_rows = lax.ppermute(w_out, ("seq", "dp"), moved(True))
    tokens_c = [flip(sequences[b], 1, f"tokens{b}_c") for b in range(count)]

    front_z = pack[..., :front_wide].reshape(TEAM, share, front_wide)
    got = [flip_z(front_z, mask, f"front_z{mask}") for mask in range(1, ndp)]
    front_z = jnp.stack(by_place([front_z] + got, z_bits), axis=1)
    down_x = jnp.concatenate(gather_x(w_down[None], "down"))
    front_z, pack, out_rows, across[0] = hold(front_z, pack, out_rows, across[0])
    for b in range(1, count):
        across.append(flip(after(sequences[b], across[b - 1]), top, f"tokens{b}_y"))
    tokens = [[sequences[0], across[0], tokens_c[0], flip(across[0], 1, "tokens0_yc")]]
    front_parts = gather_x(front_z.reshape(TEAM, ndp * share, front_wide), "front")
    more = jnp.concatenate(
        [pack[..., front_wide:].reshape(TEAM, share, hidden), out_rows.reshape(1, share, width)]
    )
    more_got, join_more = begin_z(more[:, None], 1, "more", far_masks)
    front_parts, tokens[0], down_x = hold(front_parts, tokens[0], down_x)
    own_rank = own.reshape(1).astype(jnp.int32)
    own_place = jnp.stack([own_x, own_z]).astype(jnp.int32)
    tables = [jnp.asarray(part) for part in angle_tables(rows, nseq)]

    def by_r(*last):
        return pl.BlockSpec((1,) + last, lambda r, *_: (r,) + (0,) * len(last))

    members = [pl.BlockSpec(memory_space=pl.ANY)] * TEAM

    def near(*last):
        return pl.BlockSpec((1,) + last, lambda r, *_: (jnp.minimum(r, 1),) + (0,) * len(last))

    def far(*last):
        return pl.BlockSpec((1,) + last, lambda r, *_: (jnp.maximum(r - 2, 0),) + (0,) * len(last))

    def call(kernel, scalar, inputs, in_specs, out_specs, out_shape, scratch, limit, micros, name, steps=TEAM):
        return pl.pallas_call(
            kernel,
            grid_spec=pltpu.PrefetchScalarGridSpec(
                num_scalar_prefetch=1,
                grid=(steps,),
                in_specs=in_specs,
                out_specs=out_specs,
                scratch_shapes=scratch,
            ),
            out_shape=out_shape,
            compiler_params=params(limit),
            cost_estimate=cost(micros),
            name=name,
        )(scalar, *inputs)

    table = by_r(rows, WIDE)
    block = [pltpu.VMEM((2, 1, rows, width), BF), pltpu.SemaphoreType.DMA((2,))]

    def prepare(b, weights):
        first = b == 0
        many = 1 if b < count - 1 else count
        held = tokens[b] + sum(tokens[: many - 1], [])
        outs = [struct((TEAM, rows, 2 * WIDE), BF), struct((TEAM, rows, WIDE), BF)]
        if first:
            outs += [struct((width, front_wide), BF), struct((8, width), F32)]
        else:
            outs += [struct((TEAM, many, rows, width), BF)]
        return call(
            functools.partial(prepare_kernel, len(weights), first, many, top, wide),
            own_rank,
            [*held, *weights, *tables],
            members * many + [whole(*part.shape) for part in [*weights, *tables]],
            [whole(*out.shape) for out in outs],
            outs,
            [pltpu.VMEM((many * TEAM, 1, rows, width), BF), pltpu.SemaphoreType.DMA((many * TEAM,))],
            16 if first else 24,
            0.5,
            "prepare",
            1,
        )

    *made_first, front, norm_rows = prepare(0, front_parts)
    prepared = [made_first]
    prepared[0], front, across[1:], more_got = hold(prepared[0], front, across[1:], more_got)
    for b in range(1, count):
        tokens.append([sequences[b], across[b], tokens_c[b], flip(across[b], 1, f"tokens{b}_yc")])
    more_got, join_more = begin_z(join_more(more_got), 1, "more", near_masks)
    prepared += [prepare(b, [front, norm_rows]) for b in range(1, count)]
    normed_mlp = prepared[-1][-1]
    queries, keyvals = [[part[index] for part in prepared] for index in range(2)]

    def keys_of_all(value, what):
        parts = [value]
        mask = 1
        while mask < wide:
            sent = jnp.concatenate(parts) if mask > 1 else parts[0]
            parts.append(flip(sent, 2 * mask, f"{what}_x{mask}"))
            mask *= 2
        return parts

    everyone = [keys_of_all(keyvals[b], f"keyval{b}") for b in range(count)]
    kv_specs = [whole(*part.shape) for part in everyone[0]]
    kv_scratch = [pltpu.VMEM((slots * rows, WIDE), BF)] * 2

    def by_pair(*last):
        return pl.BlockSpec((2, 1) + last, lambda y, *_: (0, y) + (0,) * len(last))

    def paired(value):
        return value.reshape((2, 2) + value.shape[1:])

    grads_y = flip(after(out_cotangent, tokens[-1][1]), top, "grads_y")
    grads_c = flip(out_cotangent, 1, "grads_c")
    everyone[0], queries, keyvals, more_got = hold(everyone[0], queries, keyvals, more_got)
    more_parts = gather_x(join_more(more_got).reshape(TEAM + 1, ndp * share, width), "more")
    down_got, join_down = begin_z(after(down_x, more_parts[0])[:, None], 1, "down", far_masks)
    contexts = []
    marked_queries = []
    for b in range(count):
        context, marked_query = call(
            functools.partial(forward_kernel, top, wide),
            own_rank,
            [paired(queries[b]), *everyone[b]],
            [by_pair(rows, 2 * WIDE)] + kv_specs,
            [by_pair(rows, 2 * WIDE), by_pair(MINE, rows, WIDE)],
            [struct((2, 2, rows, 2 * WIDE), BF), struct((2, 2, MINE, rows, WIDE), BF)],
            [
                pltpu.VMEM((2 * MINE * rows, WIDE), BF),
                pltpu.VMEM((slots // 2, 2 * MINE * rows, 2 * rows), F32),
                pltpu.VMEM((2 * MINE * rows, WIDE), F32),
            ]
            + kv_scratch,
            32,
            15,
            "attend",
            2,
        )
        context = context.reshape((TEAM,) + context.shape[2:])
        contexts.append(context)
        marked_queries.append(marked_query)
        if b == 0:
            contexts[0], everyone[1:], queries, grads_y, down_got = hold(
                contexts[0], everyone[1:], queries, grads_y, down_got
            )
            down_got, join_down = begin_z(join_down(down_got), 1, "down", near_masks)
            grads = [out_cotangent, grads_y, grads_c, flip(grads_y, 1, "grads_yc")]
    contexts, grads, more_parts, down_got = hold(contexts, grads, more_parts, down_got)
    down_parts = [join_down(down_got).reshape(wide, 1, ndp * down_share, width)]

    half = max(wide // 2, 1)
    more_half = (half, TEAM + 1, ndp * share, width)
    down_half = (wide, ndp // 2, down_share, width)
    made, made_far, d_normed, marked_grad, more_keep, more_send, down_keep, down_send = call(
        functools.partial(hidden_kernel, count, len(more_parts), len(down_parts)),
        own_place,
        [*grads, normed_mlp, *contexts, *more_parts, *down_parts],
        members
        + [by_r(count, rows, width)]
        + [by_r(rows, 2 * WIDE)] * count
        + [whole(*part.shape) for part in more_parts + down_parts],
        [
            near(count, rows, width),
            far(count, rows, width),
            by_r(count, rows, width),
            by_r(count, MINE, rows, WIDE),
            whole(*more_half),
            whole(*more_half),
            whole(*down_half),
            whole(*down_half),
        ],
        [
            struct((2, count, rows, width), BF),
            struct((2, count, rows, width), BF),
            struct((TEAM, count, rows, width), BF),
            struct((TEAM, count, MINE, rows, WIDE), BF),
            struct(more_half, BF),
            struct(more_half, BF),
            struct(down_half, BF),
            struct(down_half, BF),
        ],
        [
            pltpu.VMEM((width, hidden), F32),
            pltpu.VMEM((hidden + 2 * WIDE, width), F32),
            pltpu.VMEM((2, count, rows, width), BF),
            pltpu.SemaphoreType.DMA((2,)),
            pltpu.VMEM((width, hidden), BF),
            pltpu.VMEM((hidden + 2 * WIDE, width), BF),
        ],
        52,
        27,
        "hidden",
    )

    def sum_c(value, what, *others):
        return value[0].astype(F32) + after(flip(value[1], 1, what + "_c"), *others).astype(F32)

    def sum_y(value, what, *others):
        got = flip(value[1].astype(BF), top, what + "_y")
        return value[0] + after(got, *others).astype(F32)

    d_queries = []
    kept = []
    sent = []
    key_half = (slots // 2, rows, WIDE)
    for b in range(count):
        d_query, keep, send = call(
            functools.partial(backward_kernel, top, wide),
            own_rank,
            [marked_queries[b], paired(marked_grad), *tables, *everyone[b]],
            [
                by_pair(MINE, rows, WIDE),
                pl.BlockSpec((2, 1, None, MINE, rows, WIDE), lambda y, *_, b=b: (0, y, b, 0, 0, 0)),
            ]
            + [whole(*part.shape) for part in tables]
            + kv_specs,
            [by_pair(rows, 2 * WIDE), whole(*key_half), whole(*key_half)],
            [struct((2, 2, rows, 2 * WIDE), BF), struct(key_half, F32), struct(key_half, BF)],
            [pltpu.VMEM((2, MINE, WIDE, rows), F32)]
            + kv_scratch
            + [pltpu.VMEM((slots * rows, WIDE), F32)],
            16,
            20,
            "attend_back",
            2,
        )
        d_query = d_query.reshape((TEAM,) + d_query.shape[2:])
        d_queries.append(d_query)
        kept.append(keep)
        sent.append(send)
        if b == 0:
            got_c = flip(made_far, 1, "made_c")
            got_x = flip_x(more_send, "gmore")
            down_got = flip_z(down_send, 1, "gdown_z1")
            (d_queries, kept, sent, marked_grad, made, got_c, more_keep, got_x, down_keep, down_got) = hold(
                d_queries, kept, sent, marked_grad, made, got_c, more_keep, got_x, down_keep, down_got
            )
            made = made.astype(F32) + got_c.astype(F32)
            more_grads = scatter_x(more_keep, got_x, "gmore").reshape(TEAM + 1, ndp, share, width)
            got_y = flip(made[1].astype(BF), top, "made_y")
            more_z = halve_z(more_grads, 1, "gmore", 1)
            keys_got = flip_x(sent[0], "gkeyval0")
            down_grads = down_keep.astype(F32) + down_got.astype(F32)
            mask = 2
            while mask < ndp:
                down_z = halve_z(down_grads, 1, "gdown", mask)
                down_grads = add_z(down_z) if 2 * mask < ndp else down_grads
                mask *= 2
    (d_queries, kept, sent, made, got_y, more_z, keys_got) = hold(
        d_queries, kept, sent, made, got_y, more_z, keys_got
    )
    output = (inputs.astype(F32) + made[0] + got_y.astype(F32)).astype(BF)
    more_grads = add_z(more_z)
    keys_gots = [keys_got] + [flip_x(sent[b], f"gkeyval{b}") for b in range(1, count)]

    def keys_back(b):
        keep, got = kept[b], keys_gots[b]
        mask = wide // 2
        while True:
            value = keep + got.astype(F32)
            mask //= 2
            if mask == 0:
                return value
            keep = value[: value.shape[0] // 2]
            got = flip(value[value.shape[0] // 2 :].astype(BF), 2 * mask, f"gkeyval{b}_x{mask}")

    def join_c(value, got):
        mine = pick(value.reshape((2, 2) + value.shape[1:]), own_c, 1)
        got = got.astype(F32)
        return jnp.where(own_c == 0, mine, got), jnp.where(own_c == 0, got, mine)

    def join_y(value, got):
        mine = pick(value, own_y, 0)
        got = got.astype(F32)
        return jnp.where(own_y == 0, mine, got), jnp.where(own_y == 0, got, mine)

    pulled = []
    carried = []
    front_half = (half, TEAM, ndp * share, front_wide)
    for b in range(count):
        last = b == count - 1
        outs = [struct((2, rows, width), BF), struct((2, rows, width), BF)]
        out_specs = [near(rows, width), far(rows, width)]
        sums = [struct((width, front_wide), F32), struct((8, width), F32)]
        if last:
            outs += [struct(front_half, F32), struct(front_half, BF)]
        else:
            outs += sums
        d_tokens, d_tokens_far, *carried = call(
            functools.partial(tokens_kernel, last, top, wide),
            own_rank,
            [
                *tokens[b],
                d_normed,
                d_queries[b],
                keys_back(b),
                kv_cotangent,
                front,
                norm_rows,
                *tables,
                *carried,
            ],
            members
            + [
                pl.BlockSpec((1, 1, rows, width), lambda r, *_, b=b: (r, b, 0, 0)),
                by_r(rows, 2 * WIDE),
                table,
                pl.BlockSpec((1, rows, WIDE), lambda r, *_, b=b: (b, 0, 0)),
                whole(width, front_wide),
                whole(8, width),
            ]
            + [whole(*part.shape) for part in tables]
            + [whole(*part.shape) for part in carried],
            out_specs + [whole(*out.shape) for out in outs[2:]],
            outs,
            ([pltpu.VMEM(out.shape, F32) for out in sums] if last else []) + block,
            14,
            7,
            "pull_tokens",
        )
        pulled.append((d_tokens, d_tokens_far))
        if b == 0:
            mask = 2
            while mask < ndp:
                more_z = halve_z(more_grads, 1, "gmore", mask)
                more_grads = add_z(more_z) if 2 * mask < ndp else more_grads
                mask *= 2
            (carried, pulled, down_z, keys_gots, kept, d_queries) = hold(
                carried, pulled, down_z, keys_gots, kept, d_queries
            )
            got_c = flip(pulled[0][1], 1, "dtokens0_c")
            down_grads = jnp.squeeze(add_z(down_z), 1)
            x_half = down_grads.reshape((2, -1) + down_grads.shape[1:])
            x_bit = own_x // (wide // 2)
            down_keep = pick(x_half, x_bit, 0)
            down_got = flip_x(pick(x_half, 1 - x_bit, 0).astype(BF), "gdown")
    front_keep, front_send = carried
    front_keep, front_send, pulled, got_c, more_z = hold(front_keep, front_send, pulled, got_c, more_z)
    more_grads = jnp.squeeze(add_z(more_z), 1)
    down_grads = scatter_x(down_keep, down_got, "gdown")

    def add_c(pair, got):
        return pair[0].astype(F32) + got.astype(F32)

    front_got = flip_x(front_send, "gfront")
    halves = [add_c(pulled[0], got_c)]
    got_y = flip(halves[0][1].astype(BF), top, "dtokens0_y")
    gots_c = [flip(pulled[b][1], 1, f"dtokens{b}_c") for b in range(1, count)]
    ups_c = flip(
        pick(more_grads[:TEAM].reshape(2, 2, share, hidden), 1 - own_c, 1).astype(BF), 1, "gup_c"
    )
    front_keep, front_got, gots_c, more_grads, ups_c = hold(
        front_keep, front_got, gots_c, more_grads, ups_c
    )
    ups = jnp.concatenate(join_c(more_grads[:TEAM], ups_c), axis=-1)
    ups_y = flip(pick(ups, 1 - own_y, 0).astype(BF), top, "gup_y")
    halves += [add_c(pulled[b], gots_c[b - 1]) for b in range(1, count)]
    with jax.named_scope("swap_gout_moved"):
        grad_out = lax.ppermute(more_grads[TEAM].astype(BF), ("seq", "dp"), moved(False)).astype(F32)
    front_grads = scatter_x(front_keep, front_got, "gfront").reshape(TEAM, ndp, share, front_wide)
    mine = pick(front_grads, own_z, 1)
    got = [
        flip_z(pick(front_grads, own_z ^ mask, 1).astype(BF), mask, f"gfront_z{mask}")
        for mask in range(1, ndp)
    ]
    gots_y = [got_y] + [
        flip(halves[b][1].astype(BF), top, f"dtokens{b}_y") for b in range(1, count)
    ]
    mine, got, halves, ups, ups_y, gots_y = hold(mine, got, halves, ups, ups_y, gots_y)
    front_grads = sum([part.astype(F32) for part in got], mine).reshape(2, 2, share, front_wide)

    piece = hidden // wide
    ups = join_y(ups, ups_y)
    grad_up = jnp.concatenate(
        [
            ups[y][:, hidden * c + piece * x : hidden * c + piece * (x + 1)]
            for y in range(2)
            for x in range(wide)
            for c in range(2)
        ],
        axis=-1,
    )
    got = [
        flip(
            pick(pick(front_grads, own_y ^ (d // 2), 0), own_c ^ (d % 2), 0).astype(BF),
            top * (d // 2) + d % 2,
            f"gfront_{d}",
        )
        for d in range(1, TEAM)
    ]
    mine = pick(pick(front_grads, own_y, 0), own_c, 0)
    d_rows = [halves[b][0] + gots_y[b].astype(F32) for b in range(count)]
    grad_inputs = out_cotangent.astype(F32) + jnp.stack(d_rows)
    mine, got, grad_inputs, grad_up, grad_out = hold(mine, got, grad_inputs, grad_up, grad_out)
    grad_query, grad_keyval, grad_gain, grad_bias = pl.pallas_call(
        finish_kernel,
        in_specs=[pl.BlockSpec(memory_space=pltpu.SMEM)] + [whole(share, front_wide)] * TEAM,
        out_specs=[whole(share, TEAM * heads_wide), whole(share, WIDE), whole(2, share), whole(2, share)],
        out_shape=[
            struct((share, TEAM * heads_wide), F32),
            struct((share, WIDE), F32),
            struct((2, share), F32),
            struct((2, share), F32),
        ],
        scratch_shapes=[pltpu.VMEM((WIDE, WIDE), F32)],
        cost_estimate=cost(1),
        name="finish",
    )(jnp.stack([own_c, own_y]).astype(jnp.int32), mine, *got)
    return (
        output,
        jnp.stack([part[0] for part in keyvals]),
        grad_inputs,
        grad_query,
        grad_keyval,
        grad_out,
        grad_up,
        down_grads,
        grad_gain.T,
        grad_bias.T,
    )


def solution(mesh):
    rows = P("dp", "seq", None)
    split = P(("seq", "dp"), None)
    return jax.shard_map(
        functools.partial(on_device, mesh.shape["seq"], mesh.shape["dp"]),
        mesh=mesh,
        in_specs=(rows,) + (split,) * 7 + (rows, rows),
        out_specs=(rows,) * 3 + (split,) * 7,
        check_vma=False,
    )
```

profile of v0, /device:TPU:0, one launch (start us, length us, event | category | flops | bytes accessed | tf_op | source)
XLA Modules:
  0.0 210.5 jit_solution(140947630673799826)
XLA Ops:
  0.7 0.9 reshape.399
  2.4 1.0 reshape.400
  5.1 2.6 %collective-permute-start.1 = (bf16[24,1152]{1,0:T(8,128)(2,1)S(1)}, bf16[24,1152]{1,0:T(8,128)(2,1)S(1)}, u32[]{:S(2)}, u32[]{:S(2)}) collective-permute-start(bf16[24,1152]{1,0:T(8,128)(2,1)S(1)} %get-tuple-element.318), channel_id=1, source_target_pairs={{0,16},{4,20},{8,24},{12,28},{16,0},{20,4},{24,8},{28,12},{1,17},{... | collective-permute-start | bytes 165896 | tf_op jit(solution)/shard_map/swap_pack_2/ppermute | solution.py:525
  7.8 2.3 %collective-permute-done.1 = bf16[24,1152]{1,0:T(8,128)(2,1)S(1)} collective-permute-done((bf16[24,1152]{1,0:T(8,128)(2,1)S(1)}, bf16[24,1152]{1,0:T(8,128)(2,1)S(1)}, u32[]{:S(2)}, u32[]{:S(2)}) %collective-permute-start.1) | collective-permute-done | bytes 55328 | tf_op jit(solution)/shard_map/swap_pack_2/ppermute | solution.py:525
  10.2 1.4 collective-permute-done.2
  11.6 1.6 collective-permute-start.3
  13.3 2.6 %collective-permute-start.4 = (bf16[4,24,384]{2,1,0:T(8,128)(2,1)S(1)}, bf16[4,24,384]{2,1,0:T(8,128)(2,1)S(1)}, u32[]{:S(2)}, u32[]{:S(2)}) collective-permute-start(bf16[4,24,384]{2,1,0:T(8,128)(2,1)S(1)} %bitcast.198), channel_id=1, source_target_pairs={{0,2},{1,3},{2,0},{3,1},{4,6},{5,7},{6,4},{7,5},{8,10},{9,11},{10,... | collective-permute-start | bytes 221192 | tf_op jit(solution)/shard_map/swap_front_z2/ppermute | solution.py:529
  16.1 1.1 collective-permute-start.7
  17.2 1.5 collective-permute-start.11
  18.7 3.4 %collective-permute-done.4 = bf16[4,24,384]{2,1,0:T(8,128)(2,1)S(1)} collective-permute-done((bf16[4,24,384]{2,1,0:T(8,128)(2,1)S(1)}, bf16[4,24,384]{2,1,0:T(8,128)(2,1)S(1)}, u32[]{:S(2)}, u32[]{:S(2)}) %collective-permute-start.4) | collective-permute-done | bytes 73760 | tf_op jit(solution)/shard_map/swap_front_z2/ppermute | solution.py:529
  22.9 3.6 %collective-permute-done.7.refs_1_.refs_5_.x1_ref = bf16[1,256,768]{2,1,0:T(8,128)(2,1)S(1)} collective-permute-done((bf16[1,256,768]{2,1,0:T(8,128)(2,1)S(1)}, bf16[1,256,768]{2,1,0:T(8,128)(2,1)S(1)}, u32[]{:S(2)}, u32[]{:S(2)}) %collective-permute-start.7) | collective-permute-done | bytes 393248 | tf_op jit(solution)/shard_map/swap_tokens0_y/ppermute | solution.py:525
  26.5 0.8 collective-permute-start.10
  27.4 1.6 collective-permute-start.8
  29.0 1.2 collective-permute-start.12
  30.2 0.8 fusion.12
  31.0 0.8 collective-permute-start.13
  32.3 1.0 pad_maximum_fusion.4
  33.4 3.2 %collective-permute-done.8.refs_5_ = bf16[1,4,96,384]{3,2,1,0:T(8,128)(2,1)S(1)} collective-permute-done((bf16[1,4,96,384]{3,2,1,0:T(8,128)(2,1)S(1)}, bf16[1,4,96,384]{3,2,1,0:T(8,128)(2,1)S(1)}, u32[]{:S(2)}, u32[]{:S(2)}) %collective-permute-start.8) | collective-permute-done | bytes 294944 | tf_op jit(solution)/shard_map/swap_front_x1/ppermute | solution.py:525
  36.7 4.3 %prepare.2 = (bf16[4,256,256]{2,1,0:T(8,128)(2,1)S(1)}, bf16[4,256,128]{2,1,0:T(8,128)(2,1)S(1)}, bf16[768,384]{1,0:T(8,128)(2,1)S(1)}, f32[8,768]{1,0:T(8,128)S(1)}) custom-call(s32[1]{0:T(128)} %bitcast.own_ref, bf16[1,256,768]{2,1,0:T(8,128)(2,1)S(1)} %get-tuple-element.162.refs_0_.refs_4_.x0_ref, ...), custom_call_target="tpu_custom_call" | custom-call | flops 550000000 | tf_op jit(solution)/shard_map/prepare/pallas_call | solution.py:700
  41.0 1.6 collective-permute-done.13
  43.0 1.3 maximum_select_fusion.4
  44.4 1.1 pad_maximum_fusion
  45.5 1.3 collective-permute-start.19
  46.8 5.5 %prepare.3 = (bf16[4,256,256]{2,1,0:T(8,128)(2,1)S(1)}, bf16[4,256,128]{2,1,0:T(8,128)(2,1)S(1)}, bf16[4,2,256,768]{3,2,1,0:T(8,128)(2,1)S(1)}) custom-call(s32[1]{0:T(128)} %bitcast.own_ref, bf16[1,256,768]{2,1,0:T(8,128)(2,1)S(1)} %get-tuple-element.172.refs_0_.x0_ref, bf16[1,256,768]{2,1,0:T(8,128)(2,1)S(1)} %collective-permute-done.12.refs_1_.x1_ref, ...), custom_call_target="tpu_custom_call" | custom-call | flops 550000000 | tf_op jit(solution)/shard_map/prepare/pallas_call | solution.py:700
  52.3 1.6 copy-done.2
  53.9 1.2 collective-permute-start.18
  55.4 1.7 collective-permute-start.23
  57.1 2.2 %collective-permute-start.20 = (bf16[2,1,1,96,768]{4,3,0,1,2:T(8,128)(2,1)S(1)}, bf16[2,1,1,96,768]{4,3,0,1,2:T(8,128)(2,1)S(1)}, u32[]{:S(2)}, u32[]{:S(2)}) collective-permute-start(bf16[2,1,1,96,768]{4,3,0,1,2:T(8,128)(2,1)S(1)} %bitcast.176), channel_id=1, source_target_pairs={{0,2},{1,3},{2,0},{3,1},{4,6},{5,7},{6,4},{7,5},{8,10},{9,11},{10,... | collective-permute-start | bytes 884744 | tf_op jit(solution)/shard_map/swap_down_z2/ppermute | solution.py:529
  59.3 8.0 %attend.2 = (bf16[2,2,256,256]{3,2,1,0:T(8,128)(2,1)S(1)}, bf16[2,2,3,256,128]{4,3,2,1,0:T(8,128)(2,1)S(1)}) custom-call(s32[1]{0:T(128)} %bitcast.own_ref, bf16[2,2,256,256]{3,2,1,0:T(8,128)(2,1)S(1)} %bitcast.166, bf16[4,256,128]{2,1,0:T(8,128)(2,1)S(1)} %get-tuple-element.234.refs_0_, bf16[4,256,128]{2,1,0:T(8,128)(2,1)S(1)} %collective-permute-done.14.refs_1_), custom_call_target="tpu_custom_call" | custom-call | flops 16499999744 | tf_op jit(solution)/shard_map/attend/pallas_call | solution.py:700
  68.0 4.7 %collective-permute-done.20 = bf16[2,1,1,96,768]{4,3,0,1,2:T(8,128)(2,1)S(1)} collective-permute-done((bf16[2,1,1,96,768]{4,3,0,1,2:T(8,128)(2,1)S(1)}, bf16[2,1,1,96,768]{4,3,0,1,2:T(8,128)(2,1)S(1)}, u32[]{:S(2)}, u32[]{:S(2)}) %collective-permute-start.20) | collective-permute-done | bytes 294944 | tf_op jit(solution)/shard_map/swap_down_z2/ppermute | solution.py:529
  72.9 8.0 %attend.3 = (bf16[2,2,256,256]{3,2,1,0:T(8,128)(2,1)S(1)}, bf16[2,2,3,256,128]{4,3,2,1,0:T(8,128)(2,1)S(1)}) custom-call(s32[1]{0:T(128)} %bitcast.own_ref, bf16[2,2,256,256]{3,2,1,0:T(8,128)(2,1)S(1)} %bitcast.167, bf16[4,256,128]{2,1,0:T(8,128)(2,1)S(1)} %get-tuple-element.235.refs_0_, bf16[4,256,128]{2,1,0:T(8,128)(2,1)S(1)} %collective-permute-done.18.refs_1_), custom_call_target="tpu_custom_call" | custom-call | flops 16499999744 | tf_op jit(solution)/shard_map/attend/pallas_call | solution.py:700
  81.0 7.6 %collective-permute-done.24 = bf16[2,2,1,96,768]{4,3,0,1,2:T(8,128)(2,1)S(1)} collective-permute-done((bf16[2,2,1,96,768]{4,3,0,1,2:T(8,128)(2,1)S(1)}, bf16[2,2,1,96,768]{4,3,0,1,2:T(8,128)(2,1)S(1)}, u32[]{:S(2)}, u32[]{:S(2)}) %collective-permute-start.24) | collective-permute-done | bytes 589856 | tf_op jit(solution)/shard_map/swap_down_z1/ppermute | solution.py:529
  88.8 1.1 copy.58
  89.9 29.1 %hidden.1 = (bf16[2,2,256,768]{3,2,1,0:T(8,128)(2,1)}, bf16[2,2,256,768]{3,2,1,0:T(8,128)(2,1)}, bf16[4,2,256,768]{3,2,1,0:T(8,128)(2,1)}, bf16[4,2,3,256,128]{4...) custom-call(s32[2]{0:T(128)S(1)} %pad_add_fusion.own_ref, ...), custom_call_target="tpu_custom_call" | custom-call | flops 29699999744 | tf_op jit(solution)/shard_map/hidden/pallas_call | solution.py:700
  119.9 1.4 copy-done.4
  121.3 11.0 %attend_back.2 = (bf16[2,2,256,256]{3,2,1,0:T(8,128)(2,1)S(1)}, f32[4,256,128]{2,1,0:T(8,128)S(1)}, bf16[4,256,128]{2,1,0:T(8,128)(2,1)S(1)}) custom-call(s32[1]{0:T(128)} %bitcast.own_ref, bf16[2,2,3,256,128]{4,3,2,1,0:T(8,128)(2,1)S(1)} %get-tuple-element.186.query_ref, bf16[2,2,2,3,256,128]{5,4,3,2,1,0:T(8,128)(2,1)S(1)} %bitcast.168, ...), custom_call_target="tpu_custom_call" | custom-call | flops 22000001024 | tf_op jit(solution)/shard_map/attend_back/pallas_call | solution.py:700
  132.3 2.9 %collective-permute-done.27 = bf16[2,2,96,768]{3,2,1,0:T(8,128)(2,1)S(1)} collective-permute-done((bf16[2,2,96,768]{3,2,1,0:T(8,128)(2,1)}, bf16[2,2,96,768]{3,2,1,0:T(8,128)(2,1)S(1)}, u32[]{:S(2)}, u32[]{:S(2)}) %collective-permute-start.27) | collective-permute-done | bytes 589856 | tf_op jit(solution)/shard_map/swap_gdown_z1/ppermute | solution.py:529
  135.2 3.0 %collective-permute-done.26 = bf16[1,5,96,768]{3,2,1,0:T(8,128)(2,1)S(1)} collective-permute-done((bf16[1,5,96,768]{3,2,1,0:T(8,128)(2,1)}, bf16[1,5,96,768]{3,2,1,0:T(8,128)(2,1)S(1)}, u32[]{:S(2)}, u32[]{:S(2)}) %collective-permute-start.26) | collective-permute-done | bytes 737312 | tf_op jit(solution)/shard_map/swap_gmore_x1/ppermute | solution.py:525
  138.7 0.9 collective-permute-start.28
  140.3 1.5 collective-permute-start.30
  142.0 1.7 collective-permute-start.31
  143.7 11.0 %attend_back.3 = (bf16[2,2,256,256]{3,2,1,0:T(8,128)(2,1)S(1)}, f32[4,256,128]{2,1,0:T(8,128)S(1)}, bf16[4,256,128]{2,1,0:T(8,128)(2,1)S(1)}) custom-call(s32[1]{0:T(128)} %bitcast.own_ref, bf16[2,2,3,256,128]{4,3,2,1,0:T(8,128)(2,1)S(1)} %get-tuple-element.221.query_ref, bf16[2,2,2,3,256,128]{5,4,3,2,1,0:T(8,128)(2,1)S(1)} %bitcast.169, ...), custom_call_target="tpu_custom_call" | custom-call | flops 22000001024 | tf_op jit(solution)/shard_map/attend_back/pallas_call | solution.py:700
  154.8 0.7 collective-permute-done.29
  155.5 2.4 %collective-permute-done.28 = bf16[2,256,768]{2,1,0:T(8,128)(2,1)S(1)} collective-permute-done((bf16[2,256,768]{2,1,0:T(8,128)(2,1)S(1)}, bf16[2,256,768]{2,1,0:T(8,128)(2,1)S(1)}, u32[]{:S(2)}, u32[]{:S(2)}) %collective-permute-start.28) | collective-permute-done | bytes 786464 | tf_op jit(solution)/shard_map/swap_made_y/ppermute | solution.py:525
  158.1 2.2 %collective-permute-start.32 = (bf16[4,256,128]{2,1,0:T(8,128)(2,1)S(1)}, bf16[4,256,128]{2,1,0:T(8,128)(2,1)S(1)}, u32[]{:S(2)}, u32[]{:S(2)}) collective-permute-start(bf16[4,256,128]{2,1,0:T(8,128)(2,1)S(1)} %get-tuple-element.246), channel_id=1, source_target_pairs={{0,8},{4,12},{8,0},{12,4},{16,24},{20,28},{24,16},{28,20},{1,9},{5... | collective-permute-start | bytes 786440 | tf_op jit(solution)/shard_map/swap_gkeyval1_x1/ppermute | solution.py:525
  160.2 1.0 collective-permute-start.34
  161.3 7.1 %pull_tokens.2 = (bf16[2,256,768]{2,1,0:T(8,128)(2,1)S(1)}, bf16[2,256,768]{2,1,0:T(8,128)(2,1)S(1)}, f32[768,384]{1,0:T(8,128)S(1)}, f32[8,768]{1,0:T(8,128)S(1)}) custom-call(s32[1]{0:T(128)} %bitcast.own_ref, bf16[1,256,768]{2,1,0:T(8,128)(2,1)S(1)} %get-tuple-element.162.refs_0_.refs_4_.x0_ref, ...), custom_call_target="tpu_custom_call" | custom-call | flops 7699999744 | tf_op jit(solution)/shard_map/pull_tokens/pallas_call | solution.py:700
  168.5 1.2 fusion.1
  170.4 7.4 %pull_tokens.3 = (bf16[2,256,768]{2,1,0:T(8,128)(2,1)S(1)}, bf16[2,256,768]{2,1,0:T(8,128)(2,1)S(1)}, f32[1,4,96,384]{3,2,1,0:T(8,128)S(1)}, bf16[1,4,96,384]{3,2,1,0:T(8,128)(2,1)S(1)}) custom-call(s32[1]{0:T(128)} %bitcast.own_ref, bf16[1,256,768]{2,1,0:T(8,128)(2,1)S(1)} %get-tuple-element.172.refs_0_.x0_ref, ...), custom_call_target="tpu_custom_call" | custom-call | flops 7699999744 | tf_op jit(solution)/shard_map/pull_tokens/pallas_call | solution.py:700
  177.8 0.8 fusion.8
  178.6 1.5 collective-permute-start.35
  181.0 1.1 collective-permute-start.42
  182.5 5.2 %collective-permute-done.35 = bf16[1,4,96,384]{3,2,1,0:T(8,128)(2,1)S(1)} collective-permute-done((bf16[1,4,96,384]{3,2,1,0:T(8,128)(2,1)S(1)}, bf16[1,4,96,384]{3,2,1,0:T(8,128)(2,1)S(1)}, u32[]{:S(2)}, u32[]{:S(2)}) %collective-permute-start.35) | collective-permute-done | bytes 294944 | tf_op jit(solution)/shard_map/swap_gfront_x1/ppermute | solution.py:525
  187.9 1.6 collective-permute-start.38
  189.5 1.2 collective-permute-start.39
  190.9 1.1 collective-permute-start.43
  192.8 1.7 collective-permute-start.40
  194.5 1.0 collective-permute-start.41
  196.2 2.9 %collective-permute-done.40 = bf16[4,24,384]{2,1,0:T(8,128)(2,1)S(1)} collective-permute-done((bf16[4,24,384]{2,1,0:T(8,128)(2,1)S(1)}, bf16[4,24,384]{2,1,0:T(8,128)(2,1)S(1)}, u32[]{:S(2)}, u32[]{:S(2)}) %collective-permute-start.40) | collective-permute-done | bytes 73760 | tf_op jit(solution)/shard_map/swap_gfront_z3/ppermute | solution.py:529
  199.0 3.4 %collective-permute-done.41 = bf16[24,1536]{1,0:T(8,128)(2,1)S(1)} collective-permute-done((bf16[24,1536]{1,0:T(8,128)(2,1)S(1)}, bf16[24,1536]{1,0:T(8,128)(2,1)S(1)}, u32[]{:S(2)}, u32[]{:S(2)}) %collective-permute-start.41) | collective-permute-done | bytes 73760 | tf_op jit(solution)/shard_map/swap_gup_y/ppermute | solution.py:525
  202.6 1.1 collective-permute-start.45
  203.7 0.7 collective-permute-start.46
  205.8 1.3 maximum_add_fusion
  209.0 1.5 finish.1
  (173 shorter events, 15.7 us)
Async XLA Ops:
  0.6 7.1 %copy-start.7 = (bf16[2,256,768]{2,1,0:T(8,128)(2,1)S(1)}, bf16[2,256,768]{2,1,0:T(8,128)(2,1)}, u32[]{:S(2)}) copy-start(bf16[2,256,768]{2,1,0:T(8,128)(2,1)} %param.12) | copy-start | bytes 2359300
  4.5 17.6 %copy-start.20 = (bf16[24,768]{1,0:T(8,128)(2,1)S(1)}, bf16[24,768]{1,0:T(8,128)(2,1)}, u32[]{:S(2)}) copy-start(bf16[24,768]{1,0:T(8,128)(2,1)} %param.15) | copy-start | bytes 110596
  4.6 3.3 %collective-permute-start = (bf16[24,1152]{1,0:T(8,128)(2,1)S(1)}, bf16[24,1152]{1,0:T(8,128)(2,1)S(1)}, u32[]{:S(2)}, u32[]{:S(2)}) collective-permute-start(bf16[24,1152]{1,0:T(8,128)(2,1)S(1)} %get-tuple-element.319), channel_id=1, source_target_pairs={{0,4},{4,0},{8,12},{12,8},{16,20},{20,16},{24,28},{28,24},{1,5},{5... | collective-permute-start | bytes 165896 | tf_op jit(solution)/shard_map/swap_pack_1/ppermute | solution.py:525
  5.1 5.1 %collective-permute-start.1 = (bf16[24,1152]{1,0:T(8,128)(2,1)S(1)}, bf16[24,1152]{1,0:T(8,128)(2,1)S(1)}, u32[]{:S(2)}, u32[]{:S(2)}) collective-permute-start(bf16[24,1152]{1,0:T(8,128)(2,1)S(1)} %get-tuple-element.318), channel_id=1, source_target_pairs={{0,16},{4,20},{8,24},{12,28},{16,0},{20,4},{24,8},{28,12},{1,17},{... | collective-permute-start | bytes 165896 | tf_op jit(solution)/shard_map/swap_pack_2/ppermute | solution.py:525
  7.7 3.8 %collective-permute-start.2 = (bf16[24,1152]{1,0:T(8,128)(2,1)S(1)}, bf16[24,1152]{1,0:T(8,128)(2,1)S(1)}, u32[]{:S(2)}, u32[]{:S(2)}) collective-permute-start(bf16[24,1152]{1,0:T(8,128)(2,1)S(1)} %get-tuple-element.317), channel_id=1, source_target_pairs={{0,20},{4,16},{8,28},{12,24},{16,4},{20,0},{24,12},{28,8},{1,21},{... | collective-permute-start | bytes 165896 | tf_op jit(solution)/shard_map/swap_pack_3/ppermute | solution.py:525
  11.6 25.1 %copy-start = (f32[2,256,128]{2,1,0:T(8,128)S(1)}, f32[2,256,128]{2,1,0:T(8,128)}, u32[]{:S(2)}) copy-start(f32[2,256,128]{2,1,0:T(8,128)} %constant.366.clone.refs_6_.refs_10_.place_ref) | copy-start | bytes 786436
  11.6 25.1 %copy-start.1 = (f32[2,8,128]{2,1,0:T(8,128)S(1)}, f32[2,8,128]{2,1,0:T(8,128)}, u32[]{:S(2)}) copy-start(f32[2,8,128]{2,1,0:T(8,128)} %constant.367.clone.refs_7_.refs_11_.start_ref) | copy-start | bytes 24580
  11.6 7.1 %collective-permute-start.3 = (bf16[4,24,384]{2,1,0:T(8,128)(2,1)S(1)}, bf16[4,24,384]{2,1,0:T(8,128)(2,1)S(1)}, u32[]{:S(2)}, u32[]{:S(2)}) collective-permute-start(bf16[4,24,384]{2,1,0:T(8,128)(2,1)S(1)} %bitcast.197), channel_id=1, source_target_pairs={{0,1},{1,0},{2,3},{3,2},{4,5},{5,4},{6,7},{7,6},{8,9},{9,8},{10,11... | collective-permute-start | bytes 221192 | tf_op jit(solution)/shard_map/swap_front_z1/ppermute | solution.py:529
  13.3 8.9 %collective-permute-start.4 = (bf16[4,24,384]{2,1,0:T(8,128)(2,1)S(1)}, bf16[4,24,384]{2,1,0:T(8,128)(2,1)S(1)}, u32[]{:S(2)}, u32[]{:S(2)}) collective-permute-start(bf16[4,24,384]{2,1,0:T(8,128)(2,1)S(1)} %bitcast.198), channel_id=1, source_target_pairs={{0,2},{1,3},{2,0},{3,1},{4,6},{5,7},{6,4},{7,5},{8,10},{9,11},{10,... | collective-permute-start | bytes 221192 | tf_op jit(solution)/shard_map/swap_front_z2/ppermute | solution.py:529
  15.9 6.9 %collective-permute-start.5 = (bf16[4,24,384]{2,1,0:T(8,128)(2,1)S(1)}, bf16[4,24,384]{2,1,0:T(8,128)(2,1)S(1)}, u32[]{:S(2)}, u32[]{:S(2)}) collective-permute-start(bf16[4,24,384]{2,1,0:T(8,128)(2,1)S(1)} %bitcast.199), channel_id=1, source_target_pairs={{0,3},{1,2},{2,1},{3,0},{4,7},{5,6},{6,5},{7,4},{8,11},{9,10},{10,... | collective-permute-start | bytes 221192 | tf_op jit(solution)/shard_map/swap_front_z3/ppermute | solution.py:529
  16.1 10.4 %collective-permute-start.7 = (bf16[1,256,768]{2,1,0:T(8,128)(2,1)S(1)}, bf16[1,256,768]{2,1,0:T(8,128)(2,1)S(1)}, u32[]{:S(2)}, u32[]{:S(2)}) collective-permute-start(bf16[1,256,768]{2,1,0:T(8,128)(2,1)S(1)} %get-tuple-element.162.refs_0_.refs_4_.x0_ref), channel_id=1, source_target_pairs={{0,16},{4,20},{8,24},{12,28},{16,0},{20,4},{24,8},{28,12},{1,17},{... | collective-permute-start | bytes 1179656 | tf_op jit(solution)/shard_map/swap_tokens0_y/ppermute | solution.py:525
  17.2 13.7 %collective-permute-start.11 = (bf16[1,1,96,768]{3,2,1,0:T(8,128)(2,1)}, bf16[1,1,96,768]{3,2,1,0:T(8,128)(2,1)}, u32[]{:S(2)}, u32[]{:S(2)}) collective-permute-start(bf16[1,1,96,768]{3,2,1,0:T(8,128)(2,1)} %bitcast.21), channel_id=1, source_target_pairs={{0,8},{4,12},{8,0},{12,4},{16,24},{20,28},{24,16},{28,20},{1,9},{5... | collective-permute-start | bytes 442376 | tf_op jit(solution)/shard_map/swap_down_x1/ppermute | solution.py:525
  18.7 14.6 %collective-permute-start.9 = (bf16[1,256,768]{2,1,0:T(8,128)(2,1)S(1)}, bf16[1,256,768]{2,1,0:T(8,128)(2,1)S(1)}, u32[]{:S(2)}, u32[]{:S(2)}) collective-permute-start(bf16[1,256,768]{2,1,0:T(8,128)(2,1)S(1)} %get-tuple-element.162.refs_0_.refs_4_.x0_ref), channel_id=1, source_target_pairs={{0,4},{4,0},{8,12},{12,8},{16,20},{20,16},{24,28},{28,24},{1,5},{5... | collective-permute-start | bytes 1179656 | tf_op jit(solution)/shard_map/swap_tokens0_c/ppermute | solution.py:525
  22.1 0.8 collective-permute-start.6
  26.5 10.2 %collective-permute-start.10 = (bf16[1,256,768]{2,1,0:T(8,128)(2,1)S(1)}, bf16[1,256,768]{2,1,0:T(8,128)(2,1)S(1)}, u32[]{:S(2)}, u32[]{:S(2)}) collective-permute-start(bf16[1,256,768]{2,1,0:T(8,128)(2,1)S(1)} %collective-permute-done.7.refs_1_.refs_5_.x1_ref), channel_id=1, source_target_pairs={{0,4},{4,0},{8,12},{12,8},{16,20},{20,16},{24,28},{28,24},{1,5},{5... | collective-permute-start | bytes 1179656 | tf_op jit(solution)/shard_map/swap_tokens0_yc/ppermute | solution.py:525
  27.4 9.3 %collective-permute-start.8 = (bf16[1,4,96,384]{3,2,1,0:T(8,128)(2,1)S(1)}, bf16[1,4,96,384]{3,2,1,0:T(8,128)(2,1)S(1)}, u32[]{:S(2)}, u32[]{:S(2)}) collective-permute-start(bf16[1,4,96,384]{3,2,1,0:T(8,128)(2,1)S(1)} %bitcast.164), channel_id=1, source_target_pairs={{0,8},{4,12},{8,0},{12,4},{16,24},{20,28},{24,16},{28,20},{1,9},{5... | collective-permute-start | bytes 884744 | tf_op jit(solution)/shard_map/swap_front_x1/ppermute | solution.py:525
  29.0 13.6 %collective-permute-start.12 = (bf16[1,256,768]{2,1,0:T(8,128)(2,1)S(1)}, bf16[1,256,768]{2,1,0:T(8,128)(2,1)S(1)}, u32[]{:S(2)}, u32[]{:S(2)}) collective-permute-start(bf16[1,256,768]{2,1,0:T(8,128)(2,1)S(1)} %get-tuple-element.172.refs_0_.x0_ref), channel_id=1, source_target_pairs={{0,16},{4,20},{8,24},{12,28},{16,0},{20,4},{24,8},{28,12},{1,17},{... | collective-permute-start | bytes 1179656 | tf_op jit(solution)/shard_map/swap_tokens1_y/ppermute | solution.py:525
  31.0 11.7 %collective-permute-start.13 = (bf16[5,1,24,768]{3,2,1,0:T(8,128)(2,1)}, bf16[5,1,24,768]{3,2,1,0:T(8,128)(2,1)}, u32[]{:S(2)}, u32[]{:S(2)}) collective-permute-start(bf16[5,1,24,768]{3,2,1,0:T(8,128)(2,1)} %get-tuple-element.321), channel_id=1, source_target_pairs={{0,2},{1,3},{2,0},{3,1},{4,6},{5,7},{6,4},{7,5},{8,10},{9,11},{10,... | collective-permute-start | bytes 552968 | tf_op jit(solution)/shard_map/swap_more_z2/ppermute | solution.py:529
  33.4 47.6 %collective-permute-start.21 = (bf16[2,256,768]{2,1,0:T(8,128)(2,1)}, bf16[2,256,768]{2,1,0:T(8,128)(2,1)S(1)}, u32[]{:S(2)}, u32[]{:S(2)}) collective-permute-start(bf16[2,256,768]{2,1,0:T(8,128)(2,1)} %refs_0_), channel_id=1, source_target_pairs={{0,4},{4,0},{8,12},{12,8},{16,20},{20,16},{24,28},{28,24},{1,5},{5... | collective-permute-start | bytes 2359304 | tf_op jit(solution)/shard_map/swap_grads_c/ppermute | solution.py:525
  36.7 8.9 %collective-permute-start.15 = (bf16[1,256,768]{2,1,0:T(8,128)(2,1)S(1)}, bf16[1,256,768]{2,1,0:T(8,128)(2,1)S(1)}, u32[]{:S(2)}, u32[]{:S(2)}) collective-permute-start(bf16[1,256,768]{2,1,0:T(8,128)(2,1)S(1)} %get-tuple-element.172.refs_0_.x0_ref), channel_id=1, source_target_pairs={{0,4},{4,0},{8,12},{12,8},{16,20},{20,16},{24,28},{28,24},{1,5},{5... | collective-permute-start | bytes 1179656 | tf_op jit(solution)/shard_map/swap_tokens1_c/ppermute | solution.py:525
  36.7 7.7 %copy-start.14 = (bf16[5,1,1,24,768]{4,3,0,2,1:T(8,128)(2,1)S(1)}, bf16[5,1,1,24,768]{4,3,0,2,1:T(8,128)(2,1)}, u32[]{:S(2)}) copy-start(bf16[5,1,1,24,768]{4,3,0,2,1:T(8,128)(2,1)} %get-tuple-element.320) | copy-start | bytes 552964
  41.0 4.5 %copy-start.10 = (bf16[2,256,768]{2,1,0:T(8,128)(2,1)S(1)}, bf16[2,256,768]{2,1,0:T(8,128)(2,1)}, u32[]{:S(2)}) copy-start(bf16[2,256,768]{2,1,0:T(8,128)(2,1)} %refs_0_) | copy-start | bytes 2359300
  42.6 12.5 %collective-permute-start.14 = (bf16[4,256,128]{2,1,0:T(8,128)(2,1)S(1)}, bf16[4,256,128]{2,1,0:T(8,128)(2,1)S(1)}, u32[]{:S(2)}, u32[]{:S(2)}) collective-permute-start(bf16[4,256,128]{2,1,0:T(8,128)(2,1)S(1)} %get-tuple-element.234.refs_0_), channel_id=1, source_target_pairs={{0,8},{4,12},{8,0},{12,4},{16,24},{20,28},{24,16},{28,20},{1,9},{5... | collective-permute-start | bytes 786440 | tf_op jit(solution)/shard_map/swap_keyval0_x1/ppermute | solution.py:525
  43.0 3.8 %collective-permute-start.16 = (bf16[1,256,768]{2,1,0:T(8,128)(2,1)S(1)}, bf16[1,256,768]{2,1,0:T(8,128)(2,1)S(1)}, u32[]{:S(2)}, u32[]{:S(2)}) collective-permute-start(bf16[1,256,768]{2,1,0:T(8,128)(2,1)S(1)} %collective-permute-done.12.refs_1_.x1_ref), channel_id=1, source_target_pairs={{0,4},{4,0},{8,12},{12,8},{16,20},{20,16},{24,28},{28,24},{1,5},{5... | collective-permute-start | bytes 1179656 | tf_op jit(solution)/shard_map/swap_tokens1_yc/ppermute | solution.py:525
  44.3 11.0 %collective-permute-start.17 = (bf16[5,2,24,768]{3,2,1,0:T(8,128)(2,1)S(1)}, bf16[5,2,24,768]{3,2,1,0:T(8,128)(2,1)S(1)}, u32[]{:S(2)}, u32[]{:S(2)}) collective-permute-start(bf16[5,2,24,768]{3,2,1,0:T(8,128)(2,1)S(1)} %maximum_select_fusion.4), channel_id=1, source_target_pairs={{0,1},{1,0},{2,3},{3,2},{4,5},{5,4},{6,7},{7,6},{8,9},{9,8},{10,11... | collective-permute-start | bytes 1105928 | tf_op jit(solution)/shard_map/swap_more_z1/ppermute | solution.py:529
  45.5 27.2 %collective-permute-start.19 = (bf16[2,256,768]{2,1,0:T(8,128)(2,1)S(1)}, bf16[2,256,768]{2,1,0:T(8,128)(2,1)S(1)}, u32[]{:S(2)}, u32[]{:S(2)}) collective-permute-start(bf16[2,256,768]{2,1,0:T(8,128)(2,1)S(1)} %copy-done.10), channel_id=1, source_target_pairs={{0,16},{4,20},{8,24},{12,28},{16,0},{20,4},{24,8},{28,12},{1,17},{... | collective-permute-start | bytes 2359304 | tf_op jit(solution)/shard_map/swap_grads_y/ppermute | solution.py:525
  53.9 14.1 %collective-permute-start.18 = (bf16[4,256,128]{2,1,0:T(8,128)(2,1)S(1)}, bf16[4,256,128]{2,1,0:T(8,128)(2,1)S(1)}, u32[]{:S(2)}, u32[]{:S(2)}) collective-permute-start(bf16[4,256,128]{2,1,0:T(8,128)(2,1)S(1)} %get-tuple-element.235.refs_0_), channel_id=1, source_target_pairs={{0,8},{4,12},{8,0},{12,4},{16,24},{20,28},{24,16},{28,20},{1,9},{5... | collective-permute-start | bytes 786440 | tf_op jit(solution)/shard_map/swap_keyval1_x1/ppermute | solution.py:525
  55.4 11.9 %copy-start.12 = (bf16[5,2,2,24,768]{4,3,2,1,0:T(8,128)(2,1)}, bf16[5,2,2,24,768]{4,3,2,1,0:T(8,128)(2,1)S(1)}, u32[]{:S(2)}) copy-start(bf16[5,2,2,24,768]{4,3,2,1,0:T(8,128)(2,1)S(1)} %maximum_select_fusion.1) | copy-start | bytes 2211844
  55.4 25.6 %collective-permute-start.23 = (bf16[1,5,96,768]{3,2,1,0:T(8,128)(2,1)S(1)}, bf16[1,5,96,768]{3,2,1,0:T(8,128)(2,1)S(1)}, u32[]{:S(2)}, u32[]{:S(2)}) collective-permute-start(bf16[1,5,96,768]{3,2,1,0:T(8,128)(2,1)S(1)} %bitcast.187), channel_id=1, source_target_pairs={{0,8},{4,12},{8,0},{12,4},{16,24},{20,28},{24,16},{28,20},{1,9},{5... | collective-permute-start | bytes 2211848 | tf_op jit(solution)/shard_map/swap_more_x1/ppermute | solution.py:525
  57.1 15.6 %collective-permute-start.20 = (bf16[2,1,1,96,768]{4,3,0,1,2:T(8,128)(2,1)S(1)}, bf16[2,1,1,96,768]{4,3,0,1,2:T(8,128)(2,1)S(1)}, u32[]{:S(2)}, u32[]{:S(2)}) collective-permute-start(bf16[2,1,1,96,768]{4,3,0,1,2:T(8,128)(2,1)S(1)} %bitcast.176), channel_id=1, source_target_pairs={{0,2},{1,3},{2,0},{3,1},{4,6},{5,7},{6,4},{7,5},{8,10},{9,11},{10,... | collective-permute-start | bytes 884744 | tf_op jit(solution)/shard_map/swap_down_z2/ppermute | solution.py:529
  72.7 8.2 %copy-start.17 = (bf16[2,256,768]{2,1,0:T(8,128)(2,1)}, bf16[2,256,768]{2,1,0:T(8,128)(2,1)S(1)}, u32[]{:S(2)}) copy-start(bf16[2,256,768]{2,1,0:T(8,128)(2,1)S(1)} %collective-permute-done.19.refs_1_) | copy-start | bytes 2359300
  72.7 15.9 %collective-permute-start.22 = (bf16[2,256,768]{2,1,0:T(8,128)(2,1)S(1)}, bf16[2,256,768]{2,1,0:T(8,128)(2,1)S(1)}, u32[]{:S(2)}, u32[]{:S(2)}) collective-permute-start(bf16[2,256,768]{2,1,0:T(8,128)(2,1)S(1)} %collective-permute-done.19.refs_1_), channel_id=1, source_target_pairs={{0,4},{4,0},{8,12},{12,8},{16,20},{20,16},{24,28},{28,24},{1,5},{5... | collective-permute-start | bytes 2359304 | tf_op jit(solution)/shard_map/swap_grads_yc/ppermute | solution.py:525
  72.8 15.8 %collective-permute-start.24 = (bf16[2,2,1,96,768]{4,3,0,1,2:T(8,128)(2,1)S(1)}, bf16[2,2,1,96,768]{4,3,0,1,2:T(8,128)(2,1)S(1)}, u32[]{:S(2)}, u32[]{:S(2)}) collective-permute-start(bf16[2,2,1,96,768]{4,3,0,1,2:T(8,128)(2,1)S(1)} %maximum_select_fusion.2), channel_id=1, source_target_pairs={{0,1},{1,0},{2,3},{3,2},{4,5},{5,4},{6,7},{7,6},{8,9},{9,8},{10,11... | collective-permute-start | bytes 1769480 | tf_op jit(solution)/shard_map/swap_down_z1/ppermute | solution.py:529
  81.0 8.9 %copy-start.16 = (bf16[2,256,768]{2,1,0:T(8,128)(2,1)}, bf16[2,256,768]{2,1,0:T(8,128)(2,1)S(1)}, u32[]{:S(2)}) copy-start(bf16[2,256,768]{2,1,0:T(8,128)(2,1)S(1)} %collective-permute-done.21.refs_2_) | copy-start | bytes 2359300
  81.0 8.9 %copy-start.19 = (bf16[1,5,96,768]{3,2,1,0:T(8,128)(2,1)}, bf16[1,5,96,768]{3,2,1,0:T(8,128)(2,1)S(1)}, u32[]{:S(2)}) copy-start(bf16[1,5,96,768]{3,2,1,0:T(8,128)(2,1)S(1)} %collective-permute-done.23.refs_8_) | copy-start | bytes 2211844
  119.1 19.2 %collective-permute-start.25 = (bf16[2,2,256,768]{3,2,1,0:T(8,128)(2,1)}, bf16[2,2,256,768]{3,2,1,0:T(8,128)(2,1)S(1)}, u32[]{:S(2)}, u32[]{:S(2)}) collective-permute-start(bf16[2,2,256,768]{3,2,1,0:T(8,128)(2,1)} %get-tuple-element.215), channel_id=1, source_target_pairs={{0,4},{4,0},{8,12},{12,8},{16,20},{20,16},{24,28},{28,24},{1,5},{5... | collective-permute-start | bytes 4718600 | tf_op jit(solution)/shard_map/swap_made_c/ppermute | solution.py:525
  119.1 19.1 %collective-permute-start.26 = (bf16[1,5,96,768]{3,2,1,0:T(8,128)(2,1)}, bf16[1,5,96,768]{3,2,1,0:T(8,128)(2,1)S(1)}, u32[]{:S(2)}, u32[]{:S(2)}) collective-permute-start(bf16[1,5,96,768]{3,2,1,0:T(8,128)(2,1)} %get-tuple-element.217), channel_id=1, source_target_pairs={{0,8},{4,12},{8,0},{12,4},{16,24},{20,28},{24,16},{28,20},{1,9},{5... | collective-permute-start | bytes 2211848 | tf_op jit(solution)/shard_map/swap_gmore_x1/ppermute | solution.py:525
  119.6 15.6 %collective-permute-start.27 = (bf16[2,2,96,768]{3,2,1,0:T(8,128)(2,1)}, bf16[2,2,96,768]{3,2,1,0:T(8,128)(2,1)S(1)}, u32[]{:S(2)}, u32[]{:S(2)}) collective-permute-start(bf16[2,2,96,768]{3,2,1,0:T(8,128)(2,1)} %get-tuple-element.219), channel_id=1, source_target_pairs={{0,1},{1,0},{2,3},{3,2},{4,5},{5,4},{6,7},{7,6},{8,9},{9,8},{10,11... | collective-permute-start | bytes 1769480 | tf_op jit(solution)/shard_map/swap_gdown_z1/ppermute | solution.py:529
  121.3 16.9 %copy-start.9 = (bf16[2,2,256,768]{3,2,1,0:T(8,128)(2,1)S(1)}, bf16[2,2,256,768]{3,2,1,0:T(8,128)(2,1)}, u32[]{:S(2)}) copy-start(bf16[2,2,256,768]{3,2,1,0:T(8,128)(2,1)} %get-tuple-element.228) | copy-start | bytes 4718596
  138.7 19.2 %collective-permute-start.28 = (bf16[2,256,768]{2,1,0:T(8,128)(2,1)S(1)}, bf16[2,256,768]{2,1,0:T(8,128)(2,1)S(1)}, u32[]{:S(2)}, u32[]{:S(2)}) collective-permute-start(bf16[2,256,768]{2,1,0:T(8,128)(2,1)S(1)} %fusion.2), channel_id=1, source_target_pairs={{0,16},{4,20},{8,24},{12,28},{16,0},{20,4},{24,8},{28,12},{1,17},{... | collective-permute-start | bytes 2359304 | tf_op jit(solution)/shard_map/swap_made_y/ppermute | solution.py:525
  140.0 3.7 %copy-start.5 = (bf16[4,2,3,256,128]{4,3,2,1,0:T(8,128)(2,1)S(1)}, bf16[4,2,3,256,128]{4,3,2,1,0:T(8,128)(2,1)}, u32[]{:S(2)}) copy-start(bf16[4,2,3,256,128]{4,3,2,1,0:T(8,128)(2,1)} %get-tuple-element.222) | copy-start | bytes 4718596
  140.0 15.5 %collective-permute-start.29 = (bf16[5,2,24,768]{3,2,0,1:T(8,128)(2,1)S(1)}, bf16[5,2,24,768]{3,2,0,1:T(8,128)(2,1)S(1)}, u32[]{:S(2)}, u32[]{:S(2)}) collective-permute-start(bf16[5,2,24,768]{3,2,0,1:T(8,128)(2,1)S(1)} %fusion.7), channel_id=1, source_target_pairs={{0,1},{1,0},{2,3},{3,2},{4,5},{5,4},{6,7},{7,6},{8,9},{9,8},{10,11... | collective-permute-start | bytes 1105928 | tf_op jit(solution)/shard_map/swap_gmore_z1/ppermute | solution.py:529
  140.3 14.5 %collective-permute-start.30 = (bf16[4,256,128]{2,1,0:T(8,128)(2,1)S(1)}, bf16[4,256,128]{2,1,0:T(8,128)(2,1)S(1)}, u32[]{:S(2)}, u32[]{:S(2)}) collective-permute-start(bf16[4,256,128]{2,1,0:T(8,128)(2,1)S(1)} %get-tuple-element.226), channel_id=1, source_target_pairs={{0,8},{4,12},{8,0},{12,4},{16,24},{20,28},{24,16},{28,20},{1,9},{5... | collective-permute-start | bytes 786440 | tf_op jit(solution)/shard_map/swap_gkeyval0_x1/ppermute | solution.py:525
  142.0 27.7 %collective-permute-start.31 = (bf16[2,1,96,768]{3,2,1,0:T(8,128)(2,1)S(1)}, bf16[2,1,96,768]{3,2,1,0:T(8,128)(2,1)S(1)}, u32[]{:S(2)}, u32[]{:S(2)}) collective-permute-start(bf16[2,1,96,768]{3,2,1,0:T(8,128)(2,1)S(1)} %dynamic-slice_convert_fusion), channel_id=1, source_target_pairs={{0,2},{1,3},{2,0},{3,1},{4,6},{5,7},{6,4},{7,5},{8,10},{9,11},{10,... | collective-permute-start | bytes 884744 | tf_op jit(solution)/shard_map/swap_gdown_z2/ppermute | solution.py:529
  157.9 3.4 %copy-start.6 = (bf16[4,2,256,768]{3,2,1,0:T(8,128)(2,1)S(1)}, bf16[4,2,256,768]{3,2,1,0:T(8,128)(2,1)}, u32[]{:S(2)}) copy-start(bf16[4,2,256,768]{3,2,1,0:T(8,128)(2,1)} %get-tuple-element.236.dnormed_ref) | copy-start | bytes 9437188
  158.0 3.3 %copy-start.3 = (bf16[2,256,128]{2,1,0:T(8,128)(2,1)S(1)}, bf16[2,256,128]{2,1,0:T(8,128)(2,1)}, u32[]{:S(2)}) copy-start(bf16[2,256,128]{2,1,0:T(8,128)(2,1)} %cotangent_ref.3) | copy-start | bytes 393220
  158.1 11.6 %collective-permute-start.32 = (bf16[4,256,128]{2,1,0:T(8,128)(2,1)S(1)}, bf16[4,256,128]{2,1,0:T(8,128)(2,1)S(1)}, u32[]{:S(2)}, u32[]{:S(2)}) collective-permute-start(bf16[4,256,128]{2,1,0:T(8,128)(2,1)S(1)} %get-tuple-element.246), channel_id=1, source_target_pairs={{0,8},{4,12},{8,0},{12,4},{16,24},{20,28},{24,16},{28,20},{1,9},{5... | collective-permute-start | bytes 786440 | tf_op jit(solution)/shard_map/swap_gkeyval1_x1/ppermute | solution.py:525
  160.2 18.3 %collective-permute-start.34 = (bf16[5,1,24,768]{3,2,0,1:T(8,128)(2,1)S(1)}, bf16[5,1,24,768]{3,2,0,1:T(8,128)(2,1)S(1)}, u32[]{:S(2)}, u32[]{:S(2)}) collective-permute-start(bf16[5,1,24,768]{3,2,0,1:T(8,128)(2,1)S(1)} %dynamic-slice_convert_fusion.1), channel_id=1, source_target_pairs={{0,2},{1,3},{2,0},{3,1},{4,6},{5,7},{6,4},{7,5},{8,10},{9,11},{10,... | collective-permute-start | bytes 552968 | tf_op jit(solution)/shard_map/swap_gmore_z2/ppermute | solution.py:529
  161.3 7.2 %copy-start.8 = (bf16[2,256,768]{2,1,0:T(8,128)(2,1)S(1)}, bf16[2,256,768]{2,1,0:T(8,128)(2,1)}, u32[]{:S(2)}) copy-start(bf16[2,256,768]{2,1,0:T(8,128)(2,1)} %param.12) | copy-start | bytes 2359300
  169.7 8.9 %collective-permute-start.33 = (bf16[2,256,768]{2,1,0:T(8,128)(2,1)S(1)}, bf16[2,256,768]{2,1,0:T(8,128)(2,1)S(1)}, u32[]{:S(2)}, u32[]{:S(2)}) collective-permute-start(bf16[2,256,768]{2,1,0:T(8,128)(2,1)S(1)} %get-tuple-element.257), channel_id=1, source_target_pairs={{0,4},{4,0},{8,12},{12,8},{16,20},{20,16},{24,28},{28,24},{1,5},{5... | collective-permute-start | bytes 2359304 | tf_op jit(solution)/shard_map/swap_dtokens0_c/ppermute | solution.py:525
  169.8 8.0 %collective-permute-start.48 = (bf16[1,96,768]{2,1,0:T(8,128)(2,1)S(1)}, bf16[1,96,768]{2,1,0:T(8,128)(2,1)S(1)}, u32[]{:S(2)}, u32[]{:S(2)}) collective-permute-start(bf16[1,96,768]{2,1,0:T(8,128)(2,1)S(1)} %fusion.9), channel_id=1, source_target_pairs={{0,8},{4,12},{8,0},{12,4},{16,24},{20,28},{24,16},{28,20},{1,9},{5... | collective-permute-start | bytes 442376 | tf_op jit(solution)/shard_map/swap_gdown_x1/ppermute | solution.py:525
  178.6 9.1 %collective-permute-start.35 = (bf16[1,4,96,384]{3,2,1,0:T(8,128)(2,1)S(1)}, bf16[1,4,96,384]{3,2,1,0:T(8,128)(2,1)S(1)}, u32[]{:S(2)}, u32[]{:S(2)}) collective-permute-start(bf16[1,4,96,384]{3,2,1,0:T(8,128)(2,1)S(1)} %get-tuple-element.263), channel_id=1, source_target_pairs={{0,8},{4,12},{8,0},{12,4},{16,24},{20,28},{24,16},{28,20},{1,9},{5... | collective-permute-start | bytes 884744 | tf_op jit(solution)/shard_map/swap_gfront_x1/ppermute | solution.py:525
  180.1 7.6 %collective-permute-start.36 = (bf16[2,256,768]{2,1,0:T(8,128)(2,1)S(1)}, bf16[2,256,768]{2,1,0:T(8,128)(2,1)S(1)}, u32[]{:S(2)}, u32[]{:S(2)}) collective-permute-start(bf16[2,256,768]{2,1,0:T(8,128)(2,1)S(1)} %get-tuple-element.264), channel_id=1, source_target_pairs={{0,4},{4,0},{8,12},{12,8},{16,20},{20,16},{24,28},{28,24},{1,5},{5... | collective-permute-start | bytes 2359304 | tf_op jit(solution)/shard_map/swap_dtokens1_c/ppermute | solution.py:525
  180.2 2.3 %collective-permute-start.37 = (bf16[2,24,768]{2,1,0:T(8,128)(2,1)S(1)}, bf16[2,24,768]{2,1,0:T(8,128)(2,1)S(1)}, u32[]{:S(2)}, u32[]{:S(2)}) collective-permute-start(bf16[2,24,768]{2,1,0:T(8,128)(2,1)S(1)} %fusion.14), channel_id=1, source_target_pairs={{0,4},{4,0},{8,12},{12,8},{16,20},{20,16},{24,28},{28,24},{1,5},{5... | collective-permute-start | bytes 221192 | tf_op jit(solution)/shard_map/swap_gup_c/ppermute | solution.py:525
  181.0 11.8 %collective-permute-start.42 = (bf16[256,768]{1,0:T(8,128)(2,1)S(1)}, bf16[256,768]{1,0:T(8,128)(2,1)S(1)}, u32[]{:S(2)}, u32[]{:S(2)}) collective-permute-start(bf16[256,768]{1,0:T(8,128)(2,1)S(1)} %fusion.5), channel_id=1, source_target_pairs={{0,16},{4,20},{8,24},{12,28},{16,0},{20,4},{24,8},{28,12},{1,17},{... | collective-permute-start | bytes 1179656 | tf_op jit(solution)/shard_map/swap_dtokens0_y/ppermute | solution.py:525
  187.9 8.3 %collective-permute-start.38 = (bf16[4,24,384]{2,1,0:T(8,128)(2,1)S(1)}, bf16[4,24,384]{2,1,0:T(8,128)(2,1)S(1)}, u32[]{:S(2)}, u32[]{:S(2)}) collective-permute-start(bf16[4,24,384]{2,1,0:T(8,128)(2,1)S(1)} %get-tuple-element.302), channel_id=1, source_target_pairs={{0,1},{1,0},{2,3},{3,2},{4,5},{5,4},{6,7},{7,6},{8,9},{9,8},{10,11... | collective-permute-start | bytes 221192 | tf_op jit(solution)/shard_map/swap_gfront_z1/ppermute | solution.py:529
  189.5 6.7 %collective-permute-start.39 = (bf16[4,24,384]{2,1,0:T(8,128)(2,1)S(1)}, bf16[4,24,384]{2,1,0:T(8,128)(2,1)S(1)}, u32[]{:S(2)}, u32[]{:S(2)}) collective-permute-start(bf16[4,24,384]{2,1,0:T(8,128)(2,1)S(1)} %get-tuple-element.301), channel_id=1, source_target_pairs={{0,2},{1,3},{2,0},{3,1},{4,6},{5,7},{6,4},{7,5},{8,10},{9,11},{10,... | collective-permute-start | bytes 221192 | tf_op jit(solution)/shard_map/swap_gfront_z2/ppermute | solution.py:529
  190.9 11.5 %collective-permute-start.43 = (bf16[256,768]{1,0:T(8,128)(2,1)S(1)}, bf16[256,768]{1,0:T(8,128)(2,1)S(1)}, u32[]{:S(2)}, u32[]{:S(2)}) collective-permute-start(bf16[256,768]{1,0:T(8,128)(2,1)S(1)} %fusion.6), channel_id=1, source_target_pairs={{0,16},{4,20},{8,24},{12,28},{16,0},{20,4},{24,8},{28,12},{1,17},{... | collective-permute-start | bytes 1179656 | tf_op jit(solution)/shard_map/swap_dtokens1_y/ppermute | solution.py:525
  192.1 2.5 %collective-permute-start.47 = (bf16[24,768]{1,0:T(8,128)(2,1)S(1)}, bf16[24,768]{1,0:T(8,128)(2,1)S(1)}, u32[]{:S(2)}, u32[]{:S(2)}) collective-permute-start(bf16[24,768]{1,0:T(8,128)(2,1)S(1)} %fusion.19), channel_id=1, source_target_pairs={{0,0},{1,1},{2,2},{3,3},{4,8},{5,9},{6,10},{7,11},{8,4},{9,5},{10,... | collective-permute-start | bytes 110600 | tf_op jit(solution)/shard_map/swap_gout_moved/ppermute | solution.py:1016
  192.8 6.2 %collective-permute-start.40 = (bf16[4,24,384]{2,1,0:T(8,128)(2,1)S(1)}, bf16[4,24,384]{2,1,0:T(8,128)(2,1)S(1)}, u32[]{:S(2)}, u32[]{:S(2)}) collective-permute-start(bf16[4,24,384]{2,1,0:T(8,128)(2,1)S(1)} %get-tuple-element.300), channel_id=1, source_target_pairs={{0,3},{1,2},{2,1},{3,0},{4,7},{5,6},{6,5},{7,4},{8,11},{9,10},{10,... | collective-permute-start | bytes 221192 | tf_op jit(solution)/shard_map/swap_gfront_z3/ppermute | solution.py:529
  194.5 7.9 %collective-permute-start.41 = (bf16[24,1536]{1,0:T(8,128)(2,1)S(1)}, bf16[24,1536]{1,0:T(8,128)(2,1)S(1)}, u32[]{:S(2)}, u32[]{:S(2)}) collective-permute-start(bf16[24,1536]{1,0:T(8,128)(2,1)S(1)} %fusion.18), channel_id=1, source_target_pairs={{0,16},{4,20},{8,24},{12,28},{16,0},{20,4},{24,8},{28,12},{1,17},{... | collective-permute-start | bytes 221192 | tf_op jit(solution)/shard_map/swap_gup_y/ppermute | solution.py:525
  202.5 5.3 %collective-permute-start.44 = (bf16[24,384]{1,0:T(8,128)(2,1)S(1)}, bf16[24,384]{1,0:T(8,128)(2,1)S(1)}, u32[]{:S(2)}, u32[]{:S(2)}) collective-permute-start(bf16[24,384]{1,0:T(8,128)(2,1)S(1)} %get-tuple-element.324), channel_id=1, source_target_pairs={{0,4},{4,0},{8,12},{12,8},{16,20},{20,16},{24,28},{28,24},{1,5},{5... | collective-permute-start | bytes 55304 | tf_op jit(solution)/shard_map/swap_gfront_1/ppermute | solution.py:525
  202.6 5.2 %collective-permute-start.45 = (bf16[24,384]{1,0:T(8,128)(2,1)S(1)}, bf16[24,384]{1,0:T(8,128)(2,1)S(1)}, u32[]{:S(2)}, u32[]{:S(2)}) collective-permute-start(bf16[24,384]{1,0:T(8,128)(2,1)S(1)} %get-tuple-element.323), channel_id=1, source_target_pairs={{0,16},{4,20},{8,24},{12,28},{16,0},{20,4},{24,8},{28,12},{1,17},{... | collective-permute-start | bytes 55304 | tf_op jit(solution)/shard_map/swap_gfront_2/ppermute | solution.py:525
  203.7 4.1 %collective-permute-start.46 = (bf16[24,384]{1,0:T(8,128)(2,1)S(1)}, bf16[24,384]{1,0:T(8,128)(2,1)S(1)}, u32[]{:S(2)}, u32[]{:S(2)}) collective-permute-start(bf16[24,384]{1,0:T(8,128)(2,1)S(1)} %get-tuple-element.322), channel_id=1, source_target_pairs={{0,20},{4,16},{8,28},{12,24},{16,4},{20,0},{24,12},{28,8},{1,21},{... | collective-permute-start | bytes 55304 | tf_op jit(solution)/shard_map/swap_gfront_3/ppermute | solution.py:525
  (9 other events, 9.2 us)
where the time goes:
time: 211 us; the launch traced here: 210 us
  Pallas kernels  92.8 us (44%)
  waiting for transfers between devices  49 us (23%)
  starting transfers between devices  43.7 us (21%)
  other arithmetic  12.3 us (6%)
  local copies, waits for them, and re-layouts  11 us (5%)
    pallas_call x9, Pallas kernels, call(): pl.pallas_call(kernel, grid_spec=pltpu.PrefetchScalarGridSpec(num_scalar_...  91.3 us
    ppermute x33, starting transfers between devices, flip(): return lax.ppermute(value, 'seq', [(i, i ^ mask) for i in range(nseq)])  27 us
    ppermute x33, waiting for transfers between devices, flip(): return lax.ppermute(value, 'seq', [(i, i ^ mask) for i in range(nseq)])  24.9 us
    ppermute x14, waiting for transfers between devices, flip_z(): return lax.ppermute(value, 'dp', [(i, i ^ mask) for i in range(ndp)])  24.1 us
    ppermute x14, starting transfers between devices, flip_z(): return lax.ppermute(value, 'dp', [(i, i ^ mask) for i in range(ndp)])  15.4 us
    unnamed x55, local copies, waits for them, and re-layouts  5.54 us
  transfers between devices with their start and end apart: 49, of which 17 were waited for; matrix products, arithmetic and copies ran while one was open for 6% of the time, Pallas kernels for 30%

commit v1 on v0

--- a/solution.py
+++ b/solution.py
@@ -362,6 +362,15 @@
                 ref[x, index] = total[pl.ds(start, block), :].astype(ref.dtype)
 
 
+def join_rows(own_x, own_z, refs, held):
+    for side, ref in enumerate(refs):
+        for away in range(ref.shape[0]):
+            for index in range(ref.shape[1]):
+                place = ((own_x ^ away) * ref.shape[1] + index) * 2 + (own_z % 2 ^ side)
+                start = pl.multiple_of(place * ref.shape[2], ref.shape[2])
+                held[pl.ds(start, ref.shape[2])] = ref[away, index]
+
+
 def hidden_kernel(count, parts, down_parts, own_ref, *refs):
     grad_refs, refs = refs[:4], refs[4:]
     normed_ref, *refs = refs
@@ -380,7 +389,25 @@
         low_ref[units:] = jnp.zeros_like(low_ref[units:])
         assemble(own_x, more_refs, TEAM, up_ref)
         assemble(own_x, [ref.at[:, TEAM:] for ref in more_refs], 1, low_ref.at[units:])
-        assemble(own_x, down_refs, 1, low_ref)
+        if down_parts == 1:
+            assemble(own_x, down_refs, 1, low_ref)
+        else:
+            join_rows(own_x, own_ref[1], down_refs, low_ref)
+
+    rows = context_refs[0].shape[1]
+    units = up_ref.shape[1]
+
+    @pl.when(step == 0)
+    def _():
+        low_ref[units:] = jnp.zeros_like(low_ref[units:])
+        assemble(own_x, more_refs, TEAM, up_ref)
+        assemble(own_x, [ref.at[:, TEAM:] for ref in more_refs], 1, low_ref.at[units:])
+        for side, ref in enumerate(down_refs):
+            for away in range(ref.shape[0]):
+                for index in range(ref.shape[1]):
+                    place = ((own_x ^ away) * ref.shape[1] + index) * 2 + (own_ref[1] % 2 ^ side)
+                    start = pl.multiple_of(place * ref.shape[2], ref.shape[2])
+                    low_ref[pl.ds(start, ref.shape[2])] = ref[away, index]
 
     normed = normed_ref[0].reshape(count * rows, normed_ref.shape[-1])
     context = jnp.concatenate([ref[0] for ref in context_refs], axis=0)
@@ -476,7 +503,8 @@
 
 
 def finish_kernel(own_ref, mine_ref, c_ref, y_ref, both_ref, query_ref, keyval_ref, gain_ref, bias_ref, turned_ref):
-    parts = [mine_ref[...]] + [ref[...].astype(F32) for ref in (c_ref, y_ref, both_ref)]
+    mine = mine_ref[own_ref[1] * 2 + own_ref[0]]
+    parts = [mine] + [ref[...].astype(F32) for ref in (c_ref, y_ref, both_ref)]
     total = parts[0] + parts[1] + parts[2] + parts[3]
     keyval_ref[...] = total[:, :WIDE]
     turned_ref[...] = jnp.zeros_like(turned_ref)
@@ -663,15 +691,16 @@
     across = [flip(sequences[0], top, "tokens0_y")]
     mine = pick(pick(pack, own_y, 0), own_c, 0)
     pack = jnp.stack(by_place([mine] + got, [own_c, own_y])).reshape(2, 2, share, -1)
+    tokens_c = [flip(sequences[b], 1, f"tokens{b}_c") for b in range(count)]
+
+    front_z = pack[..., :front_wide].reshape(TEAM, share, front_wide)
+    got = [flip_z(front_z, mask, f"front_z{mask}") for mask in range(1, ndp)]
+    got, across[0] = hold(got, across[0])
+    front_z = jnp.stack(by_place([front_z] + got, z_bits), axis=1)
+    down_x = jnp.concatenate(gather_x(w_down[None], "down"))
+    front_z, pack, w_out, across[0] = hold(front_z, pack, w_out, across[0])
     with jax.named_scope("swap_out_moved"):
         out_rows = lax.ppermute(w_out, ("seq", "dp"), moved(True))
-    tokens_c = [flip(sequences[b], 1, f"tokens{b}_c") for b in range(count)]
-
-    front_z = pack[..., :front_wide].reshape(TEAM, share, front_wide)
-    got = [flip_z(front_z, mask, f"front_z{mask}") for mask in range(1, ndp)]
-    front_z = jnp.stack(by_place([front_z] + got, z_bits), axis=1)
-    down_x = jnp.concatenate(gather_x(w_down[None], "down"))
-    front_z, pack, out_rows, across[0] = hold(front_z, pack, out_rows, across[0])
     for b in range(1, count):
         across.append(flip(after(sequences[b], across[b - 1]), top, f"tokens{b}_y"))
     tokens = [[sequences[0], across[0], tokens_c[0], flip(across[0], 1, "tokens0_yc")]]
@@ -680,7 +709,7 @@
         [pack[..., front_wide:].reshape(TEAM, share, hidden), out_rows.reshape(1, share, width)]
     )
     more_got, join_more = begin_z(more[:, None], 1, "more", far_masks)
-    front_parts, tokens[0], down_x = hold(front_parts, tokens[0], down_x)
+    front_parts, tokens[0] = hold(front_parts, tokens[0])
     own_rank = own.reshape(1).astype(jnp.int32)
     own_place = jnp.stack([own_x, own_z]).astype(jnp.int32)
     tables = [jnp.asarray(part) for part in angle_tables(rows, nseq)]
@@ -740,7 +769,10 @@
 
     *made_first, front, norm_rows = prepare(0, front_parts)
     prepared = [made_first]
-    prepared[0], front, across[1:], more_got = hold(prepared[0], front, across[1:], more_got)
+    prepared[0], front, across[1:], more_got, down_x = hold(
+        prepared[0], front, across[1:], more_got, down_x
+    )
+    down_got, join_down = begin_z(down_x[:, None], 1, "down", far_masks)
     for b in range(1, count):
         tokens.append([sequences[b], across[b], tokens_c[b], flip(across[b], 1, f"tokens{b}_yc")])
     more_got, join_more = begin_z(join_more(more_got), 1, "more", near_masks)
@@ -769,9 +801,7 @@
 
     grads_y = flip(after(out_cotangent, tokens[-1][1]), top, "grads_y")
     grads_c = flip(out_cotangent, 1, "grads_c")
-    everyone[0], queries, keyvals, more_got = hold(everyone[0], queries, keyvals, more_got)
-    more_parts = gather_x(join_more(more_got).reshape(TEAM + 1, ndp * share, width), "more")
-    down_got, join_down = begin_z(after(down_x, more_parts[0])[:, None], 1, "down", far_masks)
+    everyone[0], queries, keyvals = hold(everyone[0], queries, keyvals)
     contexts = []
     marked_queries = []
     for b in range(count):
@@ -788,7 +818,7 @@
                 pltpu.VMEM((2 * MINE * rows, WIDE), F32),
             ]
             + kv_scratch,
-            32,
+            7 + 7 * slots // 4,
             15,
             "attend",
             2,
@@ -797,13 +827,18 @@
         contexts.append(context)
         marked_queries.append(marked_query)
         if b == 0:
-            contexts[0], everyone[1:], queries, grads_y, down_got = hold(
-                contexts[0], everyone[1:], queries, grads_y, down_got
+            contexts[0], everyone[1:], queries, grads_y, down_got, more_got = hold(
+                contexts[0], everyone[1:], queries, grads_y, down_got, more_got
             )
-            down_got, join_down = begin_z(join_down(down_got), 1, "down", near_masks)
+            more_parts = gather_x(join_more(more_got).reshape(TEAM + 1, ndp * share, width), "more")
+            down_z = join_down(down_got)
+            down_got = flip_z(down_z, 1, "down_z1")
             grads = [out_cotangent, grads_y, grads_c, flip(grads_y, 1, "grads_yc")]
     contexts, grads, more_parts, down_got = hold(contexts, grads, more_parts, down_got)
-    down_parts = [join_down(down_got).reshape(wide, 1, ndp * down_share, width)]
+    if down_share % 16:
+        down_parts = [in_order(own_z % 2, down_z, down_got, 2).reshape(wide, 1, ndp * down_share, width)]
+    else:
+        down_parts = [part.reshape(wide, ndp // 2, down_share, width) for part in (down_z, down_got)]
 
     half = max(wide // 2, 1)
     more_half = (half, TEAM + 1, ndp * share, width)
@@ -844,7 +879,7 @@
             pltpu.VMEM((width, hidden), BF),
             pltpu.VMEM((hidden + 2 * WIDE, width), BF),
         ],
-        52,
+        36,
         27,
         "hidden",
     )
@@ -982,8 +1017,12 @@
                 more_z = halve_z(more_grads, 1, "gmore", mask)
                 more_grads = add_z(more_z) if 2 * mask < ndp else more_grads
                 mask *= 2
-            (carried, pulled, down_z, keys_gots, kept, d_queries) = hold(
-                carried, pulled, down_z, keys_gots, kept, d_queries
+            (carried, pulled, down_z, more_z, keys_gots, kept, d_queries) = hold(
+                carried, pulled, down_z, more_z, keys_gots, kept, d_queries
+            )
+            more_grads = jnp.squeeze(add_z(more_z), 1)
+            ups_c = flip(
+                pick(more_grads[:TEAM].reshape(2, 2, share, hidden), 1 - own_c, 1).astype(BF), 1, "gup_c"
             )
             got_c = flip(pulled[0][1], 1, "dtokens0_c")
             down_grads = jnp.squeeze(add_z(down_z), 1)
@@ -992,8 +1031,9 @@
             down_keep = pick(x_half, x_bit, 0)
             down_got = flip_x(pick(x_half, 1 - x_bit, 0).astype(BF), "gdown")
     front_keep, front_send = carried
-    front_keep, front_send, pulled, got_c, more_z = hold(front_keep, front_send, pulled, got_c, more_z)
-    more_grads = jnp.squeeze(add_z(more_z), 1)
+    front_keep, front_send, pulled, got_c, ups_c = hold(front_keep, front_send, pulled, got_c, ups_c)
+    ups = jnp.concatenate(join_c(more_grads[:TEAM], ups_c), axis=-1)
+    ups_y = flip(pick(ups, 1 - own_y, 0).astype(BF), top, "gup_y")
     down_grads = scatter_x(down_keep, down_got, "gdown")
 
     def add_c(pair, got):
@@ -1003,17 +1043,10 @@
     halves = [add_c(pulled[0], got_c)]
     got_y = flip(halves[0][1].astype(BF), top, "dtokens0_y")
     gots_c = [flip(pulled[b][1], 1, f"dtokens{b}_c") for b in range(1, count)]
-    ups_c = flip(
-        pick(more_grads[:TEAM].reshape(2, 2, share, hidden), 1 - own_c, 1).astype(BF), 1, "gup_c"
-    )
-    front_keep, front_got, gots_c, more_grads, ups_c = hold(
-        front_keep, front_got, gots_c, more_grads, ups_c
-    )
-    ups = jnp.concatenate(join_c(more_grads[:TEAM], ups_c), axis=-1)
-    ups_y = flip(pick(ups, 1 - own_y, 0).astype(BF), top, "gup_y")
-    halves += [add_c(pulled[b], gots_c[b - 1]) for b in range(1, count)]
+    front_keep, front_got, gots_c, more_grads = hold(front_keep, front_got, gots_c, more_grads)
     with jax.named_scope("swap_gout_moved"):
         grad_out = lax.ppermute(more_grads[TEAM].astype(BF), ("seq", "dp"), moved(False)).astype(F32)
+    halves += [add_c(pulled[b], gots_c[b - 1]) for b in range(1, count)]
     front_grads = scatter_x(front_keep, front_got, "gfront").reshape(TEAM, ndp, share, front_wide)
     mine = pick(front_grads, own_z, 1)
     got = [
@@ -1045,13 +1078,14 @@
         )
         for d in range(1, TEAM)
     ]
-    mine = pick(pick(front_grads, own_y, 0), own_c, 0)
+    mine = front_grads.reshape(TEAM, share, front_wide)
     d_rows = [halves[b][0] + gots_y[b].astype(F32) for b in range(count)]
     grad_inputs = out_cotangent.astype(F32) + jnp.stack(d_rows)
     mine, got, grad_inputs, grad_up, grad_out = hold(mine, got, grad_inputs, grad_up, grad_out)
     grad_query, grad_keyval, grad_gain, grad_bias = pl.pallas_call(
         finish_kernel,
-        in_specs=[pl.BlockSpec(memory_space=pltpu.SMEM)] + [whole(share, front_wide)] * TEAM,
+        in_specs=[pl.BlockSpec(memory_space=pltpu.SMEM), whole(TEAM, share, front_wide)]
+        + [whole(share, front_wide)] * (TEAM - 1),
         out_specs=[whole(share, TEAM * heads_wide), whole(share, WIDE), whole(2, share), whole(2, share)],
         out_shape=[
             struct((share, TEAM * heads_wide), F32),
@@ -1060,6 +1094,7 @@
             struct((2, share), F32),
         ],
         scratch_shapes=[pltpu.VMEM((WIDE, WIDE), F32)],
+        compiler_params=params(60),
         cost_estimate=cost(1),
         name="finish",
     )(jnp.stack([own_c, own_y]).astype(jnp.int32), mine, *got)

time: 211 us -> 202 us (0.957)
  starting transfers between devices: 43.7 us -> 53.4 us
  waiting for transfers between devices: 49 us -> 40.3 us
  local copies, waits for them, and re-layouts: 11 us -> 4.62 us
  Pallas kernels: 92.8 us -> 89.6 us
    ppermute x33, starting transfers between devices: 27 us -> 33.2 us  [flip(): return lax.ppermute(value, 'seq', [(i, i ^ mask) for i in range(nseq)])]
    ppermute x33, waiting for transfers between devices: 24.9 us -> 19.8 us  [flip(): return lax.ppermute(value, 'seq', [(i, i ^ mask) for i in range(nseq)])]
    unnamed x55 -> x31, local copies, waits for them, and re-layouts: 5.54 us -> 0.84 us
    ppermute x14, waiting for transfers between devices: 24.1 us -> 20.5 us  [flip_z(): return lax.ppermute(value, 'dp', [(i, i ^ mask) for i in range(ndp)])]
    pallas_call x9, Pallas kernels: 91.3 us -> 87.9 us  [call(): pl.pallas_call(kernel, grid_spec=pltpu.PrefetchScalarGridSpec(num_scalar_...]
    ppermute x14, starting transfers between devices: 15.4 us -> 18.1 us  [flip_z(): return lax.ppermute(value, 'dp', [(i, i ^ mask) for i in range(ndp)])]
  transfers between devices with their start and end apart: 49 -> 49, of which waited for: 17 -> 18; matrix products, arithmetic and copies ran while one was open for 6% -> 6% of each run, Pallas kernels for 30% -> 31%
where the time goes in v1:
time: 202 us; the launch traced here: 201 us
  Pallas kernels  89.6 us (44%)
  starting transfers between devices  53.4 us (26%)
  waiting for transfers between devices  40.3 us (20%)
  other arithmetic  12 us (6%)
  local copies, waits for them, and re-layouts  4.62 us (2%)
    pallas_call x9, Pallas kernels, call(): pl.pallas_call(kernel, grid_spec=pltpu.PrefetchScalarGridSpec(num_scalar_...  87.9 us
    ppermute x33, starting transfers between devices, flip(): return lax.ppermute(value, 'seq', [(i, i ^ mask) for i in range(nseq)])  33.2 us
    ppermute x14, waiting for transfers between devices, flip_z(): return lax.ppermute(value, 'dp', [(i, i ^ mask) for i in range(ndp)])  20.5 us
    ppermute x33, waiting for transfers between devices, flip(): return lax.ppermute(value, 'seq', [(i, i ^ mask) for i in range(nseq)])  19.8 us
    ppermute x14, starting transfers between devices, flip_z(): return lax.ppermute(value, 'dp', [(i, i ^ mask) for i in range(ndp)])  18.1 us
  transfers between devices with their start and end apart: 49, of which 18 were waited for; matrix products, arithmetic and copies ran while one was open for 6% of the time, Pallas kernels for 31%

profile of v1, /device:TPU:0, one launch (start us, length us, event | category | flops | bytes accessed | tf_op | source)
XLA Modules:
  0.0 201.3 jit_solution(13578167936966233444)
XLA Ops:
  0.7 0.9 reshape.314
  2.4 1.0 reshape.315
  5.1 2.6 %collective-permute-start.1 = (bf16[24,1152]{1,0:T(8,128)(2,1)S(1)}, bf16[24,1152]{1,0:T(8,128)(2,1)S(1)}, u32[]{:S(2)}, u32[]{:S(2)}) collective-permute-start(bf16[24,1152]{1,0:T(8,128)(2,1)S(1)} %get-tuple-element.324), channel_id=1, source_target_pairs={{0,16},{4,20},{8,24},{12,28},{16,0},{20,4},{24,8},{28,12},{1,17},{... | collective-permute-start | bytes 165896 | tf_op jit(solution)/shard_map/swap_pack_2/ppermute | solution.py:553
  7.8 2.3 %collective-permute-done.1 = bf16[24,1152]{1,0:T(8,128)(2,1)S(1)} collective-permute-done((bf16[24,1152]{1,0:T(8,128)(2,1)S(1)}, bf16[24,1152]{1,0:T(8,128)(2,1)S(1)}, u32[]{:S(2)}, u32[]{:S(2)}) %collective-permute-start.1) | collective-permute-done | bytes 55328 | tf_op jit(solution)/shard_map/swap_pack_2/ppermute | solution.py:553
  10.1 1.4 collective-permute-done.2
  11.5 1.1 collective-permute-start.6
  12.8 1.6 collective-permute-start.3
  14.4 2.6 %collective-permute-start.4 = (bf16[4,24,384]{2,1,0:T(8,128)(2,1)S(1)}, bf16[4,24,384]{2,1,0:T(8,128)(2,1)S(1)}, u32[]{:S(2)}, u32[]{:S(2)}) collective-permute-start(bf16[4,24,384]{2,1,0:T(8,128)(2,1)S(1)} %bitcast.186), channel_id=1, source_target_pairs={{0,2},{1,3},{2,0},{3,1},{4,6},{5,7},{6,4},{7,5},{8,10},{9,11},{10,... | collective-permute-start | bytes 221192 | tf_op jit(solution)/shard_map/swap_front_z2/ppermute | solution.py:557
  17.2 1.5 collective-permute-start.13
  18.7 3.7 %collective-permute-done.4 = bf16[4,24,384]{2,1,0:T(8,128)(2,1)S(1)} collective-permute-done((bf16[4,24,384]{2,1,0:T(8,128)(2,1)S(1)}, bf16[4,24,384]{2,1,0:T(8,128)(2,1)S(1)}, u32[]{:S(2)}, u32[]{:S(2)}) %collective-permute-start.4) | collective-permute-done | bytes 73760 | tf_op jit(solution)/shard_map/swap_front_z2/ppermute | solution.py:557
  22.4 0.8 collective-permute-done.5
  23.4 1.4 collective-permute-start.11
  24.9 2.6 %collective-permute-start.7 = (bf16[1,4,96,384]{3,2,1,0:T(8,128)(2,1)S(1)}, bf16[1,4,96,384]{3,2,1,0:T(8,128)(2,1)}, u32[]{:S(2)}, u32[]{:S(2)}) collective-permute-start(bf16[1,4,96,384]{3,2,1,0:T(8,128)(2,1)S(1)} %bitcast.157), channel_id=1, source_target_pairs={{0,8},{4,12},{8,0},{12,4},{16,24},{20,28},{24,16},{28,20},{1,9},{5... | collective-permute-start | bytes 884744 | tf_op jit(solution)/shard_map/swap_front_x1/ppermute | solution.py:553
  27.6 1.0 collective-permute-start.10
  28.6 0.7 fusion.12
  29.3 2.4 %collective-permute-start.12 = (bf16[5,1,24,768]{3,2,1,0:T(8,128)(2,1)}, bf16[5,1,24,768]{3,2,1,0:T(8,128)(2,1)}, u32[]{:S(2)}, u32[]{:S(2)}) collective-permute-start(bf16[5,1,24,768]{3,2,1,0:T(8,128)(2,1)} %get-tuple-element.327), channel_id=1, source_target_pairs={{0,2},{1,3},{2,0},{3,1},{4,6},{5,7},{6,4},{7,5},{8,10},{9,11},{10,... | collective-permute-start | bytes 552968 | tf_op jit(solution)/shard_map/swap_more_z2/ppermute | solution.py:557
  32.2 1.0 pad_maximum_fusion.4
  33.2 1.3 collective-permute-start.21
  34.5 1.5 collective-permute-done.7.refs_5_
  36.1 5.3 %prepare.2 = (bf16[4,256,256]{2,1,0:T(8,128)(2,1)S(1)}, bf16[4,256,128]{2,1,0:T(8,128)(2,1)S(1)}, bf16[768,384]{1,0:T(8,128)(2,1)S(1)}, f32[8,768]{1,0:T(8,128)S(1)}) custom-call(s32[1]{0:T(128)} %bitcast.own_ref, bf16[1,256,768]{2,1,0:T(8,128)(2,1)S(1)} %get-tuple-element.169.refs_0_.refs_4_.x0_ref, ...), custom_call_target="tpu_custom_call" | custom-call | flops 550000000 | tf_op jit(solution)/shard_map/prepare/pallas_call | solution.py:729
  41.9 0.8 collective-permute-start.14
  42.7 0.9 collective-permute-start.18
  43.6 1.3 maximum_select_fusion.3
  44.9 1.1 pad_maximum_fusion
  46.0 2.4 %collective-permute-start.19 = (bf16[2,1,1,96,768]{4,3,1,0,2:T(8,128)(2,1)S(1)}, bf16[2,1,1,96,768]{4,3,1,0,2:T(8,128)(2,1)S(1)}, u32[]{:S(2)}, u32[]{:S(2)}) collective-permute-start(bf16[2,1,1,96,768]{4,3,1,0,2:T(8,128)(2,1)S(1)} %bitcast.172), channel_id=1, source_target_pairs={{0,2},{1,3},{2,0},{3,1},{4,6},{5,7},{6,4},{7,5},{8,10},{9,11},{10,... | collective-permute-start | bytes 884744 | tf_op jit(solution)/shard_map/swap_down_z2/ppermute | solution.py:557
  48.5 1.6 collective-permute-start.20
  50.0 5.3 %prepare.3 = (bf16[4,256,256]{2,1,0:T(8,128)(2,1)S(1)}, bf16[4,256,128]{2,1,0:T(8,128)(2,1)S(1)}, bf16[4,2,256,768]{3,2,1,0:T(8,128)(2,1)S(1)}) custom-call(s32[1]{0:T(128)} %bitcast.own_ref, bf16[1,256,768]{2,1,0:T(8,128)(2,1)S(1)} %get-tuple-element.179.refs_0_.x0_ref, bf16[1,256,768]{2,1,0:T(8,128)(2,1)} %collective-permute-done.10.refs_1_.x1_ref, ...), custom_call_target="tpu_custom_call" | custom-call | flops 550000000 | tf_op jit(solution)/shard_map/prepare/pallas_call | solution.py:729
  55.4 1.3 collective-permute-start.17
  56.6 7.9 %attend.2 = (bf16[2,2,256,256]{3,2,1,0:T(8,128)(2,1)S(1)}, bf16[2,2,3,256,128]{4,3,2,1,0:T(8,128)(2,1)S(1)}) custom-call(s32[1]{0:T(128)} %bitcast.own_ref, bf16[2,2,256,256]{3,2,1,0:T(8,128)(2,1)S(1)} %bitcast.162, bf16[4,256,128]{2,1,0:T(8,128)(2,1)S(1)} %get-tuple-element.240.refs_0_, bf16[4,256,128]{2,1,0:T(8,128)(2,1)S(1)} %collective-permute-done.14.refs_1_), custom_call_target="tpu_custom_call" | custom-call | flops 16499999744 | tf_op jit(solution)/shard_map/attend/pallas_call | solution.py:729
  65.5 3.6 %collective-permute-start.23 = (bf16[1,5,96,768]{3,2,1,0:T(8,128)(2,1)S(1)}, bf16[1,5,96,768]{3,2,1,0:T(8,128)(2,1)S(1)}, u32[]{:S(2)}, u32[]{:S(2)}) collective-permute-start(bf16[1,5,96,768]{3,2,1,0:T(8,128)(2,1)S(1)} %bitcast.159), channel_id=1, source_target_pairs={{0,8},{4,12},{8,0},{12,4},{16,24},{20,28},{24,16},{28,20},{1,9},{5... | collective-permute-start | bytes 2211848 | tf_op jit(solution)/shard_map/swap_more_x1/ppermute | solution.py:553
  69.6 7.9 %attend.3 = (bf16[2,2,256,256]{3,2,1,0:T(8,128)(2,1)S(1)}, bf16[2,2,3,256,128]{4,3,2,1,0:T(8,128)(2,1)S(1)}) custom-call(s32[1]{0:T(128)} %bitcast.own_ref, bf16[2,2,256,256]{3,2,1,0:T(8,128)(2,1)S(1)} %bitcast.163, bf16[4,256,128]{2,1,0:T(8,128)(2,1)S(1)} %get-tuple-element.241.refs_0_, bf16[4,256,128]{2,1,0:T(8,128)(2,1)S(1)} %collective-permute-done.17.refs_1_), custom_call_target="tpu_custom_call" | custom-call | flops 16499999744 | tf_op jit(solution)/shard_map/attend/pallas_call | solution.py:729
  77.7 6.9 %collective-permute-done.24 = bf16[2,2,1,96,768]{4,3,1,0,2:T(8,128)(2,1)S(1)} collective-permute-done((bf16[2,2,1,96,768]{4,3,1,0,2:T(8,128)(2,1)S(1)}, bf16[2,2,1,96,768]{4,3,1,0,2:T(8,128)(2,1)S(1)}, u32[]{:S(2)}, u32[]{:S(2)}) %collective-permute-start.24) | collective-permute-done | bytes 589856 | tf_op jit(solution)/shard_map/swap_down_z1/ppermute | solution.py:557
  84.6 1.6 collective-permute-done.23.refs_8_
  86.2 25.4 %hidden.1 = (bf16[2,2,256,768]{3,2,1,0:T(8,128)(2,1)S(1)}, bf16[2,2,256,768]{3,2,1,0:T(8,128)(2,1)S(1)}, bf16[4,2,256,768]{3,2,1,0:T(8,128)(2,1)S(1)}, bf16[4,2,...) custom-call(s32[2]{0:T(128)S(1)} %pad_add_fusion.own_ref, ...), custom_call_target="tpu_custom_call" | custom-call | flops 29699999744 | tf_op jit(solution)/shard_map/hidden/pallas_call | solution.py:729
  111.7 1.8 collective-permute-start.26
  114.0 11.0 %attend_back.2 = (bf16[2,2,256,256]{3,2,1,0:T(8,128)(2,1)S(1)}, f32[4,256,128]{2,1,0:T(8,128)S(1)}, bf16[4,256,128]{2,1,0:T(8,128)(2,1)S(1)}) custom-call(s32[1]{0:T(128)} %bitcast.own_ref, bf16[2,2,3,256,128]{4,3,2,1,0:T(8,128)(2,1)S(1)} %get-tuple-element.192.query_ref, bf16[2,2,2,3,256,128]{5,4,3,2,1,0:T(8,128)(2,1)S(1)} %bitcast.164, ...), custom_call_target="tpu_custom_call" | custom-call | flops 22000001024 | tf_op jit(solution)/shard_map/attend_back/pallas_call | solution.py:729
  125.0 4.0 %collective-permute-done.27 = bf16[2,2,96,768]{3,2,1,0:T(8,128)(2,1)S(1)} collective-permute-done((bf16[2,2,96,768]{3,2,1,0:T(8,128)(2,1)S(1)}, bf16[2,2,96,768]{3,2,1,0:T(8,128)(2,1)S(1)}, u32[]{:S(2)}, u32[]{:S(2)}) %collective-permute-start.27) | collective-permute-done | bytes 589856 | tf_op jit(solution)/shard_map/swap_gdown_z1/ppermute | solution.py:557
  128.9 1.7 collective-permute-done.26
  131.0 0.8 collective-permute-start.28
  132.1 0.8 collective-permute-start.29
  132.8 1.7 collective-permute-start.30
  134.7 0.8 collective-permute-start.31
  135.5 11.0 %attend_back.3 = (bf16[2,2,256,256]{3,2,1,0:T(8,128)(2,1)S(1)}, f32[4,256,128]{2,1,0:T(8,128)S(1)}, bf16[4,256,128]{2,1,0:T(8,128)(2,1)S(1)}) custom-call(s32[1]{0:T(128)} %bitcast.own_ref, bf16[2,2,3,256,128]{4,3,2,1,0:T(8,128)(2,1)S(1)} %get-tuple-element.227.query_ref, bf16[2,2,2,3,256,128]{5,4,3,2,1,0:T(8,128)(2,1)S(1)} %bitcast.165, ...), custom_call_target="tpu_custom_call" | custom-call | flops 22000001024 | tf_op jit(solution)/shard_map/attend_back/pallas_call | solution.py:729
  147.0 3.2 %collective-permute-done.28 = bf16[2,256,768]{2,1,0:T(8,128)(2,1)S(1)} collective-permute-done((bf16[2,256,768]{2,1,0:T(8,128)(2,1)S(1)}, bf16[2,256,768]{2,1,0:T(8,128)(2,1)S(1)}, u32[]{:S(2)}, u32[]{:S(2)}) %collective-permute-start.28) | collective-permute-done | bytes 786464 | tf_op jit(solution)/shard_map/swap_made_y/ppermute | solution.py:553
  150.7 2.9 %collective-permute-start.33 = (bf16[4,256,128]{2,1,0:T(8,128)(2,1)S(1)}, bf16[4,256,128]{2,1,0:T(8,128)(2,1)S(1)}, u32[]{:S(2)}, u32[]{:S(2)}) collective-permute-start(bf16[4,256,128]{2,1,0:T(8,128)(2,1)S(1)} %get-tuple-element.254), channel_id=1, source_target_pairs={{0,8},{4,12},{8,0},{12,4},{16,24},{20,28},{24,16},{28,20},{1,9},{5... | collective-permute-start | bytes 786440 | tf_op jit(solution)/shard_map/swap_gkeyval1_x1/ppermute | solution.py:553
  153.7 7.0 %pull_tokens.2 = (bf16[2,256,768]{2,1,0:T(8,128)(2,1)S(1)}, bf16[2,256,768]{2,1,0:T(8,128)(2,1)S(1)}, f32[768,384]{1,0:T(8,128)S(1)}, f32[8,768]{1,0:T(8,128)S(1)}) custom-call(s32[1]{0:T(128)} %bitcast.own_ref, bf16[1,256,768]{2,1,0:T(8,128)(2,1)S(1)} %get-tuple-element.169.refs_0_.refs_4_.x0_ref, ...), custom_call_target="tpu_custom_call" | custom-call | flops 7699999744 | tf_op jit(solution)/shard_map/pull_tokens/pallas_call | solution.py:729
  160.8 1.2 fusion.1
  163.1 7.1 %pull_tokens.3 = (bf16[2,256,768]{2,1,0:T(8,128)(2,1)S(1)}, bf16[2,256,768]{2,1,0:T(8,128)(2,1)S(1)}, f32[1,4,96,384]{3,2,1,0:T(8,128)S(1)}, bf16[1,4,96,384]{3,2,1,0:T(8,128)(2,1)S(1)}) custom-call(s32[1]{0:T(128)} %bitcast.own_ref, bf16[1,256,768]{2,1,0:T(8,128)(2,1)S(1)} %get-tuple-element.179.refs_0_.x0_ref, ...), custom_call_target="tpu_custom_call" | custom-call | flops 7699999744 | tf_op jit(solution)/shard_map/pull_tokens/pallas_call | solution.py:729
  170.1 0.7 fusion.8
  170.9 1.9 collective-permute-start.36
  172.9 1.1 collective-permute-start.41
  174.2 1.1 collective-permute-start.42
  175.3 4.4 %collective-permute-done.36 = bf16[1,4,96,384]{3,2,1,0:T(8,128)(2,1)S(1)} collective-permute-done((bf16[1,4,96,384]{3,2,1,0:T(8,128)(2,1)S(1)}, bf16[1,4,96,384]{3,2,1,0:T(8,128)(2,1)S(1)}, u32[]{:S(2)}, u32[]{:S(2)}) %collective-permute-start.36) | collective-permute-done | bytes 294944 | tf_op jit(solution)/shard_map/swap_gfront_x1/ppermute | solution.py:553
  180.0 1.1 collective-permute-start.43
  181.9 1.6 collective-permute-start.38
  183.5 1.1 collective-permute-start.39
  184.6 1.7 collective-permute-start.40
  187.0 2.5 %collective-permute-done.39 = bf16[4,24,384]{2,1,0:T(8,128)(2,1)S(1)} collective-permute-done((bf16[4,24,384]{2,1,0:T(8,128)(2,1)S(1)}, bf16[4,24,384]{2,1,0:T(8,128)(2,1)S(1)}, u32[]{:S(2)}, u32[]{:S(2)}) %collective-permute-start.39) | collective-permute-done | bytes 73760 | tf_op jit(solution)/shard_map/swap_gfront_z2/ppermute | solution.py:557
  189.4 2.1 %collective-permute-done.40 = bf16[4,24,384]{2,1,0:T(8,128)(2,1)S(1)} collective-permute-done((bf16[4,24,384]{2,1,0:T(8,128)(2,1)S(1)}, bf16[4,24,384]{2,1,0:T(8,128)(2,1)S(1)}, u32[]{:S(2)}, u32[]{:S(2)}) %collective-permute-start.40) | collective-permute-done | bytes 73760 | tf_op jit(solution)/shard_map/swap_gfront_z3/ppermute | solution.py:557
  191.5 3.0 %collective-permute-done.43 = bf16[256,768]{1,0:T(8,128)(2,1)S(1)} collective-permute-done((bf16[256,768]{1,0:T(8,128)(2,1)S(1)}, bf16[256,768]{1,0:T(8,128)(2,1)S(1)}, u32[]{:S(2)}, u32[]{:S(2)}) %collective-permute-start.43) | collective-permute-done | bytes 393248 | tf_op jit(solution)/shard_map/swap_dtokens1_y/ppermute | solution.py:553
  194.6 1.1 collective-permute-start.45
  195.7 0.8 collective-permute-start.46
  196.8 1.3 maximum_add_fusion
  199.7 1.7 finish.1
  (146 shorter events, 13.1 us)
Async XLA Ops:
  0.6 7.1 %copy-start.5 = (bf16[2,256,768]{2,1,0:T(8,128)(2,1)S(1)}, bf16[2,256,768]{2,1,0:T(8,128)(2,1)}, u32[]{:S(2)}) copy-start(bf16[2,256,768]{2,1,0:T(8,128)(2,1)} %param.12) | copy-start | bytes 2359300
  4.6 3.3 %collective-permute-start = (bf16[24,1152]{1,0:T(8,128)(2,1)S(1)}, bf16[24,1152]{1,0:T(8,128)(2,1)S(1)}, u32[]{:S(2)}, u32[]{:S(2)}) collective-permute-start(bf16[24,1152]{1,0:T(8,128)(2,1)S(1)} %get-tuple-element.325), channel_id=1, source_target_pairs={{0,4},{4,0},{8,12},{12,8},{16,20},{20,16},{24,28},{28,24},{1,5},{5... | collective-permute-start | bytes 165896 | tf_op jit(solution)/shard_map/swap_pack_1/ppermute | solution.py:553
  5.1 5.1 %collective-permute-start.1 = (bf16[24,1152]{1,0:T(8,128)(2,1)S(1)}, bf16[24,1152]{1,0:T(8,128)(2,1)S(1)}, u32[]{:S(2)}, u32[]{:S(2)}) collective-permute-start(bf16[24,1152]{1,0:T(8,128)(2,1)S(1)} %get-tuple-element.324), channel_id=1, source_target_pairs={{0,16},{4,20},{8,24},{12,28},{16,0},{20,4},{24,8},{28,12},{1,17},{... | collective-permute-start | bytes 165896 | tf_op jit(solution)/shard_map/swap_pack_2/ppermute | solution.py:553
  7.7 3.8 %collective-permute-start.2 = (bf16[24,1152]{1,0:T(8,128)(2,1)S(1)}, bf16[24,1152]{1,0:T(8,128)(2,1)S(1)}, u32[]{:S(2)}, u32[]{:S(2)}) collective-permute-start(bf16[24,1152]{1,0:T(8,128)(2,1)S(1)} %get-tuple-element.323), channel_id=1, source_target_pairs={{0,20},{4,16},{8,28},{12,24},{16,4},{20,0},{24,12},{28,8},{1,21},{... | collective-permute-start | bytes 165896 | tf_op jit(solution)/shard_map/swap_pack_3/ppermute | solution.py:553
  11.5 11.8 %collective-permute-start.6 = (bf16[1,256,768]{2,1,0:T(8,128)(2,1)S(1)}, bf16[1,256,768]{2,1,0:T(8,128)(2,1)S(1)}, u32[]{:S(2)}, u32[]{:S(2)}) collective-permute-start(bf16[1,256,768]{2,1,0:T(8,128)(2,1)S(1)} %get-tuple-element.169.refs_0_.refs_4_.x0_ref), channel_id=1, source_target_pairs={{0,16},{4,20},{8,24},{12,28},{16,0},{20,4},{24,8},{28,12},{1,17},{... | collective-permute-start | bytes 1179656 | tf_op jit(solution)/shard_map/swap_tokens0_y/ppermute | solution.py:553
  12.7 20.5 %copy-start.1 = (bf16[2,256,768]{2,1,0:T(8,128)(2,1)S(1)}, bf16[2,256,768]{2,1,0:T(8,128)(2,1)}, u32[]{:S(2)}) copy-start(bf16[2,256,768]{2,1,0:T(8,128)(2,1)} %refs_0_) | copy-start | bytes 2359300
  12.7 23.4 %copy-start = (f32[2,256,128]{2,1,0:T(8,128)S(1)}, f32[2,256,128]{2,1,0:T(8,128)}, u32[]{:S(2)}) copy-start(f32[2,256,128]{2,1,0:T(8,128)} %constant.338.clone.refs_6_.refs_10_.place_ref) | copy-start | bytes 786436
  12.7 23.4 %copy-start.2 = (f32[2,8,128]{2,1,0:T(8,128)S(1)}, f32[2,8,128]{2,1,0:T(8,128)}, u32[]{:S(2)}) copy-start(f32[2,8,128]{2,1,0:T(8,128)} %constant.339.clone.refs_7_.refs_11_.start_ref) | copy-start | bytes 24580
  12.8 5.9 %collective-permute-start.3 = (bf16[4,24,384]{2,1,0:T(8,128)(2,1)S(1)}, bf16[4,24,384]{2,1,0:T(8,128)(2,1)S(1)}, u32[]{:S(2)}, u32[]{:S(2)}) collective-permute-start(bf16[4,24,384]{2,1,0:T(8,128)(2,1)S(1)} %bitcast.185), channel_id=1, source_target_pairs={{0,1},{1,0},{2,3},{3,2},{4,5},{5,4},{6,7},{7,6},{8,9},{9,8},{10,11... | collective-permute-start | bytes 221192 | tf_op jit(solution)/shard_map/swap_front_z1/ppermute | solution.py:557
  14.4 8.0 %collective-permute-start.4 = (bf16[4,24,384]{2,1,0:T(8,128)(2,1)S(1)}, bf16[4,24,384]{2,1,0:T(8,128)(2,1)S(1)}, u32[]{:S(2)}, u32[]{:S(2)}) collective-permute-start(bf16[4,24,384]{2,1,0:T(8,128)(2,1)S(1)} %bitcast.186), channel_id=1, source_target_pairs={{0,2},{1,3},{2,0},{3,1},{4,6},{5,7},{6,4},{7,5},{8,10},{9,11},{10,... | collective-permute-start | bytes 221192 | tf_op jit(solution)/shard_map/swap_front_z2/ppermute | solution.py:557
  17.0 6.3 %collective-permute-start.5 = (bf16[4,24,384]{2,1,0:T(8,128)(2,1)S(1)}, bf16[4,24,384]{2,1,0:T(8,128)(2,1)S(1)}, u32[]{:S(2)}, u32[]{:S(2)}) collective-permute-start(bf16[4,24,384]{2,1,0:T(8,128)(2,1)S(1)} %bitcast.187), channel_id=1, source_target_pairs={{0,3},{1,2},{2,1},{3,0},{4,7},{5,6},{6,5},{7,4},{8,11},{9,10},{10,... | collective-permute-start | bytes 221192 | tf_op jit(solution)/shard_map/swap_front_z3/ppermute | solution.py:557
  17.2 12.0 %collective-permute-start.13 = (bf16[1,1,96,768]{3,2,0,1:T(8,128)(2,1)}, bf16[1,1,96,768]{3,2,0,1:T(8,128)(2,1)}, u32[]{:S(2)}, u32[]{:S(2)}) collective-permute-start(bf16[1,1,96,768]{3,2,0,1:T(8,128)(2,1)} %bitcast.24), channel_id=1, source_target_pairs={{0,8},{4,12},{8,0},{12,4},{16,24},{20,28},{24,16},{28,20},{1,9},{5... | collective-permute-start | bytes 442376 | tf_op jit(solution)/shard_map/swap_down_x1/ppermute | solution.py:553
  18.7 14.5 %collective-permute-start.8 = (bf16[1,256,768]{2,1,0:T(8,128)(2,1)S(1)}, bf16[1,256,768]{2,1,0:T(8,128)(2,1)S(1)}, u32[]{:S(2)}, u32[]{:S(2)}) collective-permute-start(bf16[1,256,768]{2,1,0:T(8,128)(2,1)S(1)} %get-tuple-element.169.refs_0_.refs_4_.x0_ref), channel_id=1, source_target_pairs={{0,4},{4,0},{8,12},{12,8},{16,20},{20,16},{24,28},{28,24},{1,5},{5... | collective-permute-start | bytes 1179656 | tf_op jit(solution)/shard_map/swap_tokens0_c/ppermute | solution.py:553
  23.4 12.7 %collective-permute-start.9 = (bf16[1,256,768]{2,1,0:T(8,128)(2,1)S(1)}, bf16[1,256,768]{2,1,0:T(8,128)(2,1)S(1)}, u32[]{:S(2)}, u32[]{:S(2)}) collective-permute-start(bf16[1,256,768]{2,1,0:T(8,128)(2,1)S(1)} %collective-permute-done.6.refs_1_.refs_5_.x1_ref), channel_id=1, source_target_pairs={{0,4},{4,0},{8,12},{12,8},{16,20},{20,16},{24,28},{28,24},{1,5},{5... | collective-permute-start | bytes 1179656 | tf_op jit(solution)/shard_map/swap_tokens0_yc/ppermute | solution.py:553
  23.4 4.1 %collective-permute-start.11 = (bf16[24,768]{1,0:T(8,128)(2,1)}, bf16[24,768]{1,0:T(8,128)(2,1)S(1)}, u32[]{:S(2)}, u32[]{:S(2)}) collective-permute-start(bf16[24,768]{1,0:T(8,128)(2,1)} %param.15), channel_id=1, source_target_pairs={{0,0},{1,1},{2,2},{3,3},{8,4},{9,5},{10,6},{11,7},{4,8},{5,9},{6,1... | collective-permute-start | bytes 110600 | tf_op jit(solution)/shard_map/swap_out_moved/ppermute | solution.py:703
  24.9 11.1 %collective-permute-start.7 = (bf16[1,4,96,384]{3,2,1,0:T(8,128)(2,1)S(1)}, bf16[1,4,96,384]{3,2,1,0:T(8,128)(2,1)}, u32[]{:S(2)}, u32[]{:S(2)}) collective-permute-start(bf16[1,4,96,384]{3,2,1,0:T(8,128)(2,1)S(1)} %bitcast.157), channel_id=1, source_target_pairs={{0,8},{4,12},{8,0},{12,4},{16,24},{20,28},{24,16},{28,20},{1,9},{5... | collective-permute-start | bytes 884744 | tf_op jit(solution)/shard_map/swap_front_x1/ppermute | solution.py:553
  27.6 13.9 %collective-permute-start.10 = (bf16[1,256,768]{2,1,0:T(8,128)(2,1)S(1)}, bf16[1,256,768]{2,1,0:T(8,128)(2,1)}, u32[]{:S(2)}, u32[]{:S(2)}) collective-permute-start(bf16[1,256,768]{2,1,0:T(8,128)(2,1)S(1)} %get-tuple-element.179.refs_0_.x0_ref), channel_id=1, source_target_pairs={{0,16},{4,20},{8,24},{12,28},{16,0},{20,4},{24,8},{28,12},{1,17},{... | collective-permute-start | bytes 1179656 | tf_op jit(solution)/shard_map/swap_tokens1_y/ppermute | solution.py:553
  29.3 12.2 %collective-permute-start.12 = (bf16[5,1,24,768]{3,2,1,0:T(8,128)(2,1)}, bf16[5,1,24,768]{3,2,1,0:T(8,128)(2,1)}, u32[]{:S(2)}, u32[]{:S(2)}) collective-permute-start(bf16[5,1,24,768]{3,2,1,0:T(8,128)(2,1)} %get-tuple-element.327), channel_id=1, source_target_pairs={{0,2},{1,3},{2,0},{3,1},{4,6},{5,7},{6,4},{7,5},{8,10},{9,11},{10,... | collective-permute-start | bytes 552968 | tf_op jit(solution)/shard_map/swap_more_z2/ppermute | solution.py:557
  33.2 44.5 %collective-permute-start.21 = (bf16[2,256,768]{2,1,0:T(8,128)(2,1)S(1)}, bf16[2,256,768]{2,1,0:T(8,128)(2,1)S(1)}, u32[]{:S(2)}, u32[]{:S(2)}) collective-permute-start(bf16[2,256,768]{2,1,0:T(8,128)(2,1)S(1)} %copy-done.1), channel_id=1, source_target_pairs={{0,4},{4,0},{8,12},{12,8},{16,20},{20,16},{24,28},{28,24},{1,5},{5... | collective-permute-start | bytes 2359304 | tf_op jit(solution)/shard_map/swap_grads_c/ppermute | solution.py:553
  36.0 10.0 %collective-permute-start.15 = (bf16[1,256,768]{2,1,0:T(8,128)(2,1)S(1)}, bf16[1,256,768]{2,1,0:T(8,128)(2,1)S(1)}, u32[]{:S(2)}, u32[]{:S(2)}) collective-permute-start(bf16[1,256,768]{2,1,0:T(8,128)(2,1)S(1)} %get-tuple-element.179.refs_0_.x0_ref), channel_id=1, source_target_pairs={{0,4},{4,0},{8,12},{12,8},{16,20},{20,16},{24,28},{28,24},{1,5},{5... | collective-permute-start | bytes 1179656 | tf_op jit(solution)/shard_map/swap_tokens1_c/ppermute | solution.py:553
  41.5 7.0 %collective-permute-start.16 = (bf16[1,256,768]{2,1,0:T(8,128)(2,1)}, bf16[1,256,768]{2,1,0:T(8,128)(2,1)S(1)}, u32[]{:S(2)}, u32[]{:S(2)}) collective-permute-start(bf16[1,256,768]{2,1,0:T(8,128)(2,1)} %collective-permute-done.10.refs_1_.x1_ref), channel_id=1, source_target_pairs={{0,4},{4,0},{8,12},{12,8},{16,20},{20,16},{24,28},{28,24},{1,5},{5... | collective-permute-start | bytes 1179656 | tf_op jit(solution)/shard_map/swap_tokens1_yc/ppermute | solution.py:553
  41.9 13.5 %collective-permute-start.14 = (bf16[4,256,128]{2,1,0:T(8,128)(2,1)S(1)}, bf16[4,256,128]{2,1,0:T(8,128)(2,1)S(1)}, u32[]{:S(2)}, u32[]{:S(2)}) collective-permute-start(bf16[4,256,128]{2,1,0:T(8,128)(2,1)S(1)} %get-tuple-element.240.refs_0_), channel_id=1, source_target_pairs={{0,8},{4,12},{8,0},{12,4},{16,24},{20,28},{24,16},{28,20},{1,9},{5... | collective-permute-start | bytes 786440 | tf_op jit(solution)/shard_map/swap_keyval0_x1/ppermute | solution.py:553
  42.7 22.6 %collective-permute-start.18 = (bf16[2,256,768]{2,1,0:T(8,128)(2,1)S(1)}, bf16[2,256,768]{2,1,0:T(8,128)(2,1)S(1)}, u32[]{:S(2)}, u32[]{:S(2)}) collective-permute-start(bf16[2,256,768]{2,1,0:T(8,128)(2,1)S(1)} %copy-done.1), channel_id=1, source_target_pairs={{0,16},{4,20},{8,24},{12,28},{16,0},{20,4},{24,8},{28,12},{1,17},{... | collective-permute-start | bytes 2359304 | tf_op jit(solution)/shard_map/swap_grads_y/ppermute | solution.py:553
  46.0 19.3 %collective-permute-start.19 = (bf16[2,1,1,96,768]{4,3,1,0,2:T(8,128)(2,1)S(1)}, bf16[2,1,1,96,768]{4,3,1,0,2:T(8,128)(2,1)S(1)}, u32[]{:S(2)}, u32[]{:S(2)}) collective-permute-start(bf16[2,1,1,96,768]{4,3,1,0,2:T(8,128)(2,1)S(1)} %bitcast.172), channel_id=1, source_target_pairs={{0,2},{1,3},{2,0},{3,1},{4,6},{5,7},{6,4},{7,5},{8,10},{9,11},{10,... | collective-permute-start | bytes 884744 | tf_op jit(solution)/shard_map/swap_down_z2/ppermute | solution.py:557
  48.5 16.8 %collective-permute-start.20 = (bf16[5,2,24,768]{3,2,1,0:T(8,128)(2,1)S(1)}, bf16[5,2,24,768]{3,2,1,0:T(8,128)(2,1)S(1)}, u32[]{:S(2)}, u32[]{:S(2)}) collective-permute-start(bf16[5,2,24,768]{3,2,1,0:T(8,128)(2,1)S(1)} %maximum_select_fusion.3), channel_id=1, source_target_pairs={{0,1},{1,0},{2,3},{3,2},{4,5},{5,4},{6,7},{7,6},{8,9},{9,8},{10,11... | collective-permute-start | bytes 1105928 | tf_op jit(solution)/shard_map/swap_more_z1/ppermute | solution.py:557
  55.3 9.2 %copy-start.3 = (bf16[4,2,256,768]{3,2,1,0:T(8,128)(2,1)}, bf16[4,2,256,768]{3,2,1,0:T(8,128)(2,1)S(1)}, u32[]{:S(2)}) copy-start(bf16[4,2,256,768]{3,2,1,0:T(8,128)(2,1)S(1)} %get-tuple-element.210.refs_4_) | copy-start | bytes 9437188
  55.4 9.9 %collective-permute-start.17 = (bf16[4,256,128]{2,1,0:T(8,128)(2,1)S(1)}, bf16[4,256,128]{2,1,0:T(8,128)(2,1)S(1)}, u32[]{:S(2)}, u32[]{:S(2)}) collective-permute-start(bf16[4,256,128]{2,1,0:T(8,128)(2,1)S(1)} %get-tuple-element.241.refs_0_), channel_id=1, source_target_pairs={{0,8},{4,12},{8,0},{12,4},{16,24},{20,28},{24,16},{28,20},{1,9},{5... | collective-permute-start | bytes 786440 | tf_op jit(solution)/shard_map/swap_keyval1_x1/ppermute | solution.py:553
  65.3 20.9 %collective-permute-start.22 = (bf16[2,256,768]{2,1,0:T(8,128)(2,1)S(1)}, bf16[2,256,768]{2,1,0:T(8,128)(2,1)S(1)}, u32[]{:S(2)}, u32[]{:S(2)}) collective-permute-start(bf16[2,256,768]{2,1,0:T(8,128)(2,1)S(1)} %collective-permute-done.18.refs_1_), channel_id=1, source_target_pairs={{0,4},{4,0},{8,12},{12,8},{16,20},{20,16},{24,28},{28,24},{1,5},{5... | collective-permute-start | bytes 2359304 | tf_op jit(solution)/shard_map/swap_grads_yc/ppermute | solution.py:553
  65.5 20.7 %collective-permute-start.23 = (bf16[1,5,96,768]{3,2,1,0:T(8,128)(2,1)S(1)}, bf16[1,5,96,768]{3,2,1,0:T(8,128)(2,1)S(1)}, u32[]{:S(2)}, u32[]{:S(2)}) collective-permute-start(bf16[1,5,96,768]{3,2,1,0:T(8,128)(2,1)S(1)} %bitcast.159), channel_id=1, source_target_pairs={{0,8},{4,12},{8,0},{12,4},{16,24},{20,28},{24,16},{28,20},{1,9},{5... | collective-permute-start | bytes 2211848 | tf_op jit(solution)/shard_map/swap_more_x1/ppermute | solution.py:553
  69.1 15.5 %collective-permute-start.24 = (bf16[2,2,1,96,768]{4,3,1,0,2:T(8,128)(2,1)S(1)}, bf16[2,2,1,96,768]{4,3,1,0,2:T(8,128)(2,1)S(1)}, u32[]{:S(2)}, u32[]{:S(2)}) collective-permute-start(bf16[2,2,1,96,768]{4,3,1,0,2:T(8,128)(2,1)S(1)} %maximum_select_fusion.1), channel_id=1, source_target_pairs={{0,1},{1,0},{2,3},{3,2},{4,5},{5,4},{6,7},{7,6},{8,9},{9,8},{10,11... | collective-permute-start | bytes 1769480 | tf_op jit(solution)/shard_map/swap_down_z1/ppermute | solution.py:557
  111.6 19.0 %collective-permute-start.25 = (bf16[2,2,256,768]{3,2,1,0:T(8,128)(2,1)S(1)}, bf16[2,2,256,768]{3,2,1,0:T(8,128)(2,1)S(1)}, u32[]{:S(2)}, u32[]{:S(2)}) collective-permute-start(bf16[2,2,256,768]{3,2,1,0:T(8,128)(2,1)S(1)} %get-tuple-element.221), channel_id=1, source_target_pairs={{0,4},{4,0},{8,12},{12,8},{16,20},{20,16},{24,28},{28,24},{1,5},{5... | collective-permute-start | bytes 4718600 | tf_op jit(solution)/shard_map/swap_made_c/ppermute | solution.py:553
  111.7 18.9 %collective-permute-start.26 = (bf16[1,5,96,768]{3,2,1,0:T(8,128)(2,1)S(1)}, bf16[1,5,96,768]{3,2,1,0:T(8,128)(2,1)S(1)}, u32[]{:S(2)}, u32[]{:S(2)}) collective-permute-start(bf16[1,5,96,768]{3,2,1,0:T(8,128)(2,1)S(1)} %get-tuple-element.223), channel_id=1, source_target_pairs={{0,8},{4,12},{8,0},{12,4},{16,24},{20,28},{24,16},{28,20},{1,9},{5... | collective-permute-start | bytes 2211848 | tf_op jit(solution)/shard_map/swap_gmore_x1/ppermute | solution.py:553
  113.5 15.4 %collective-permute-start.27 = (bf16[2,2,96,768]{3,2,1,0:T(8,128)(2,1)S(1)}, bf16[2,2,96,768]{3,2,1,0:T(8,128)(2,1)S(1)}, u32[]{:S(2)}, u32[]{:S(2)}) collective-permute-start(bf16[2,2,96,768]{3,2,1,0:T(8,128)(2,1)S(1)} %get-tuple-element.225), channel_id=1, source_target_pairs={{0,1},{1,0},{2,3},{3,2},{4,5},{5,4},{6,7},{7,6},{8,9},{9,8},{10,11... | collective-permute-start | bytes 1769480 | tf_op jit(solution)/shard_map/swap_gdown_z1/ppermute | solution.py:557
  131.0 19.2 %collective-permute-start.28 = (bf16[2,256,768]{2,1,0:T(8,128)(2,1)S(1)}, bf16[2,256,768]{2,1,0:T(8,128)(2,1)S(1)}, u32[]{:S(2)}, u32[]{:S(2)}) collective-permute-start(bf16[2,256,768]{2,1,0:T(8,128)(2,1)S(1)} %fusion.2), channel_id=1, source_target_pairs={{0,16},{4,20},{8,24},{12,28},{16,0},{20,4},{24,8},{28,12},{1,17},{... | collective-permute-start | bytes 2359304 | tf_op jit(solution)/shard_map/swap_made_y/ppermute | solution.py:553
  132.1 15.0 %collective-permute-start.29 = (bf16[5,2,24,768]{3,2,0,1:T(8,128)(2,1)S(1)}, bf16[5,2,24,768]{3,2,0,1:T(8,128)(2,1)S(1)}, u32[]{:S(2)}, u32[]{:S(2)}) collective-permute-start(bf16[5,2,24,768]{3,2,0,1:T(8,128)(2,1)S(1)} %fusion.7), channel_id=1, source_target_pairs={{0,1},{1,0},{2,3},{3,2},{4,5},{5,4},{6,7},{7,6},{8,9},{9,8},{10,11... | collective-permute-start | bytes 1105928 | tf_op jit(solution)/shard_map/swap_gmore_z1/ppermute | solution.py:557
  132.8 13.8 %collective-permute-start.30 = (bf16[4,256,128]{2,1,0:T(8,128)(2,1)S(1)}, bf16[4,256,128]{2,1,0:T(8,128)(2,1)S(1)}, u32[]{:S(2)}, u32[]{:S(2)}) collective-permute-start(bf16[4,256,128]{2,1,0:T(8,128)(2,1)S(1)} %get-tuple-element.232), channel_id=1, source_target_pairs={{0,8},{4,12},{8,0},{12,4},{16,24},{20,28},{24,16},{28,20},{1,9},{5... | collective-permute-start | bytes 786440 | tf_op jit(solution)/shard_map/swap_gkeyval0_x1/ppermute | solution.py:553
  134.7 27.2 %collective-permute-start.31 = (bf16[2,1,96,768]{3,2,1,0:T(8,128)(2,1)S(1)}, bf16[2,1,96,768]{3,2,1,0:T(8,128)(2,1)S(1)}, u32[]{:S(2)}, u32[]{:S(2)}) collective-permute-start(bf16[2,1,96,768]{3,2,1,0:T(8,128)(2,1)S(1)} %dynamic-slice_convert_fusion), channel_id=1, source_target_pairs={{0,2},{1,3},{2,0},{3,1},{4,6},{5,7},{6,4},{7,5},{8,10},{9,11},{10,... | collective-permute-start | bytes 884744 | tf_op jit(solution)/shard_map/swap_gdown_z2/ppermute | solution.py:557
  150.2 3.5 %copy-start.4 = (bf16[2,256,128]{2,1,0:T(8,128)(2,1)S(1)}, bf16[2,256,128]{2,1,0:T(8,128)(2,1)}, u32[]{:S(2)}) copy-start(bf16[2,256,128]{2,1,0:T(8,128)(2,1)} %cotangent_ref.3) | copy-start | bytes 393220
  150.3 11.7 %collective-permute-start.32 = (bf16[5,1,24,768]{3,2,0,1:T(8,128)(2,1)S(1)}, bf16[5,1,24,768]{3,2,0,1:T(8,128)(2,1)S(1)}, u32[]{:S(2)}, u32[]{:S(2)}) collective-permute-start(bf16[5,1,24,768]{3,2,0,1:T(8,128)(2,1)S(1)} %dynamic-slice_convert_fusion.1), channel_id=1, source_target_pairs={{0,2},{1,3},{2,0},{3,1},{4,6},{5,7},{6,4},{7,5},{8,10},{9,11},{10,... | collective-permute-start | bytes 552968 | tf_op jit(solution)/shard_map/swap_gmore_z2/ppermute | solution.py:557
  150.7 11.3 %collective-permute-start.33 = (bf16[4,256,128]{2,1,0:T(8,128)(2,1)S(1)}, bf16[4,256,128]{2,1,0:T(8,128)(2,1)S(1)}, u32[]{:S(2)}, u32[]{:S(2)}) collective-permute-start(bf16[4,256,128]{2,1,0:T(8,128)(2,1)S(1)} %get-tuple-element.254), channel_id=1, source_target_pairs={{0,8},{4,12},{8,0},{12,4},{16,24},{20,28},{24,16},{28,20},{1,9},{5... | collective-permute-start | bytes 786440 | tf_op jit(solution)/shard_map/swap_gkeyval1_x1/ppermute | solution.py:553
  153.7 7.0 %copy-start.6 = (bf16[2,256,768]{2,1,0:T(8,128)(2,1)S(1)}, bf16[2,256,768]{2,1,0:T(8,128)(2,1)}, u32[]{:S(2)}) copy-start(bf16[2,256,768]{2,1,0:T(8,128)(2,1)} %param.12) | copy-start | bytes 2359300
  162.0 8.9 %collective-permute-start.34 = (bf16[2,256,768]{2,1,0:T(8,128)(2,1)S(1)}, bf16[2,256,768]{2,1,0:T(8,128)(2,1)S(1)}, u32[]{:S(2)}, u32[]{:S(2)}) collective-permute-start(bf16[2,256,768]{2,1,0:T(8,128)(2,1)S(1)} %get-tuple-element.265), channel_id=1, source_target_pairs={{0,4},{4,0},{8,12},{12,8},{16,20},{20,16},{24,28},{28,24},{1,5},{5... | collective-permute-start | bytes 2359304 | tf_op jit(solution)/shard_map/swap_dtokens0_c/ppermute | solution.py:553
  162.2 8.7 %collective-permute-start.35 = (bf16[2,24,768]{2,1,0:T(8,128)(2,1)S(1)}, bf16[2,24,768]{2,1,0:T(8,128)(2,1)S(1)}, u32[]{:S(2)}, u32[]{:S(2)}) collective-permute-start(bf16[2,24,768]{2,1,0:T(8,128)(2,1)S(1)} %fusion.14), channel_id=1, source_target_pairs={{0,4},{4,0},{8,12},{12,8},{16,20},{20,16},{24,28},{28,24},{1,5},{5... | collective-permute-start | bytes 221192 | tf_op jit(solution)/shard_map/swap_gup_c/ppermute | solution.py:553
  162.8 7.3 %collective-permute-start.48 = (bf16[1,96,768]{2,1,0:T(8,128)(2,1)S(1)}, bf16[1,96,768]{2,1,0:T(8,128)(2,1)S(1)}, u32[]{:S(2)}, u32[]{:S(2)}) collective-permute-start(bf16[1,96,768]{2,1,0:T(8,128)(2,1)S(1)} %fusion.9), channel_id=1, source_target_pairs={{0,8},{4,12},{8,0},{12,4},{16,24},{20,28},{24,16},{28,20},{1,9},{5... | collective-permute-start | bytes 442376 | tf_op jit(solution)/shard_map/swap_gdown_x1/ppermute | solution.py:553
  170.9 8.8 %collective-permute-start.36 = (bf16[1,4,96,384]{3,2,1,0:T(8,128)(2,1)S(1)}, bf16[1,4,96,384]{3,2,1,0:T(8,128)(2,1)S(1)}, u32[]{:S(2)}, u32[]{:S(2)}) collective-permute-start(bf16[1,4,96,384]{3,2,1,0:T(8,128)(2,1)S(1)} %get-tuple-element.271), channel_id=1, source_target_pairs={{0,8},{4,12},{8,0},{12,4},{16,24},{20,28},{24,16},{28,20},{1,9},{5... | collective-permute-start | bytes 884744 | tf_op jit(solution)/shard_map/swap_gfront_x1/ppermute | solution.py:553
  172.8 6.9 %collective-permute-start.37 = (bf16[2,256,768]{2,1,0:T(8,128)(2,1)S(1)}, bf16[2,256,768]{2,1,0:T(8,128)(2,1)S(1)}, u32[]{:S(2)}, u32[]{:S(2)}) collective-permute-start(bf16[2,256,768]{2,1,0:T(8,128)(2,1)S(1)} %get-tuple-element.272), channel_id=1, source_target_pairs={{0,4},{4,0},{8,12},{12,8},{16,20},{20,16},{24,28},{28,24},{1,5},{5... | collective-permute-start | bytes 2359304 | tf_op jit(solution)/shard_map/swap_dtokens1_c/ppermute | solution.py:553
  172.9 10.6 %collective-permute-start.41 = (bf16[24,1536]{1,0:T(8,128)(2,1)S(1)}, bf16[24,1536]{1,0:T(8,128)(2,1)S(1)}, u32[]{:S(2)}, u32[]{:S(2)}) collective-permute-start(bf16[24,1536]{1,0:T(8,128)(2,1)S(1)} %fusion.18), channel_id=1, source_target_pairs={{0,16},{4,20},{8,24},{12,28},{16,0},{20,4},{24,8},{28,12},{1,17},{... | collective-permute-start | bytes 221192 | tf_op jit(solution)/shard_map/swap_gup_y/ppermute | solution.py:553
  174.2 12.8 %collective-permute-start.42 = (bf16[256,768]{1,0:T(8,128)(2,1)S(1)}, bf16[256,768]{1,0:T(8,128)(2,1)S(1)}, u32[]{:S(2)}, u32[]{:S(2)}) collective-permute-start(bf16[256,768]{1,0:T(8,128)(2,1)S(1)} %fusion.5), channel_id=1, source_target_pairs={{0,16},{4,20},{8,24},{12,28},{16,0},{20,4},{24,8},{28,12},{1,17},{... | collective-permute-start | bytes 1179656 | tf_op jit(solution)/shard_map/swap_dtokens0_y/ppermute | solution.py:553
  180.0 14.5 %collective-permute-start.43 = (bf16[256,768]{1,0:T(8,128)(2,1)S(1)}, bf16[256,768]{1,0:T(8,128)(2,1)S(1)}, u32[]{:S(2)}, u32[]{:S(2)}) collective-permute-start(bf16[256,768]{1,0:T(8,128)(2,1)S(1)} %fusion.6), channel_id=1, source_target_pairs={{0,16},{4,20},{8,24},{12,28},{16,0},{20,4},{24,8},{28,12},{1,17},{... | collective-permute-start | bytes 1179656 | tf_op jit(solution)/shard_map/swap_dtokens1_y/ppermute | solution.py:553
  181.1 3.6 %collective-permute-start.47 = (bf16[24,768]{1,0:T(8,128)(2,1)S(1)}, bf16[24,768]{1,0:T(8,128)(2,1)S(1)}, u32[]{:S(2)}, u32[]{:S(2)}) collective-permute-start(bf16[24,768]{1,0:T(8,128)(2,1)S(1)} %fusion.19), channel_id=1, source_target_pairs={{0,0},{1,1},{2,2},{3,3},{4,8},{5,9},{6,10},{7,11},{8,4},{9,5},{10,... | collective-permute-start | bytes 110600 | tf_op jit(solution)/shard_map/swap_gout_moved/ppermute | solution.py:1048
  181.9 5.1 %collective-permute-start.38 = (bf16[4,24,384]{2,1,0:T(8,128)(2,1)S(1)}, bf16[4,24,384]{2,1,0:T(8,128)(2,1)S(1)}, u32[]{:S(2)}, u32[]{:S(2)}) collective-permute-start(bf16[4,24,384]{2,1,0:T(8,128)(2,1)S(1)} %get-tuple-element.308), channel_id=1, source_target_pairs={{0,1},{1,0},{2,3},{3,2},{4,5},{5,4},{6,7},{7,6},{8,9},{9,8},{10,11... | collective-permute-start | bytes 221192 | tf_op jit(solution)/shard_map/swap_gfront_z1/ppermute | solution.py:557
  183.5 5.9 %collective-permute-start.39 = (bf16[4,24,384]{2,1,0:T(8,128)(2,1)S(1)}, bf16[4,24,384]{2,1,0:T(8,128)(2,1)S(1)}, u32[]{:S(2)}, u32[]{:S(2)}) collective-permute-start(bf16[4,24,384]{2,1,0:T(8,128)(2,1)S(1)} %get-tuple-element.307), channel_id=1, source_target_pairs={{0,2},{1,3},{2,0},{3,1},{4,6},{5,7},{6,4},{7,5},{8,10},{9,11},{10,... | collective-permute-start | bytes 221192 | tf_op jit(solution)/shard_map/swap_gfront_z2/ppermute | solution.py:557
  184.6 6.9 %collective-permute-start.40 = (bf16[4,24,384]{2,1,0:T(8,128)(2,1)S(1)}, bf16[4,24,384]{2,1,0:T(8,128)(2,1)S(1)}, u32[]{:S(2)}, u32[]{:S(2)}) collective-permute-start(bf16[4,24,384]{2,1,0:T(8,128)(2,1)S(1)} %get-tuple-element.306), channel_id=1, source_target_pairs={{0,3},{1,2},{2,1},{3,0},{4,7},{5,6},{6,5},{7,4},{8,11},{9,10},{10,... | collective-permute-start | bytes 221192 | tf_op jit(solution)/shard_map/swap_gfront_z3/ppermute | solution.py:557
  194.5 2.3 %copy-start.7 = (f32[4,24,384]{2,1,0:T(8,128)}, f32[4,24,384]{2,1,0:T(8,128)S(1)}, u32[]{:S(2)}) copy-start(f32[4,24,384]{2,1,0:T(8,128)S(1)} %convert_add_fusion.11.mine_ref) | copy-start | bytes 442372
  194.6 3.6 %collective-permute-start.44 = (bf16[24,384]{1,0:T(8,128)(2,1)S(1)}, bf16[24,384]{1,0:T(8,128)(2,1)S(1)}, u32[]{:S(2)}, u32[]{:S(2)}) collective-permute-start(bf16[24,384]{1,0:T(8,128)(2,1)S(1)} %get-tuple-element.330), channel_id=1, source_target_pairs={{0,4},{4,0},{8,12},{12,8},{16,20},{20,16},{24,28},{28,24},{1,5},{5... | collective-permute-start | bytes 55304 | tf_op jit(solution)/shard_map/swap_gfront_1/ppermute | solution.py:553
  194.6 3.8 %collective-permute-start.45 = (bf16[24,384]{1,0:T(8,128)(2,1)S(1)}, bf16[24,384]{1,0:T(8,128)(2,1)S(1)}, u32[]{:S(2)}, u32[]{:S(2)}) collective-permute-start(bf16[24,384]{1,0:T(8,128)(2,1)S(1)} %get-tuple-element.329), channel_id=1, source_target_pairs={{0,16},{4,20},{8,24},{12,28},{16,0},{20,4},{24,8},{28,12},{1,17},{... | collective-permute-start | bytes 55304 | tf_op jit(solution)/shard_map/swap_gfront_2/ppermute | solution.py:553
  195.7 3.2 %collective-permute-start.46 = (bf16[24,384]{1,0:T(8,128)(2,1)S(1)}, bf16[24,384]{1,0:T(8,128)(2,1)S(1)}, u32[]{:S(2)}, u32[]{:S(2)}) collective-permute-start(bf16[24,384]{1,0:T(8,128)(2,1)S(1)} %get-tuple-element.328), channel_id=1, source_target_pairs={{0,20},{4,16},{8,28},{12,24},{16,4},{20,0},{24,12},{28,8},{1,21},{... | collective-permute-start | bytes 55304 | tf_op jit(solution)/shard_map/swap_gfront_3/ppermute | solution.py:553
  198.2 3.2 %copy-start.8 = (f32[24,3072]{1,0:T(8,128)}, f32[24,3072]{1,0:T(8,128)S(1)}, u32[]{:S(2)}) copy-start(f32[24,3072]{1,0:T(8,128)S(1)} %slice_dynamic-update-slice_fusion) | copy-start | bytes 884740
  198.2 0.8 copy-start.9
  198.5 0.6 copy-start.10
  199.1 0.6 copy-start.11

commit v2 on v1

--- a/solution.py
+++ b/solution.py
@@ -941,7 +941,7 @@
     (d_queries, kept, sent, made, got_y, more_z, keys_got) = hold(
         d_queries, kept, sent, made, got_y, more_z, keys_got
     )
-    output = (inputs.astype(F32) + made[0] + got_y.astype(F32)).astype(BF)
+    made_rows, made_got = made[0], got_y
     more_grads = add_z(more_z)
     keys_gots = [keys_got] + [flip_x(sent[b], f"gkeyval{b}") for b in range(1, count)]
 
@@ -1034,7 +1034,6 @@
     front_keep, front_send, pulled, got_c, ups_c = hold(front_keep, front_send, pulled, got_c, ups_c)
     ups = jnp.concatenate(join_c(more_grads[:TEAM], ups_c), axis=-1)
     ups_y = flip(pick(ups, 1 - own_y, 0).astype(BF), top, "gup_y")
-    down_grads = scatter_x(down_keep, down_got, "gdown")
 
     def add_c(pair, got):
         return pair[0].astype(F32) + got.astype(F32)
@@ -1043,7 +1042,12 @@
     halves = [add_c(pulled[0], got_c)]
     got_y = flip(halves[0][1].astype(BF), top, "dtokens0_y")
     gots_c = [flip(pulled[b][1], 1, f"dtokens{b}_c") for b in range(1, count)]
-    front_keep, front_got, gots_c, more_grads = hold(front_keep, front_got, gots_c, more_grads)
+    made_got, down_got = hold(made_got, down_got, front_send)[:2]
+    down_grads = scatter_x(down_keep, down_got, "gdown")
+    output = (inputs.astype(F32) + made_rows + made_got.astype(F32)).astype(BF)
+    front_keep, front_got, gots_c, more_grads, output = hold(
+        front_keep, front_got, gots_c, more_grads, output
+    )
     with jax.named_scope("swap_gout_moved"):
         grad_out = lax.ppermute(more_grads[TEAM].astype(BF), ("seq", "dp"), moved(False)).astype(F32)
     halves += [add_c(pulled[b], gots_c[b - 1]) for b in range(1, count)]

time: 202 us -> 199 us (0.985)
  waiting for transfers between devices: 40.3 us -> 37.7 us
    ppermute x14, waiting for transfers between devices: 20.5 us -> 13.3 us  [flip_z(): return lax.ppermute(value, 'dp', [(i, i ^ mask) for i in range(ndp)])]
    ppermute x33, waiting for transfers between devices: 19.8 us -> 24.3 us  [flip(): return lax.ppermute(value, 'seq', [(i, i ^ mask) for i in range(nseq)])]
    ppermute x14, starting transfers between devices: 18.1 us -> 20.4 us  [flip_z(): return lax.ppermute(value, 'dp', [(i, i ^ mask) for i in range(ndp)])]
  transfers between devices with their start and end apart: 49 -> 49, of which waited for: 18 -> 16; matrix products, arithmetic and copies ran while one was open for 6% -> 6% of each run, Pallas kernels for 31% -> 31%
where the time goes in v2:
time: 199 us
  Pallas kernels  89.7 us (45%)
  starting transfers between devices  53.8 us (27%)
  waiting for transfers between devices  37.7 us (19%)
  other arithmetic  11.9 us (6%)
  local copies, waits for them, and re-layouts  4.49 us (2%)
    pallas_call x9, Pallas kernels, call(): pl.pallas_call(kernel, grid_spec=pltpu.PrefetchScalarGridSpec(num_scalar_...  88.1 us
    ppermute x33, starting transfers between devices, flip(): return lax.ppermute(value, 'seq', [(i, i ^ mask) for i in range(nseq)])  31.2 us
    ppermute x33, waiting for transfers between devices, flip(): return lax.ppermute(value, 'seq', [(i, i ^ mask) for i in range(nseq)])  24.3 us
    ppermute x14, starting transfers between devices, flip_z(): return lax.ppermute(value, 'dp', [(i, i ^ mask) for i in range(ndp)])  20.4 us
    ppermute x14, waiting for transfers between devices, flip_z(): return lax.ppermute(value, 'dp', [(i, i ^ mask) for i in range(ndp)])  13.3 us
  transfers between devices with their start and end apart: 49, of which 16 were waited for; matrix products, arithmetic and copies ran while one was open for 6% of the time, Pallas kernels for 31%

profile of v2, /device:TPU:0, one launch (start us, length us, event | category | flops | bytes accessed | tf_op | source)
XLA Modules:
  0.0 199.0 jit_solution(27571194508764832)
XLA Ops:
  0.7 1.1 reshape.315
  2.0 0.9 reshape.314
  2.9 0.7 pad_maximum_fusion.8
  3.7 0.7 broadcast_in_dim.15
  5.1 2.6 %collective-permute-start.1 = (bf16[24,1152]{1,0:T(8,128)(2,1)S(1)}, bf16[24,1152]{1,0:T(8,128)(2,1)S(1)}, u32[]{:S(2)}, u32[]{:S(2)}) collective-permute-start(bf16[24,1152]{1,0:T(8,128)(2,1)S(1)} %get-tuple-element.330), channel_id=1, source_target_pairs={{0,16},{4,20},{8,24},{12,28},{16,0},{20,4},{24,8},{28,12},{1,17},{... | collective-permute-start | bytes 165896 | tf_op jit(solution)/shard_map/swap_pack_2/ppermute | solution.py:553
  7.8 2.3 %collective-permute-done.1 = bf16[24,1152]{1,0:T(8,128)(2,1)S(1)} collective-permute-done((bf16[24,1152]{1,0:T(8,128)(2,1)S(1)}, bf16[24,1152]{1,0:T(8,128)(2,1)S(1)}, u32[]{:S(2)}, u32[]{:S(2)}) %collective-permute-start.1) | collective-permute-done | bytes 55328 | tf_op jit(solution)/shard_map/swap_pack_2/ppermute | solution.py:553
  10.1 1.4 collective-permute-done.2
  11.5 1.1 collective-permute-start.6
  12.7 1.6 collective-permute-start.3
  14.4 2.6 %collective-permute-start.4 = (bf16[4,24,384]{2,1,0:T(8,128)(2,1)S(1)}, bf16[4,24,384]{2,1,0:T(8,128)(2,1)S(1)}, u32[]{:S(2)}, u32[]{:S(2)}) collective-permute-start(bf16[4,24,384]{2,1,0:T(8,128)(2,1)S(1)} %bitcast.186), channel_id=1, source_target_pairs={{0,2},{1,3},{2,0},{3,1},{4,6},{5,7},{6,4},{7,5},{8,10},{9,11},{10,... | collective-permute-start | bytes 221192 | tf_op jit(solution)/shard_map/swap_front_z2/ppermute | solution.py:557
  17.2 1.5 collective-permute-start.13
  18.7 3.7 %collective-permute-done.4 = bf16[4,24,384]{2,1,0:T(8,128)(2,1)S(1)} collective-permute-done((bf16[4,24,384]{2,1,0:T(8,128)(2,1)S(1)}, bf16[4,24,384]{2,1,0:T(8,128)(2,1)S(1)}, u32[]{:S(2)}, u32[]{:S(2)}) %collective-permute-start.4) | collective-permute-done | bytes 73760 | tf_op jit(solution)/shard_map/swap_front_z2/ppermute | solution.py:557
  22.4 0.8 collective-permute-done.5
  23.3 1.4 collective-permute-start.11
  24.8 2.2 %collective-permute-start.9 = (bf16[1,256,768]{2,1,0:T(8,128)(2,1)S(1)}, bf16[1,256,768]{2,1,0:T(8,128)(2,1)S(1)}, u32[]{:S(2)}, u32[]{:S(2)}) collective-permute-start(bf16[1,256,768]{2,1,0:T(8,128)(2,1)S(1)} %collective-permute-done.6.refs_1_.refs_5_.x1_ref), channel_id=1, source_target_pairs={{0,4},{4,0},{8,12},{12,8},{16,20},{20,16},{24,28},{28,24},{1,5},{5... | collective-permute-start | bytes 1179656 | tf_op jit(solution)/shard_map/swap_tokens0_yc/ppermute | solution.py:553
  27.1 1.0 collective-permute-start.10
  28.1 0.7 fusion.12
  28.8 2.4 %collective-permute-start.12 = (bf16[5,1,24,768]{3,2,1,0:T(8,128)(2,1)}, bf16[5,1,24,768]{3,2,1,0:T(8,128)(2,1)}, u32[]{:S(2)}, u32[]{:S(2)}) collective-permute-start(bf16[5,1,24,768]{3,2,1,0:T(8,128)(2,1)} %get-tuple-element.333), channel_id=1, source_target_pairs={{0,2},{1,3},{2,0},{3,1},{4,6},{5,7},{6,4},{7,5},{8,10},{9,11},{10,... | collective-permute-start | bytes 552968 | tf_op jit(solution)/shard_map/swap_more_z2/ppermute | solution.py:557
  31.7 1.0 pad_maximum_fusion.4
  32.7 1.0 collective-permute-start.21
  33.8 2.4 %collective-permute-done.7.refs_5_ = bf16[1,4,96,384]{3,2,1,0:T(8,128)(2,1)} collective-permute-done((bf16[1,4,96,384]{3,2,1,0:T(8,128)(2,1)S(1)}, bf16[1,4,96,384]{3,2,1,0:T(8,128)(2,1)}, u32[]{:S(2)}, u32[]{:S(2)}) %collective-permute-start.7) | collective-permute-done | bytes 294944 | tf_op jit(solution)/shard_map/swap_front_x1/ppermute | solution.py:553
  36.2 5.2 %prepare.2 = (bf16[4,256,256]{2,1,0:T(8,128)(2,1)S(1)}, bf16[4,256,128]{2,1,0:T(8,128)(2,1)S(1)}, bf16[768,384]{1,0:T(8,128)(2,1)S(1)}, f32[8,768]{1,0:T(8,128)S(1)}) custom-call(s32[1]{0:T(128)} %bitcast.own_ref, bf16[1,256,768]{2,1,0:T(8,128)(2,1)S(1)} %get-tuple-element.173.refs_0_.refs_4_.x0_ref, ...), custom_call_target="tpu_custom_call" | custom-call | flops 550000000 | tf_op jit(solution)/shard_map/prepare/pallas_call | solution.py:729
  42.0 1.3 maximum_select_fusion.3
  43.2 1.4 collective-permute-start.20
  45.2 1.1 pad_maximum_fusion
  46.4 1.0 collective-permute-start.18
  47.4 2.6 %collective-permute-start.19 = (bf16[2,1,1,96,768]{4,3,1,0,2:T(8,128)(2,1)S(1)}, bf16[2,1,1,96,768]{4,3,1,0,2:T(8,128)(2,1)S(1)}, u32[]{:S(2)}, u32[]{:S(2)}) collective-permute-start(bf16[2,1,1,96,768]{4,3,1,0,2:T(8,128)(2,1)S(1)} %bitcast.172), channel_id=1, source_target_pairs={{0,2},{1,3},{2,0},{3,1},{4,6},{5,7},{6,4},{7,5},{8,10},{9,11},{10,... | collective-permute-start | bytes 884744 | tf_op jit(solution)/shard_map/swap_down_z2/ppermute | solution.py:557
  50.0 5.3 %prepare.3 = (bf16[4,256,256]{2,1,0:T(8,128)(2,1)S(1)}, bf16[4,256,128]{2,1,0:T(8,128)(2,1)S(1)}, bf16[4,2,256,768]{3,2,1,0:T(8,128)(2,1)S(1)}) custom-call(s32[1]{0:T(128)} %bitcast.own_ref, bf16[1,256,768]{2,1,0:T(8,128)(2,1)S(1)} %get-tuple-element.182.refs_0_.x0_ref, bf16[1,256,768]{2,1,0:T(8,128)(2,1)} %collective-permute-done.10.refs_1_.x1_ref, ...), custom_call_target="tpu_custom_call" | custom-call | flops 550000000 | tf_op jit(solution)/shard_map/prepare/pallas_call | solution.py:729
  55.3 1.5 collective-permute-start.17
  56.8 7.9 %attend.2 = (bf16[2,2,256,256]{3,2,1,0:T(8,128)(2,1)S(1)}, bf16[2,2,3,256,128]{4,3,2,1,0:T(8,128)(2,1)S(1)}) custom-call(s32[1]{0:T(128)} %bitcast.own_ref, bf16[2,2,256,256]{3,2,1,0:T(8,128)(2,1)S(1)} %bitcast.162, bf16[4,256,128]{2,1,0:T(8,128)(2,1)S(1)} %get-tuple-element.278.refs_0_, bf16[4,256,128]{2,1,0:T(8,128)(2,1)S(1)} %collective-permute-done.16.refs_1_), custom_call_target="tpu_custom_call" | custom-call | flops 16499999744 | tf_op jit(solution)/shard_map/attend/pallas_call | solution.py:729
  65.5 0.7 collective-permute-start.24
  66.3 3.2 %collective-permute-start.23 = (bf16[1,5,96,768]{3,2,1,0:T(8,128)(2,1)S(1)}, bf16[1,5,96,768]{3,2,1,0:T(8,128)(2,1)S(1)}, u32[]{:S(2)}, u32[]{:S(2)}) collective-permute-start(bf16[1,5,96,768]{3,2,1,0:T(8,128)(2,1)S(1)} %bitcast.159), channel_id=1, source_target_pairs={{0,8},{4,12},{8,0},{12,4},{16,24},{20,28},{24,16},{28,20},{1,9},{5... | collective-permute-start | bytes 2211848 | tf_op jit(solution)/shard_map/swap_more_x1/ppermute | solution.py:553
  69.5 7.9 %attend.3 = (bf16[2,2,256,256]{3,2,1,0:T(8,128)(2,1)S(1)}, bf16[2,2,3,256,128]{4,3,2,1,0:T(8,128)(2,1)S(1)}) custom-call(s32[1]{0:T(128)} %bitcast.own_ref, bf16[2,2,256,256]{3,2,1,0:T(8,128)(2,1)S(1)} %bitcast.163, bf16[4,256,128]{2,1,0:T(8,128)(2,1)S(1)} %get-tuple-element.279.refs_0_, bf16[4,256,128]{2,1,0:T(8,128)(2,1)S(1)} %collective-permute-done.17.refs_1_), custom_call_target="tpu_custom_call" | custom-call | flops 16499999744 | tf_op jit(solution)/shard_map/attend/pallas_call | solution.py:729
  77.6 1.8 collective-permute-done.24
  79.4 5.1 %collective-permute-done.23.refs_8_ = bf16[1,5,96,768]{3,2,1,0:T(8,128)(2,1)S(1)} collective-permute-done((bf16[1,5,96,768]{3,2,1,0:T(8,128)(2,1)S(1)}, bf16[1,5,96,768]{3,2,1,0:T(8,128)(2,1)S(1)}, u32[]{:S(2)}, u32[]{:S(2)}) %collective-permute-start.23) | collective-permute-done | bytes 737312 | tf_op jit(solution)/shard_map/swap_more_x1/ppermute | solution.py:553
  84.5 25.4 %hidden.1 = (bf16[2,2,256,768]{3,2,1,0:T(8,128)(2,1)S(1)}, bf16[2,2,256,768]{3,2,1,0:T(8,128)(2,1)S(1)}, bf16[4,2,256,768]{3,2,1,0:T(8,128)(2,1)S(1)}, bf16[4,2,...) custom-call(s32[2]{0:T(128)S(1)} %pad_add_fusion.own_ref, ...), custom_call_target="tpu_custom_call" | custom-call | flops 29699999744 | tf_op jit(solution)/shard_map/hidden/pallas_call | solution.py:729
  110.0 1.8 collective-permute-start.26
  111.8 1.6 collective-permute-start.27
  113.4 11.0 %attend_back.2 = (bf16[2,2,256,256]{3,2,1,0:T(8,128)(2,1)S(1)}, f32[4,256,128]{2,1,0:T(8,128)S(1)}, bf16[4,256,128]{2,1,0:T(8,128)(2,1)S(1)}) custom-call(s32[1]{0:T(128)} %bitcast.own_ref, bf16[2,2,3,256,128]{4,3,2,1,0:T(8,128)(2,1)S(1)} %get-tuple-element.219.query_ref, bf16[2,2,2,3,256,128]{5,4,3,2,1,0:T(8,128)(2,1)S(1)} %bitcast.164, ...), custom_call_target="tpu_custom_call" | custom-call | flops 22000001024 | tf_op jit(solution)/shard_map/attend_back/pallas_call | solution.py:729
  124.4 2.8 %collective-permute-done.27 = bf16[2,2,96,768]{3,2,1,0:T(8,128)(2,1)S(1)} collective-permute-done((bf16[2,2,96,768]{3,2,1,0:T(8,128)(2,1)S(1)}, bf16[2,2,96,768]{3,2,1,0:T(8,128)(2,1)S(1)}, u32[]{:S(2)}, u32[]{:S(2)}) %collective-permute-start.27) | collective-permute-done | bytes 589856 | tf_op jit(solution)/shard_map/swap_gdown_z1/ppermute | solution.py:557
  127.2 1.7 collective-permute-done.26
  129.2 1.6 collective-permute-start.29
  131.2 0.8 collective-permute-start.28
  132.0 1.8 collective-permute-start.30
  134.0 0.7 collective-permute-start.31
  134.7 11.0 %attend_back.3 = (bf16[2,2,256,256]{3,2,1,0:T(8,128)(2,1)S(1)}, f32[4,256,128]{2,1,0:T(8,128)S(1)}, bf16[4,256,128]{2,1,0:T(8,128)(2,1)S(1)}) custom-call(s32[1]{0:T(128)} %bitcast.own_ref, bf16[2,2,3,256,128]{4,3,2,1,0:T(8,128)(2,1)S(1)} %get-tuple-element.231.query_ref, bf16[2,2,2,3,256,128]{5,4,3,2,1,0:T(8,128)(2,1)S(1)} %bitcast.165, ...), custom_call_target="tpu_custom_call" | custom-call | flops 22000001024 | tf_op jit(solution)/shard_map/attend_back/pallas_call | solution.py:729
  145.8 4.3 %collective-permute-done.28 = bf16[2,256,768]{2,1,0:T(8,128)(2,1)S(1)} collective-permute-done((bf16[2,256,768]{2,1,0:T(8,128)(2,1)S(1)}, bf16[2,256,768]{2,1,0:T(8,128)(2,1)S(1)}, u32[]{:S(2)}, u32[]{:S(2)}) %collective-permute-start.28) | collective-permute-done | bytes 786464 | tf_op jit(solution)/shard_map/swap_made_y/ppermute | solution.py:553
  150.8 2.0 %collective-permute-start.33 = (bf16[4,256,128]{2,1,0:T(8,128)(2,1)S(1)}, bf16[4,256,128]{2,1,0:T(8,128)(2,1)S(1)}, u32[]{:S(2)}, u32[]{:S(2)}) collective-permute-start(bf16[4,256,128]{2,1,0:T(8,128)(2,1)S(1)} %get-tuple-element.253), channel_id=1, source_target_pairs={{0,8},{4,12},{8,0},{12,4},{16,24},{20,28},{24,16},{28,20},{1,9},{5... | collective-permute-start | bytes 786440 | tf_op jit(solution)/shard_map/swap_gkeyval1_x1/ppermute | solution.py:553
  152.9 7.1 %pull_tokens.2 = (bf16[2,256,768]{2,1,0:T(8,128)(2,1)S(1)}, bf16[2,256,768]{2,1,0:T(8,128)(2,1)S(1)}, f32[768,384]{1,0:T(8,128)S(1)}, f32[8,768]{1,0:T(8,128)S(1)}) custom-call(s32[1]{0:T(128)} %bitcast.own_ref, bf16[1,256,768]{2,1,0:T(8,128)(2,1)S(1)} %get-tuple-element.173.refs_0_.refs_4_.x0_ref, ...), custom_call_target="tpu_custom_call" | custom-call | flops 7699999744 | tf_op jit(solution)/shard_map/pull_tokens/pallas_call | solution.py:729
  160.2 1.7 collective-permute-start.38
  162.6 7.2 %pull_tokens.3 = (bf16[2,256,768]{2,1,0:T(8,128)(2,1)S(1)}, bf16[2,256,768]{2,1,0:T(8,128)(2,1)S(1)}, f32[1,4,96,384]{3,2,1,0:T(8,128)S(1)}, bf16[1,4,96,384]{3,2,1,0:T(8,128)(2,1)S(1)}) custom-call(s32[1]{0:T(128)} %bitcast.own_ref, bf16[1,256,768]{2,1,0:T(8,128)(2,1)S(1)} %get-tuple-element.182.refs_0_.x0_ref, ...), custom_call_target="tpu_custom_call" | custom-call | flops 7699999744 | tf_op jit(solution)/shard_map/pull_tokens/pallas_call | solution.py:729
  170.4 1.3 collective-permute-start.42
  171.9 0.8 collective-permute-start.43
  172.8 0.7 fusion.8
  173.6 1.2 fusion.1
  174.7 4.2 %collective-permute-done.36 = bf16[1,4,96,384]{3,2,1,0:T(8,128)(2,1)S(1)} collective-permute-done((bf16[1,4,96,384]{3,2,1,0:T(8,128)(2,1)S(1)}, bf16[1,4,96,384]{3,2,1,0:T(8,128)(2,1)S(1)}, u32[]{:S(2)}, u32[]{:S(2)}) %collective-permute-start.36) | collective-permute-done | bytes 294944 | tf_op jit(solution)/shard_map/swap_gfront_x1/ppermute | solution.py:553
  179.1 1.0 collective-permute-start.44
  180.9 1.8 collective-permute-start.40
  182.8 2.5 %collective-permute-start.41 = (bf16[4,24,384]{2,1,0:T(8,128)(2,1)S(1)}, bf16[4,24,384]{2,1,0:T(8,128)(2,1)S(1)}, u32[]{:S(2)}, u32[]{:S(2)}) collective-permute-start(bf16[4,24,384]{2,1,0:T(8,128)(2,1)S(1)} %get-tuple-element.312), channel_id=1, source_target_pairs={{0,3},{1,2},{2,1},{3,0},{4,7},{5,6},{6,5},{7,4},{8,11},{9,10},{10,... | collective-permute-start | bytes 221192 | tf_op jit(solution)/shard_map/swap_gfront_z3/ppermute | solution.py:557
  186.3 3.8 %collective-permute-done.41 = bf16[4,24,384]{2,1,0:T(8,128)(2,1)S(1)} collective-permute-done((bf16[4,24,384]{2,1,0:T(8,128)(2,1)S(1)}, bf16[4,24,384]{2,1,0:T(8,128)(2,1)S(1)}, u32[]{:S(2)}, u32[]{:S(2)}) %collective-permute-start.41) | collective-permute-done | bytes 73760 | tf_op jit(solution)/shard_map/swap_gfront_z3/ppermute | solution.py:557
  190.1 1.9 collective-permute-done.44
  192.3 1.3 collective-permute-start.46
  194.3 1.3 maximum_add_fusion
  197.4 1.7 finish.1
  (146 shorter events, 12.5 us)
Async XLA Ops:
  0.6 7.1 %copy-start.5 = (bf16[2,256,768]{2,1,0:T(8,128)(2,1)S(1)}, bf16[2,256,768]{2,1,0:T(8,128)(2,1)}, u32[]{:S(2)}) copy-start(bf16[2,256,768]{2,1,0:T(8,128)(2,1)} %param.12) | copy-start | bytes 2359300
  4.5 3.3 %collective-permute-start = (bf16[24,1152]{1,0:T(8,128)(2,1)S(1)}, bf16[24,1152]{1,0:T(8,128)(2,1)S(1)}, u32[]{:S(2)}, u32[]{:S(2)}) collective-permute-start(bf16[24,1152]{1,0:T(8,128)(2,1)S(1)} %get-tuple-element.331), channel_id=1, source_target_pairs={{0,4},{4,0},{8,12},{12,8},{16,20},{20,16},{24,28},{28,24},{1,5},{5... | collective-permute-start | bytes 165896 | tf_op jit(solution)/shard_map/swap_pack_1/ppermute | solution.py:553
  5.1 5.1 %collective-permute-start.1 = (bf16[24,1152]{1,0:T(8,128)(2,1)S(1)}, bf16[24,1152]{1,0:T(8,128)(2,1)S(1)}, u32[]{:S(2)}, u32[]{:S(2)}) collective-permute-start(bf16[24,1152]{1,0:T(8,128)(2,1)S(1)} %get-tuple-element.330), channel_id=1, source_target_pairs={{0,16},{4,20},{8,24},{12,28},{16,0},{20,4},{24,8},{28,12},{1,17},{... | collective-permute-start | bytes 165896 | tf_op jit(solution)/shard_map/swap_pack_2/ppermute | solution.py:553
  7.7 3.8 %collective-permute-start.2 = (bf16[24,1152]{1,0:T(8,128)(2,1)S(1)}, bf16[24,1152]{1,0:T(8,128)(2,1)S(1)}, u32[]{:S(2)}, u32[]{:S(2)}) collective-permute-start(bf16[24,1152]{1,0:T(8,128)(2,1)S(1)} %get-tuple-element.329), channel_id=1, source_target_pairs={{0,20},{4,16},{8,28},{12,24},{16,4},{20,0},{24,12},{28,8},{1,21},{... | collective-permute-start | bytes 165896 | tf_op jit(solution)/shard_map/swap_pack_3/ppermute | solution.py:553
  11.5 11.8 %collective-permute-start.6 = (bf16[1,256,768]{2,1,0:T(8,128)(2,1)S(1)}, bf16[1,256,768]{2,1,0:T(8,128)(2,1)S(1)}, u32[]{:S(2)}, u32[]{:S(2)}) collective-permute-start(bf16[1,256,768]{2,1,0:T(8,128)(2,1)S(1)} %get-tuple-element.173.refs_0_.refs_4_.x0_ref), channel_id=1, source_target_pairs={{0,16},{4,20},{8,24},{12,28},{16,0},{20,4},{24,8},{28,12},{1,17},{... | collective-permute-start | bytes 1179656 | tf_op jit(solution)/shard_map/swap_tokens0_y/ppermute | solution.py:553
  12.7 20.0 %copy-start.1 = (bf16[2,256,768]{2,1,0:T(8,128)(2,1)S(1)}, bf16[2,256,768]{2,1,0:T(8,128)(2,1)}, u32[]{:S(2)}) copy-start(bf16[2,256,768]{2,1,0:T(8,128)(2,1)} %refs_0_) | copy-start | bytes 2359300
  12.7 23.4 %copy-start = (f32[2,256,128]{2,1,0:T(8,128)S(1)}, f32[2,256,128]{2,1,0:T(8,128)}, u32[]{:S(2)}) copy-start(f32[2,256,128]{2,1,0:T(8,128)} %constant.338.clone.refs_6_.refs_10_.place_ref) | copy-start | bytes 786436
  12.7 23.4 %copy-start.2 = (f32[2,8,128]{2,1,0:T(8,128)S(1)}, f32[2,8,128]{2,1,0:T(8,128)}, u32[]{:S(2)}) copy-start(f32[2,8,128]{2,1,0:T(8,128)} %constant.339.clone.refs_7_.refs_11_.start_ref) | copy-start | bytes 24580
  12.7 5.9 %collective-permute-start.3 = (bf16[4,24,384]{2,1,0:T(8,128)(2,1)S(1)}, bf16[4,24,384]{2,1,0:T(8,128)(2,1)S(1)}, u32[]{:S(2)}, u32[]{:S(2)}) collective-permute-start(bf16[4,24,384]{2,1,0:T(8,128)(2,1)S(1)} %bitcast.185), channel_id=1, source_target_pairs={{0,1},{1,0},{2,3},{3,2},{4,5},{5,4},{6,7},{7,6},{8,9},{9,8},{10,11... | collective-permute-start | bytes 221192 | tf_op jit(solution)/shard_map/swap_front_z1/ppermute | solution.py:557
  14.4 8.0 %collective-permute-start.4 = (bf16[4,24,384]{2,1,0:T(8,128)(2,1)S(1)}, bf16[4,24,384]{2,1,0:T(8,128)(2,1)S(1)}, u32[]{:S(2)}, u32[]{:S(2)}) collective-permute-start(bf16[4,24,384]{2,1,0:T(8,128)(2,1)S(1)} %bitcast.186), channel_id=1, source_target_pairs={{0,2},{1,3},{2,0},{3,1},{4,6},{5,7},{6,4},{7,5},{8,10},{9,11},{10,... | collective-permute-start | bytes 221192 | tf_op jit(solution)/shard_map/swap_front_z2/ppermute | solution.py:557
  17.0 6.3 %collective-permute-start.5 = (bf16[4,24,384]{2,1,0:T(8,128)(2,1)S(1)}, bf16[4,24,384]{2,1,0:T(8,128)(2,1)S(1)}, u32[]{:S(2)}, u32[]{:S(2)}) collective-permute-start(bf16[4,24,384]{2,1,0:T(8,128)(2,1)S(1)} %bitcast.187), channel_id=1, source_target_pairs={{0,3},{1,2},{2,1},{3,0},{4,7},{5,6},{6,5},{7,4},{8,11},{9,10},{10,... | collective-permute-start | bytes 221192 | tf_op jit(solution)/shard_map/swap_front_z3/ppermute | solution.py:557
  17.2 11.6 %collective-permute-start.13 = (bf16[1,1,96,768]{3,2,0,1:T(8,128)(2,1)}, bf16[1,1,96,768]{3,2,0,1:T(8,128)(2,1)}, u32[]{:S(2)}, u32[]{:S(2)}) collective-permute-start(bf16[1,1,96,768]{3,2,0,1:T(8,128)(2,1)} %bitcast.24), channel_id=1, source_target_pairs={{0,8},{4,12},{8,0},{12,4},{16,24},{20,28},{24,16},{28,20},{1,9},{5... | collective-permute-start | bytes 442376 | tf_op jit(solution)/shard_map/swap_down_x1/ppermute | solution.py:553
  18.7 14.0 %collective-permute-start.8 = (bf16[1,256,768]{2,1,0:T(8,128)(2,1)S(1)}, bf16[1,256,768]{2,1,0:T(8,128)(2,1)S(1)}, u32[]{:S(2)}, u32[]{:S(2)}) collective-permute-start(bf16[1,256,768]{2,1,0:T(8,128)(2,1)S(1)} %get-tuple-element.173.refs_0_.refs_4_.x0_ref), channel_id=1, source_target_pairs={{0,4},{4,0},{8,12},{12,8},{16,20},{20,16},{24,28},{28,24},{1,5},{5... | collective-permute-start | bytes 1179656 | tf_op jit(solution)/shard_map/swap_tokens0_c/ppermute | solution.py:553
  23.3 3.8 %collective-permute-start.11 = (bf16[24,768]{1,0:T(8,128)(2,1)}, bf16[24,768]{1,0:T(8,128)(2,1)S(1)}, u32[]{:S(2)}, u32[]{:S(2)}) collective-permute-start(bf16[24,768]{1,0:T(8,128)(2,1)} %param.15), channel_id=1, source_target_pairs={{0,0},{1,1},{2,2},{3,3},{8,4},{9,5},{10,6},{11,7},{4,8},{5,9},{6,1... | collective-permute-start | bytes 110600 | tf_op jit(solution)/shard_map/swap_out_moved/ppermute | solution.py:703
  24.8 11.4 %collective-permute-start.9 = (bf16[1,256,768]{2,1,0:T(8,128)(2,1)S(1)}, bf16[1,256,768]{2,1,0:T(8,128)(2,1)S(1)}, u32[]{:S(2)}, u32[]{:S(2)}) collective-permute-start(bf16[1,256,768]{2,1,0:T(8,128)(2,1)S(1)} %collective-permute-done.6.refs_1_.refs_5_.x1_ref), channel_id=1, source_target_pairs={{0,4},{4,0},{8,12},{12,8},{16,20},{20,16},{24,28},{28,24},{1,5},{5... | collective-permute-start | bytes 1179656 | tf_op jit(solution)/shard_map/swap_tokens0_yc/ppermute | solution.py:553
  27.0 9.1 %collective-permute-start.7 = (bf16[1,4,96,384]{3,2,1,0:T(8,128)(2,1)S(1)}, bf16[1,4,96,384]{3,2,1,0:T(8,128)(2,1)}, u32[]{:S(2)}, u32[]{:S(2)}) collective-permute-start(bf16[1,4,96,384]{3,2,1,0:T(8,128)(2,1)S(1)} %bitcast.157), channel_id=1, source_target_pairs={{0,8},{4,12},{8,0},{12,4},{16,24},{20,28},{24,16},{28,20},{1,9},{5... | collective-permute-start | bytes 884744 | tf_op jit(solution)/shard_map/swap_front_x1/ppermute | solution.py:553
  27.1 14.3 %collective-permute-start.10 = (bf16[1,256,768]{2,1,0:T(8,128)(2,1)S(1)}, bf16[1,256,768]{2,1,0:T(8,128)(2,1)}, u32[]{:S(2)}, u32[]{:S(2)}) collective-permute-start(bf16[1,256,768]{2,1,0:T(8,128)(2,1)S(1)} %get-tuple-element.182.refs_0_.x0_ref), channel_id=1, source_target_pairs={{0,16},{4,20},{8,24},{12,28},{16,0},{20,4},{24,8},{28,12},{1,17},{... | collective-permute-start | bytes 1179656 | tf_op jit(solution)/shard_map/swap_tokens1_y/ppermute | solution.py:553
  28.8 12.6 %collective-permute-start.12 = (bf16[5,1,24,768]{3,2,1,0:T(8,128)(2,1)}, bf16[5,1,24,768]{3,2,1,0:T(8,128)(2,1)}, u32[]{:S(2)}, u32[]{:S(2)}) collective-permute-start(bf16[5,1,24,768]{3,2,1,0:T(8,128)(2,1)} %get-tuple-element.333), channel_id=1, source_target_pairs={{0,2},{1,3},{2,0},{3,1},{4,6},{5,7},{6,4},{7,5},{8,10},{9,11},{10,... | collective-permute-start | bytes 552968 | tf_op jit(solution)/shard_map/swap_more_z2/ppermute | solution.py:557
  32.7 44.9 %collective-permute-start.21 = (bf16[2,256,768]{2,1,0:T(8,128)(2,1)S(1)}, bf16[2,256,768]{2,1,0:T(8,128)(2,1)S(1)}, u32[]{:S(2)}, u32[]{:S(2)}) collective-permute-start(bf16[2,256,768]{2,1,0:T(8,128)(2,1)S(1)} %copy-done.1), channel_id=1, source_target_pairs={{0,4},{4,0},{8,12},{12,8},{16,20},{20,16},{24,28},{28,24},{1,5},{5... | collective-permute-start | bytes 2359304 | tf_op jit(solution)/shard_map/swap_grads_c/ppermute | solution.py:553
  36.1 10.3 %collective-permute-start.14 = (bf16[1,256,768]{2,1,0:T(8,128)(2,1)S(1)}, bf16[1,256,768]{2,1,0:T(8,128)(2,1)S(1)}, u32[]{:S(2)}, u32[]{:S(2)}) collective-permute-start(bf16[1,256,768]{2,1,0:T(8,128)(2,1)S(1)} %get-tuple-element.182.refs_0_.x0_ref), channel_id=1, source_target_pairs={{0,4},{4,0},{8,12},{12,8},{16,20},{20,16},{24,28},{28,24},{1,5},{5... | collective-permute-start | bytes 1179656 | tf_op jit(solution)/shard_map/swap_tokens1_c/ppermute | solution.py:553
  41.4 6.0 %collective-permute-start.15 = (bf16[1,256,768]{2,1,0:T(8,128)(2,1)}, bf16[1,256,768]{2,1,0:T(8,128)(2,1)S(1)}, u32[]{:S(2)}, u32[]{:S(2)}) collective-permute-start(bf16[1,256,768]{2,1,0:T(8,128)(2,1)} %collective-permute-done.10.refs_1_.x1_ref), channel_id=1, source_target_pairs={{0,4},{4,0},{8,12},{12,8},{16,20},{20,16},{24,28},{28,24},{1,5},{5... | collective-permute-start | bytes 1179656 | tf_op jit(solution)/shard_map/swap_tokens1_yc/ppermute | solution.py:553
  43.2 22.2 %collective-permute-start.20 = (bf16[5,2,24,768]{3,2,1,0:T(8,128)(2,1)S(1)}, bf16[5,2,24,768]{3,2,1,0:T(8,128)(2,1)S(1)}, u32[]{:S(2)}, u32[]{:S(2)}) collective-permute-start(bf16[5,2,24,768]{3,2,1,0:T(8,128)(2,1)S(1)} %maximum_select_fusion.3), channel_id=1, source_target_pairs={{0,1},{1,0},{2,3},{3,2},{4,5},{5,4},{6,7},{7,6},{8,9},{9,8},{10,11... | collective-permute-start | bytes 1105928 | tf_op jit(solution)/shard_map/swap_more_z1/ppermute | solution.py:557
  44.6 10.7 %collective-permute-start.16 = (bf16[4,256,128]{2,1,0:T(8,128)(2,1)S(1)}, bf16[4,256,128]{2,1,0:T(8,128)(2,1)S(1)}, u32[]{:S(2)}, u32[]{:S(2)}) collective-permute-start(bf16[4,256,128]{2,1,0:T(8,128)(2,1)S(1)} %get-tuple-element.278.refs_0_), channel_id=1, source_target_pairs={{0,8},{4,12},{8,0},{12,4},{16,24},{20,28},{24,16},{28,20},{1,9},{5... | collective-permute-start | bytes 786440 | tf_op jit(solution)/shard_map/swap_keyval0_x1/ppermute | solution.py:553
  46.4 19.1 %collective-permute-start.18 = (bf16[2,256,768]{2,1,0:T(8,128)(2,1)S(1)}, bf16[2,256,768]{2,1,0:T(8,128)(2,1)S(1)}, u32[]{:S(2)}, u32[]{:S(2)}) collective-permute-start(bf16[2,256,768]{2,1,0:T(8,128)(2,1)S(1)} %copy-done.1), channel_id=1, source_target_pairs={{0,16},{4,20},{8,24},{12,28},{16,0},{20,4},{24,8},{28,12},{1,17},{... | collective-permute-start | bytes 2359304 | tf_op jit(solution)/shard_map/swap_grads_y/ppermute | solution.py:553
  47.4 18.0 %collective-permute-start.19 = (bf16[2,1,1,96,768]{4,3,1,0,2:T(8,128)(2,1)S(1)}, bf16[2,1,1,96,768]{4,3,1,0,2:T(8,128)(2,1)S(1)}, u32[]{:S(2)}, u32[]{:S(2)}) collective-permute-start(bf16[2,1,1,96,768]{4,3,1,0,2:T(8,128)(2,1)S(1)} %bitcast.172), channel_id=1, source_target_pairs={{0,2},{1,3},{2,0},{3,1},{4,6},{5,7},{6,4},{7,5},{8,10},{9,11},{10,... | collective-permute-start | bytes 884744 | tf_op jit(solution)/shard_map/swap_down_z2/ppermute | solution.py:557
  55.3 9.4 %copy-start.3 = (bf16[4,2,256,768]{3,2,1,0:T(8,128)(2,1)}, bf16[4,2,256,768]{3,2,1,0:T(8,128)(2,1)S(1)}, u32[]{:S(2)}) copy-start(bf16[4,2,256,768]{3,2,1,0:T(8,128)(2,1)S(1)} %get-tuple-element.212.refs_4_) | copy-start | bytes 9437188
  55.3 10.1 %collective-permute-start.17 = (bf16[4,256,128]{2,1,0:T(8,128)(2,1)S(1)}, bf16[4,256,128]{2,1,0:T(8,128)(2,1)S(1)}, u32[]{:S(2)}, u32[]{:S(2)}) collective-permute-start(bf16[4,256,128]{2,1,0:T(8,128)(2,1)S(1)} %get-tuple-element.279.refs_0_), channel_id=1, source_target_pairs={{0,8},{4,12},{8,0},{12,4},{16,24},{20,28},{24,16},{28,20},{1,9},{5... | collective-permute-start | bytes 786440 | tf_op jit(solution)/shard_map/swap_keyval1_x1/ppermute | solution.py:553
  65.5 13.9 %collective-permute-start.24 = (bf16[2,2,1,96,768]{4,3,1,0,2:T(8,128)(2,1)S(1)}, bf16[2,2,1,96,768]{4,3,1,0,2:T(8,128)(2,1)S(1)}, u32[]{:S(2)}, u32[]{:S(2)}) collective-permute-start(bf16[2,2,1,96,768]{4,3,1,0,2:T(8,128)(2,1)S(1)} %maximum_select_fusion.1), channel_id=1, source_target_pairs={{0,1},{1,0},{2,3},{3,2},{4,5},{5,4},{6,7},{7,6},{8,9},{9,8},{10,11... | collective-permute-start | bytes 1769480 | tf_op jit(solution)/shard_map/swap_down_z1/ppermute | solution.py:557
  66.3 18.2 %collective-permute-start.23 = (bf16[1,5,96,768]{3,2,1,0:T(8,128)(2,1)S(1)}, bf16[1,5,96,768]{3,2,1,0:T(8,128)(2,1)S(1)}, u32[]{:S(2)}, u32[]{:S(2)}) collective-permute-start(bf16[1,5,96,768]{3,2,1,0:T(8,128)(2,1)S(1)} %bitcast.159), channel_id=1, source_target_pairs={{0,8},{4,12},{8,0},{12,4},{16,24},{20,28},{24,16},{28,20},{1,9},{5... | collective-permute-start | bytes 2211848 | tf_op jit(solution)/shard_map/swap_more_x1/ppermute | solution.py:553
  69.5 15.0 %collective-permute-start.22 = (bf16[2,256,768]{2,1,0:T(8,128)(2,1)S(1)}, bf16[2,256,768]{2,1,0:T(8,128)(2,1)S(1)}, u32[]{:S(2)}, u32[]{:S(2)}) collective-permute-start(bf16[2,256,768]{2,1,0:T(8,128)(2,1)S(1)} %collective-permute-done.18.refs_1_), channel_id=1, source_target_pairs={{0,4},{4,0},{8,12},{12,8},{16,20},{20,16},{24,28},{28,24},{1,5},{5... | collective-permute-start | bytes 2359304 | tf_op jit(solution)/shard_map/swap_grads_yc/ppermute | solution.py:553
  110.0 19.0 %collective-permute-start.25 = (bf16[2,2,256,768]{3,2,1,0:T(8,128)(2,1)S(1)}, bf16[2,2,256,768]{3,2,1,0:T(8,128)(2,1)S(1)}, u32[]{:S(2)}, u32[]{:S(2)}) collective-permute-start(bf16[2,2,256,768]{3,2,1,0:T(8,128)(2,1)S(1)} %get-tuple-element.225), channel_id=1, source_target_pairs={{0,4},{4,0},{8,12},{12,8},{16,20},{20,16},{24,28},{28,24},{1,5},{5... | collective-permute-start | bytes 4718600 | tf_op jit(solution)/shard_map/swap_made_c/ppermute | solution.py:553
  110.0 18.9 %collective-permute-start.26 = (bf16[1,5,96,768]{3,2,1,0:T(8,128)(2,1)S(1)}, bf16[1,5,96,768]{3,2,1,0:T(8,128)(2,1)S(1)}, u32[]{:S(2)}, u32[]{:S(2)}) collective-permute-start(bf16[1,5,96,768]{3,2,1,0:T(8,128)(2,1)S(1)} %get-tuple-element.227), channel_id=1, source_target_pairs={{0,8},{4,12},{8,0},{12,4},{16,24},{20,28},{24,16},{28,20},{1,9},{5... | collective-permute-start | bytes 2211848 | tf_op jit(solution)/shard_map/swap_gmore_x1/ppermute | solution.py:553
  111.8 15.4 %collective-permute-start.27 = (bf16[2,2,96,768]{3,2,1,0:T(8,128)(2,1)S(1)}, bf16[2,2,96,768]{3,2,1,0:T(8,128)(2,1)S(1)}, u32[]{:S(2)}, u32[]{:S(2)}) collective-permute-start(bf16[2,2,96,768]{3,2,1,0:T(8,128)(2,1)S(1)} %get-tuple-element.229), channel_id=1, source_target_pairs={{0,1},{1,0},{2,3},{3,2},{4,5},{5,4},{6,7},{7,6},{8,9},{9,8},{10,11... | collective-permute-start | bytes 1769480 | tf_op jit(solution)/shard_map/swap_gdown_z1/ppermute | solution.py:557
  129.2 16.6 %collective-permute-start.29 = (bf16[5,2,24,768]{3,2,0,1:T(8,128)(2,1)S(1)}, bf16[5,2,24,768]{3,2,0,1:T(8,128)(2,1)S(1)}, u32[]{:S(2)}, u32[]{:S(2)}) collective-permute-start(bf16[5,2,24,768]{3,2,0,1:T(8,128)(2,1)S(1)} %fusion.7), channel_id=1, source_target_pairs={{0,1},{1,0},{2,3},{3,2},{4,5},{5,4},{6,7},{7,6},{8,9},{9,8},{10,11... | collective-permute-start | bytes 1105928 | tf_op jit(solution)/shard_map/swap_gmore_z1/ppermute | solution.py:557
  131.2 18.9 %collective-permute-start.28 = (bf16[2,256,768]{2,1,0:T(8,128)(2,1)S(1)}, bf16[2,256,768]{2,1,0:T(8,128)(2,1)S(1)}, u32[]{:S(2)}, u32[]{:S(2)}) collective-permute-start(bf16[2,256,768]{2,1,0:T(8,128)(2,1)S(1)} %fusion.2), channel_id=1, source_target_pairs={{0,16},{4,20},{8,24},{12,28},{16,0},{20,4},{24,8},{28,12},{1,17},{... | collective-permute-start | bytes 2359304 | tf_op jit(solution)/shard_map/swap_made_y/ppermute | solution.py:553
  132.0 13.7 %collective-permute-start.30 = (bf16[4,256,128]{2,1,0:T(8,128)(2,1)S(1)}, bf16[4,256,128]{2,1,0:T(8,128)(2,1)S(1)}, u32[]{:S(2)}, u32[]{:S(2)}) collective-permute-start(bf16[4,256,128]{2,1,0:T(8,128)(2,1)S(1)} %get-tuple-element.236), channel_id=1, source_target_pairs={{0,8},{4,12},{8,0},{12,4},{16,24},{20,28},{24,16},{28,20},{1,9},{5... | collective-permute-start | bytes 786440 | tf_op jit(solution)/shard_map/swap_gkeyval0_x1/ppermute | solution.py:553
  134.0 26.1 %collective-permute-start.31 = (bf16[2,1,96,768]{3,2,1,0:T(8,128)(2,1)S(1)}, bf16[2,1,96,768]{3,2,1,0:T(8,128)(2,1)S(1)}, u32[]{:S(2)}, u32[]{:S(2)}) collective-permute-start(bf16[2,1,96,768]{3,2,1,0:T(8,128)(2,1)S(1)} %dynamic-slice_convert_fusion), channel_id=1, source_target_pairs={{0,2},{1,3},{2,0},{3,1},{4,6},{5,7},{6,4},{7,5},{8,10},{9,11},{10,... | collective-permute-start | bytes 884744 | tf_op jit(solution)/shard_map/swap_gdown_z2/ppermute | solution.py:557
  150.1 2.8 %copy-start.4 = (bf16[2,256,128]{2,1,0:T(8,128)(2,1)S(1)}, bf16[2,256,128]{2,1,0:T(8,128)(2,1)}, u32[]{:S(2)}) copy-start(bf16[2,256,128]{2,1,0:T(8,128)(2,1)} %cotangent_ref.3) | copy-start | bytes 393220
  150.2 9.9 %collective-permute-start.32 = (bf16[5,1,24,768]{3,2,0,1:T(8,128)(2,1)S(1)}, bf16[5,1,24,768]{3,2,0,1:T(8,128)(2,1)S(1)}, u32[]{:S(2)}, u32[]{:S(2)}) collective-permute-start(bf16[5,1,24,768]{3,2,0,1:T(8,128)(2,1)S(1)} %dynamic-slice_convert_fusion.1), channel_id=1, source_target_pairs={{0,2},{1,3},{2,0},{3,1},{4,6},{5,7},{6,4},{7,5},{8,10},{9,11},{10,... | collective-permute-start | bytes 552968 | tf_op jit(solution)/shard_map/swap_gmore_z2/ppermute | solution.py:557
  150.8 9.3 %collective-permute-start.33 = (bf16[4,256,128]{2,1,0:T(8,128)(2,1)S(1)}, bf16[4,256,128]{2,1,0:T(8,128)(2,1)S(1)}, u32[]{:S(2)}, u32[]{:S(2)}) collective-permute-start(bf16[4,256,128]{2,1,0:T(8,128)(2,1)S(1)} %get-tuple-element.253), channel_id=1, source_target_pairs={{0,8},{4,12},{8,0},{12,4},{16,24},{20,28},{24,16},{28,20},{1,9},{5... | collective-permute-start | bytes 786440 | tf_op jit(solution)/shard_map/swap_gkeyval1_x1/ppermute | solution.py:553
  160.2 10.1 %collective-permute-start.38 = (bf16[1,96,768]{2,1,0:T(8,128)(2,1)S(1)}, bf16[1,96,768]{2,1,0:T(8,128)(2,1)S(1)}, u32[]{:S(2)}, u32[]{:S(2)}) collective-permute-start(bf16[1,96,768]{2,1,0:T(8,128)(2,1)S(1)} %fusion.9), channel_id=1, source_target_pairs={{0,8},{4,12},{8,0},{12,4},{16,24},{20,28},{24,16},{28,20},{1,9},{5... | collective-permute-start | bytes 442376 | tf_op jit(solution)/shard_map/swap_gdown_x1/ppermute | solution.py:553
  162.0 7.8 %collective-permute-start.35 = (bf16[2,24,768]{2,1,0:T(8,128)(2,1)S(1)}, bf16[2,24,768]{2,1,0:T(8,128)(2,1)S(1)}, u32[]{:S(2)}, u32[]{:S(2)}) collective-permute-start(bf16[2,24,768]{2,1,0:T(8,128)(2,1)S(1)} %fusion.14), channel_id=1, source_target_pairs={{0,4},{4,0},{8,12},{12,8},{16,20},{20,16},{24,28},{28,24},{1,5},{5... | collective-permute-start | bytes 221192 | tf_op jit(solution)/shard_map/swap_gup_c/ppermute | solution.py:553
  162.1 7.7 %collective-permute-start.34 = (bf16[2,256,768]{2,1,0:T(8,128)(2,1)S(1)}, bf16[2,256,768]{2,1,0:T(8,128)(2,1)S(1)}, u32[]{:S(2)}, u32[]{:S(2)}) collective-permute-start(bf16[2,256,768]{2,1,0:T(8,128)(2,1)S(1)} %get-tuple-element.264), channel_id=1, source_target_pairs={{0,4},{4,0},{8,12},{12,8},{16,20},{20,16},{24,28},{28,24},{1,5},{5... | collective-permute-start | bytes 2359304 | tf_op jit(solution)/shard_map/swap_dtokens0_c/ppermute | solution.py:553
  169.8 9.1 %collective-permute-start.36 = (bf16[1,4,96,384]{3,2,1,0:T(8,128)(2,1)S(1)}, bf16[1,4,96,384]{3,2,1,0:T(8,128)(2,1)S(1)}, u32[]{:S(2)}, u32[]{:S(2)}) collective-permute-start(bf16[1,4,96,384]{3,2,1,0:T(8,128)(2,1)S(1)} %get-tuple-element.270), channel_id=1, source_target_pairs={{0,8},{4,12},{8,0},{12,4},{16,24},{20,28},{24,16},{28,20},{1,9},{5... | collective-permute-start | bytes 884744 | tf_op jit(solution)/shard_map/swap_gfront_x1/ppermute | solution.py:553
  170.3 8.6 %collective-permute-start.37 = (bf16[2,256,768]{2,1,0:T(8,128)(2,1)S(1)}, bf16[2,256,768]{2,1,0:T(8,128)(2,1)S(1)}, u32[]{:S(2)}, u32[]{:S(2)}) collective-permute-start(bf16[2,256,768]{2,1,0:T(8,128)(2,1)S(1)} %get-tuple-element.271), channel_id=1, source_target_pairs={{0,4},{4,0},{8,12},{12,8},{16,20},{20,16},{24,28},{28,24},{1,5},{5... | collective-permute-start | bytes 2359304 | tf_op jit(solution)/shard_map/swap_dtokens1_c/ppermute | solution.py:553
  170.4 10.6 %collective-permute-start.42 = (bf16[24,1536]{1,0:T(8,128)(2,1)S(1)}, bf16[24,1536]{1,0:T(8,128)(2,1)S(1)}, u32[]{:S(2)}, u32[]{:S(2)}) collective-permute-start(bf16[24,1536]{1,0:T(8,128)(2,1)S(1)} %fusion.18), channel_id=1, source_target_pairs={{0,16},{4,20},{8,24},{12,28},{16,0},{20,4},{24,8},{28,12},{1,17},{... | collective-permute-start | bytes 221192 | tf_op jit(solution)/shard_map/swap_gup_y/ppermute | solution.py:553
  171.9 1.7 copy-start.6
  171.9 14.0 %collective-permute-start.43 = (bf16[256,768]{1,0:T(8,128)(2,1)S(1)}, bf16[256,768]{1,0:T(8,128)(2,1)S(1)}, u32[]{:S(2)}, u32[]{:S(2)}) collective-permute-start(bf16[256,768]{1,0:T(8,128)(2,1)S(1)} %fusion.5), channel_id=1, source_target_pairs={{0,16},{4,20},{8,24},{12,28},{16,0},{20,4},{24,8},{28,12},{1,17},{... | collective-permute-start | bytes 1179656 | tf_op jit(solution)/shard_map/swap_dtokens0_y/ppermute | solution.py:553
  179.1 12.9 %collective-permute-start.44 = (bf16[256,768]{1,0:T(8,128)(2,1)S(1)}, bf16[256,768]{1,0:T(8,128)(2,1)S(1)}, u32[]{:S(2)}, u32[]{:S(2)}) collective-permute-start(bf16[256,768]{1,0:T(8,128)(2,1)S(1)} %fusion.6), channel_id=1, source_target_pairs={{0,16},{4,20},{8,24},{12,28},{16,0},{20,4},{24,8},{28,12},{1,17},{... | collective-permute-start | bytes 1179656 | tf_op jit(solution)/shard_map/swap_dtokens1_y/ppermute | solution.py:553
  180.1 2.7 %collective-permute-start.48 = (bf16[24,768]{1,0:T(8,128)(2,1)S(1)}, bf16[24,768]{1,0:T(8,128)(2,1)S(1)}, u32[]{:S(2)}, u32[]{:S(2)}) collective-permute-start(bf16[24,768]{1,0:T(8,128)(2,1)S(1)} %fusion.19), channel_id=1, source_target_pairs={{0,0},{1,1},{2,2},{3,3},{4,8},{5,9},{6,10},{7,11},{8,4},{9,5},{10,... | collective-permute-start | bytes 110600 | tf_op jit(solution)/shard_map/swap_gout_moved/ppermute | solution.py:1052
  180.8 5.1 %collective-permute-start.39 = (bf16[4,24,384]{2,1,0:T(8,128)(2,1)S(1)}, bf16[4,24,384]{2,1,0:T(8,128)(2,1)S(1)}, u32[]{:S(2)}, u32[]{:S(2)}) collective-permute-start(bf16[4,24,384]{2,1,0:T(8,128)(2,1)S(1)} %get-tuple-element.314), channel_id=1, source_target_pairs={{0,1},{1,0},{2,3},{3,2},{4,5},{5,4},{6,7},{7,6},{8,9},{9,8},{10,11... | collective-permute-start | bytes 221192 | tf_op jit(solution)/shard_map/swap_gfront_z1/ppermute | solution.py:557
  180.9 5.4 %collective-permute-start.40 = (bf16[4,24,384]{2,1,0:T(8,128)(2,1)S(1)}, bf16[4,24,384]{2,1,0:T(8,128)(2,1)S(1)}, u32[]{:S(2)}, u32[]{:S(2)}) collective-permute-start(bf16[4,24,384]{2,1,0:T(8,128)(2,1)S(1)} %get-tuple-element.313), channel_id=1, source_target_pairs={{0,2},{1,3},{2,0},{3,1},{4,6},{5,7},{6,4},{7,5},{8,10},{9,11},{10,... | collective-permute-start | bytes 221192 | tf_op jit(solution)/shard_map/swap_gfront_z2/ppermute | solution.py:557
  182.8 7.3 %collective-permute-start.41 = (bf16[4,24,384]{2,1,0:T(8,128)(2,1)S(1)}, bf16[4,24,384]{2,1,0:T(8,128)(2,1)S(1)}, u32[]{:S(2)}, u32[]{:S(2)}) collective-permute-start(bf16[4,24,384]{2,1,0:T(8,128)(2,1)S(1)} %get-tuple-element.312), channel_id=1, source_target_pairs={{0,3},{1,2},{2,1},{3,0},{4,7},{5,6},{6,5},{7,4},{8,11},{9,10},{10,... | collective-permute-start | bytes 221192 | tf_op jit(solution)/shard_map/swap_gfront_z3/ppermute | solution.py:557
  192.1 2.1 %copy-start.7 = (f32[4,24,384]{2,1,0:T(8,128)}, f32[4,24,384]{2,1,0:T(8,128)S(1)}, u32[]{:S(2)}) copy-start(f32[4,24,384]{2,1,0:T(8,128)S(1)} %convert_add_fusion.11.mine_ref) | copy-start | bytes 442372
  192.2 3.4 %collective-permute-start.45 = (bf16[24,384]{1,0:T(8,128)(2,1)S(1)}, bf16[24,384]{1,0:T(8,128)(2,1)S(1)}, u32[]{:S(2)}, u32[]{:S(2)}) collective-permute-start(bf16[24,384]{1,0:T(8,128)(2,1)S(1)} %get-tuple-element.336), channel_id=1, source_target_pairs={{0,4},{4,0},{8,12},{12,8},{16,20},{20,16},{24,28},{28,24},{1,5},{5... | collective-permute-start | bytes 55304 | tf_op jit(solution)/shard_map/swap_gfront_1/ppermute | solution.py:553
  192.3 3.8 %collective-permute-start.46 = (bf16[24,384]{1,0:T(8,128)(2,1)S(1)}, bf16[24,384]{1,0:T(8,128)(2,1)S(1)}, u32[]{:S(2)}, u32[]{:S(2)}) collective-permute-start(bf16[24,384]{1,0:T(8,128)(2,1)S(1)} %get-tuple-element.335), channel_id=1, source_target_pairs={{0,16},{4,20},{8,24},{12,28},{16,0},{20,4},{24,8},{28,12},{1,17},{... | collective-permute-start | bytes 55304 | tf_op jit(solution)/shard_map/swap_gfront_2/ppermute | solution.py:553
  193.6 3.2 %collective-permute-start.47 = (bf16[24,384]{1,0:T(8,128)(2,1)S(1)}, bf16[24,384]{1,0:T(8,128)(2,1)S(1)}, u32[]{:S(2)}, u32[]{:S(2)}) collective-permute-start(bf16[24,384]{1,0:T(8,128)(2,1)S(1)} %get-tuple-element.334), channel_id=1, source_target_pairs={{0,20},{4,16},{8,28},{12,24},{16,4},{20,0},{24,12},{28,8},{1,21},{... | collective-permute-start | bytes 55304 | tf_op jit(solution)/shard_map/swap_gfront_3/ppermute | solution.py:553
  195.6 3.4 %copy-start.8 = (f32[24,3072]{1,0:T(8,128)}, f32[24,3072]{1,0:T(8,128)S(1)}, u32[]{:S(2)}) copy-start(f32[24,3072]{1,0:T(8,128)S(1)} %slice_dynamic-update-slice_fusion) | copy-start | bytes 884740
  195.6 1.1 copy-start.9
  196.1 0.7 copy-start.10
  196.8 0.6 copy-start.11
